TPU v7x, 256 devices: a whole 4x4x8 slice. The times are simulated.
256 devices in a mesh: row: 8 (over z), col: 32 (over y, x, core).
Axes of the slice: x: 4, y: 4, z: 8, core: 2. Of those that a mesh axis runs over, the one named last changes fastest.
Arguments:
- amplitudes: float32 [1024, 131072], P('col', 'row'), may hold values from -6 to 6
- integrals: float32 [131072, 3072], P(('row', 'col')), may hold values from -0.0625 to 0.0625
Outputs:
- ladder: float32 [1024, 3072], P('col', 'row')
All inputs are finite; a program needn't handle non-finite values.
Results may differ from a plain program's by a relative error of at most 0.00011.
Values sent between devices are 32-bit elements; how exact they have to be, the bound alone decides.
No kernel may reach another device: no remote copies, remote signals or barrier semaphores. Data moves between devices by JAX's collectives and lax.ppermute only.
A program may use at most 64 MiB of HBM per device.

v0:
```python
import jax
import jax.numpy as jnp
from jax import lax
from jax.sharding import PartitionSpec as P


def body(amplitudes, integrals):
    received = lax.all_to_all(amplitudes, "col", split_axis=1, concat_axis=0, tiled=True)
    by_pair = lax.psum_scatter(
        jnp.dot(
            received, integrals, precision=lax.Precision.HIGHEST, preferred_element_type=jnp.float32
        ),
        "col",
        scatter_dimension=0,
        tiled=True,
    )
    ladder = 0.5 * lax.psum_scatter(by_pair, "row", scatter_dimension=1, tiled=True)
    return ladder


def solution(mesh):
    return jax.shard_map(
        body,
        mesh=mesh,
        in_specs=(P("col", "row"), P(("row", "col"), None)),
        out_specs=P("col", "row"),
        check_vma=False,
    )
```

profile of v0, /device:TPU:2, one launch (start us, length us, event | category | flops | bytes accessed | tf_op | source)
XLA Modules:
  0.0 225.7 jit_solution(9289930068098570456)
XLA Ops:
  6.5 0.0 reduce-scatter.3.cloned.1.call-start
  6.5 0.0 copy-start
  6.5 1.9 copy.7
  8.5 34.9 %all_to_all.19 = f32[32,32,512]{2,0,1:T(8,128)S(1)} all-to-all(f32[32,32,512]{2,0,1:T(8,128)S(1)} %bitcast.10), channel_id=1, replica_groups=mesh['row'=8,'col'=32] {'col'}, dimensions={1} | all-to-all | bytes 4194304 | tf_op jit(solution)/shard_map/all_to_all | solution.py:8
  43.4 0.0 copy-done
  43.4 22.7 %fusion = f32[1024,3072]{1,0:T(8,128)} fusion(f32[1024,512]{1,0:T(8,128)S(1)} %bitcast.9, f32[512,3072]{1,0:T(8,128)S(1)} %copy-done), kind=kOutput, calls=%fused_computation.2 | convolution fusion | flops 19327352832 | bytes 20971520 | tf_op jit(solution)/shard_map/dot_general | solution.py:10
  66.1 0.0 reduce-scatter.3.cloned.1.call-update
  66.1 0.0 reduce-scatter.5.cloned.1.call-start
  66.1 111.9 %reduce-scatter.3.cloned.1.call-done = f32[32,3072]{1,0:T(8,128)} async-done(((f32[1024,3072]{1,0:T(8,128)}), f32[32,3072]{1,0:T(8,128)}) %reduce-scatter.3.cloned.1.call-update) | async-done | bytes 393232 | tf_op jit(solution)/shard_map/reduce_scatter | solution.py:9
  178.1 0.0 reduce-scatter.5.cloned.1.call-update
  178.1 39.3 %reduce-scatter.5.cloned.1.call-done = f32[32,384]{1,0:T(8,128)} async-done(((f32[32,3072]{1,0:T(8,128)}), f32[32,384]{1,0:T(8,128)}) %reduce-scatter.5.cloned.1.call-update) | async-done | bytes 49168 | tf_op jit(solution)/shard_map/reduce_scatter | solution.py:17
  217.4 1.4 broadcast_multiply_fusion
Async XLA Ops:
  6.5 171.5 %reduce-scatter.3.cloned.1.call-start = ((), (), s32[]{:S(2)}) async-start(), calls=%async_computation.3 | async-start | bytes 12976128 | tf_op jit(solution)/shard_map/reduce_scatter | solution.py:9
  6.5 36.9 %copy-start = (f32[512,3072]{1,0:T(8,128)S(1)}, f32[512,3072]{1,0:T(8,128)}, u32[]{:S(2)}) copy-start(f32[512,3072]{1,0:T(8,128)} %param.3) | copy-start | bytes 18874372
  66.1 151.3 %reduce-scatter.5.cloned.1.call-start = ((), (), s32[]{:S(2)}) async-start(), calls=%async_computation.4 | async-start | bytes 442368 | tf_op jit(solution)/shard_map/reduce_scatter | solution.py:17
Sparse Core Ops, SparseCore 0:
  66.2 111.8 reduce-scatter.2
  180.7 36.6 reduce-scatter.4
where the time goes:
time: 226 us
  waiting for transfers between devices  151 us (67%)
  blocking collectives  34.9 us (15%)
  matrix products  22.7 us (10%)
  between operations  13.4 us (6%)
    reduce_scatter x1, waiting for transfers between devices, body(): lax.psum_scatter(jnp.dot(received, integrals, precision=lax.Precision.HIG...  112 us
    reduce_scatter x1, waiting for transfers between devices, body(): lax.psum_scatter(by_pair, 'row', scatter_dimension=1, tiled=True)  39.3 us
    all_to_all x1, blocking collectives, body(): lax.all_to_all(amplitudes, 'col', split_axis=1, concat_axis=0, tiled=True)  34.9 us
    dot_general x1, matrix products, body(): jnp.dot(received, integrals, precision=lax.Precision.HIGHEST, preferred_e...  22.7 us
  transfers between devices with their start and end apart: 2, of which 2 were waited for; matrix products, arithmetic and copies ran while one was open for 0% of the time, Pallas kernels for 0%

commit v1 on v0

v1 whole, which is shorter than its diff:
```python
import functools

import jax
import jax.numpy as jnp
from jax import lax
from jax.experimental import pallas as pl
from jax.experimental.pallas import tpu as pltpu
from jax.sharding import Mesh, PartitionSpec as P

AXES = ("z", "y", "x", "core")
NZ, NY, NX = 8, 4, 4
ROWS, DEPTH, WIDTH = 32, 512, 384
GROUPS = 4
NEAR_FIRST, FAR_FIRST = (2, 1, 3, 0), (2, 3, 1, 0)


def flip(axis, mask):
    pairs = []
    for i in range(NZ * NY * NX * 2):
        at = {"z": i // 32, "y": i // 8 % 4, "x": i // 2 % 4, "core": i % 2}
        at[axis] ^= mask
        pairs.append((i, ((at["z"] * 4 + at["y"]) * 4 + at["x"]) * 2 + at["core"]))
    return pairs


def exchange(value, axis, mask):
    return lax.ppermute(value, AXES, flip(axis, mask))


def group_plan(group):
    order, masks = ((NEAR_FIRST, (1, 3)), (FAR_FIRST, (3, 1)))[group % 2]
    first, second = ("x", "y") if group < 2 else ("y", "x")
    steps = [(axis, mask) for axis in (first, second) for mask in masks]
    if first == "x":
        blocks = [qy * 4 + qx for qx in order for qy in order]
    else:
        blocks = [qy * 4 + qx for qy in order for qx in order]
    return steps, blocks


def split(value):
    high = value.astype(jnp.bfloat16)
    return high, (value - high.astype(jnp.float32)).astype(jnp.bfloat16)


def prepare_kernel(where, a_ref, hi_ref, lo_ref):
    own = pl.multiple_of(where[2] * DEPTH, DEPTH)
    other = pl.multiple_of((1 - where[2]) * DEPTH, DEPTH)
    for q in range(NY * NX):
        source = (where[0] ^ (q // 4)) * 4 + (where[1] ^ (q % 4))
        rows = pl.ds(pl.multiple_of(source * ROWS, ROWS), ROWS)
        to = pl.ds(q * ROWS, ROWS)
        for half, start in enumerate((own, other)):
            high, low = split(a_ref[rows, pl.ds(start, DEPTH)])
            hi_ref[to, pl.ds(half * DEPTH, DEPTH)] = high
            lo_ref[to, pl.ds(half * DEPTH, DEPTH)] = low


def prepare(where, a):
    shape = jax.ShapeDtypeStruct(a.shape, jnp.bfloat16)
    return pl.pallas_call(
        prepare_kernel,
        out_shape=(shape, shape),
        in_specs=[pl.BlockSpec(memory_space=pltpu.SMEM), pl.BlockSpec(memory_space=pltpu.VMEM)],
        out_specs=(pl.BlockSpec(memory_space=pltpu.VMEM),) * 2,
        compiler_params=pltpu.CompilerParams(vmem_limit_bytes=16 << 20),
    )(where, a)


def product_kernel(blocks, idx, hi_ref, lo_ref, own0, own1, oth0, oth1, send_ref, keep_ref, bhi, blo):
    for col, (own, oth) in enumerate(((own0, oth0), (own1, oth1))):
        at = pl.ds(col * WIDTH, WIDTH)
        for half, ref in enumerate((own, oth)):
            high, low = split(ref[...])
            bhi[pl.ds(half * DEPTH, DEPTH), at] = high
            blo[pl.ds(half * DEPTH, DEPTH), at] = low
    dot = functools.partial(jnp.dot, preferred_element_type=jnp.float32)
    total = dot(hi_ref[...], bhi[...]) + dot(lo_ref[...], bhi[...]) + dot(hi_ref[...], blo[...])
    for i, q in enumerate(blocks):
        value = total[q * ROWS : (q + 1) * ROWS]
        if i < 8:
            send_ref[pl.ds(i * ROWS, ROWS), :] = value
        else:
            keep_ref[pl.ds((i - 8) * ROWS, ROWS), :] = value


def product(group, idx, hi, lo, own, oth):
    _, blocks = group_plan(group)
    half = jax.ShapeDtypeStruct((8 * ROWS, 2 * WIDTH), jnp.float32)
    whole = pl.BlockSpec((16 * ROWS, 2 * DEPTH), lambda i, idx: (0, 0))
    col = lambda j: pl.BlockSpec((DEPTH, WIDTH), lambda i, idx: (0, idx[2 * group + j]))
    out = pl.BlockSpec((8 * ROWS, 2 * WIDTH), lambda i, idx: (0, 0))
    return pl.pallas_call(
        functools.partial(product_kernel, blocks),
        out_shape=(half, half),
        grid_spec=pltpu.PrefetchScalarGridSpec(
            num_scalar_prefetch=1,
            grid=(1,),
            in_specs=[whole, whole, col(0), col(1), col(0), col(1)],
            out_specs=(out, out),
            scratch_shapes=[pltpu.VMEM((2 * DEPTH, 2 * WIDTH), jnp.bfloat16)] * 2,
        ),
        compiler_params=pltpu.CompilerParams(vmem_limit_bytes=40 << 20),
        cost_estimate=pl.CostEstimate(
            flops=6 * 16 * ROWS * 2 * DEPTH * 2 * WIDTH, bytes_accessed=6 << 20, transcendentals=0
        ),
    )(idx, hi, lo, own, own, oth, oth)


def body(amplitudes, integrals):
    z, y, x, core = (lax.axis_index(name) for name in AXES)
    oth = exchange(integrals, "core", 1)
    mine = lax.all_to_all(amplitudes, ("y", "x"), split_axis=1, concat_axis=0, tiled=True)
    where = jnp.stack([y, x, core]).astype(jnp.int32)
    idx = jnp.stack([z ^ ((k >> 2) | (k & 2) | (k & 1) << 2) for k in range(NZ)]).astype(jnp.int32)
    hi, lo = prepare(where, mine)
    parts = []
    for group in range(GROUPS):
        steps, _ = group_plan(group)
        send, keep = product(group, idx, hi, lo, integrals, oth)
        for axis, mask in steps:
            total = keep + exchange(send, axis, mask)
            half = total.shape[0] // 2
            send, keep = total[:half], total[half:]
        parts.append(total)
    keep = jnp.concatenate(parts[:2], 1) + exchange(jnp.concatenate(parts[2:], 1), "z", 1)
    keep = keep[:, : 2 * WIDTH] + exchange(keep[:, 2 * WIDTH :], "z", 2)
    keep = keep[:, :WIDTH] + exchange(keep[:, WIDTH:], "z", 4)
    return 0.5 * keep


def solution(mesh):
    chips = Mesh(mesh.devices.reshape(NZ, NY, NX, 2), AXES)
    return jax.shard_map(
        body,
        mesh=chips,
        in_specs=(P(("y", "x", "core"), "z"), P(AXES, None)),
        out_specs=P(("y", "x", "core"), "z"),
        check_vma=False,
    )
```

time: 226 us -> 133 us (0.59)
  waiting for transfers between devices: 151 us -> 53 us
  starting transfers between devices: 0.04 us -> 51.3 us
  blocking collectives: 34.9 us -> 0 us
  matrix products: 22.7 us -> 0 us
  Pallas kernels: 0 us -> 19.9 us
  between operations: 13.4 us -> 0.28 us
  local copies, waits for them, and re-layouts: 1.95 us -> 6.31 us
    reduce_scatter x2 -> x0, waiting for transfers between devices: 151 us -> none  [the longest x1 112 us: body(): lax.psum_scatter(jnp.dot(received, integrals, precision=lax.Precision.HIG...]
    ppermute x0 -> x20, starting transfers between devices: none -> 43.8 us  [exchange(): return lax.ppermute(value, AXES, flip(axis, mask))]
    all_to_all x1 -> x0, blocking collectives: 34.9 us -> none  [body(): lax.all_to_all(amplitudes, 'col', split_axis=1, concat_axis=0, tiled=True)]
    all_to_all x0 -> x1, waiting for transfers between devices: none -> 29.2 us  [body(): lax.all_to_all(amplitudes, ('y', 'x'), split_axis=1, concat_axis=0, tiled...]
    ppermute x0 -> x20, waiting for transfers between devices: none -> 23.7 us  [exchange(): return lax.ppermute(value, AXES, flip(axis, mask))]
    dot_general x1 -> x0, matrix products: 22.7 us -> none  [body(): jnp.dot(received, integrals, precision=lax.Precision.HIGHEST, preferred_e...]
    pallas_call x0 -> x5, Pallas kernels: none -> 19.9 us  [the longest x4 19.1 us: product(): pl.pallas_call(functools.partial(product_kernel, blocks), out_shape=(half...]
    all_to_all x0 -> x1, starting transfers between devices: none -> 7.48 us  [body(): lax.all_to_all(amplitudes, ('y', 'x'), split_axis=1, concat_axis=0, tiled...]
  transfers between devices with their start and end apart: 2 -> 21, of which waited for: 2 -> 10; matrix products, arithmetic and copies ran while one was open for 0% -> 3% of each run, Pallas kernels for 0% -> 11%
where the time goes in v1:
time: 133 us; the launch traced here: 132 us
  waiting for transfers between devices  53 us (40%)
  starting transfers between devices  51.3 us (39%)
  Pallas kernels  19.9 us (15%)
  local copies, waits for them, and re-layouts  6.31 us (5%)
  other arithmetic  1.41 us (1%)
    ppermute x20, starting transfers between devices, exchange(): return lax.ppermute(value, AXES, flip(axis, mask))  43.8 us
    all_to_all x1, waiting for transfers between devices, body(): lax.all_to_all(amplitudes, ('y', 'x'), split_axis=1, concat_axis=0, tiled...  29.2 us
    ppermute x20, waiting for transfers between devices, exchange(): return lax.ppermute(value, AXES, flip(axis, mask))  23.7 us
    pallas_call x4, Pallas kernels, product(): pl.pallas_call(functools.partial(product_kernel, blocks), out_shape=(half...  19.1 us
    all_to_all x1, starting transfers between devices, body(): lax.all_to_all(amplitudes, ('y', 'x'), split_axis=1, concat_axis=0, tiled...  7.48 us
    all_to_all x1, local copies, waits for them, and re-layouts, body(): lax.all_to_all(amplitudes, ('y', 'x'), split_axis=1, concat_axis=0, tiled...  3.23 us
    unnamed x2, local copies, waits for them, and re-layouts  2.78 us
  transfers between devices with their start and end apart: 21, of which 10 were waited for; matrix products, arithmetic and copies ran while one was open for 3% of the time, Pallas kernels for 11%

profile of v1, /device:TPU:2, one launch (start us, length us, event | category | flops | bytes accessed | tf_op | source)
XLA Modules:
  0.0 132.1 jit_solution(14749779686377677437)
XLA Ops:
  0.0 0.0 collective-permute-start
  0.0 3.2 %copy.6 = f32[4,16,8,1024]{3,2,0,1:T(8,128)} copy(f32[4,16,8,1024]{3,2,1,0:T(8,128)} %bitcast.20) | data formatting | bytes 4194304 | tf_op jit(solution)/shard_map/all_to_all | solution.py:113
  3.2 7.5 %all-to-all-start = ((f32[32,16,1024]{2,0,1:T(8,128)}), f32[32,16,1024]{2,0,1:T(8,128)S(1)}, u32[]{:S(2)}, u32[]{:S(2)}) async-start(f32[32,16,1024]{2,0,1:T(8,128)} %bitcast.19), calls=%async_computation | async-start | bytes 4194304 | tf_op jit(solution)/shard_map/all_to_all | solution.py:113
  10.7 0.1 stack.47.idx
  10.8 0.1 pad_add_fusion.where
  10.9 29.2 %all-to-all-done = f32[32,16,1024]{2,0,1:T(8,128)S(1)} async-done(((f32[32,16,1024]{2,0,1:T(8,128)}), f32[32,16,1024]{2,0,1:T(8,128)S(1)}, u32[]{:S(2)}, u32[]{:S(2)}) %all-to-all-start) | async-done | bytes 2097184 | tf_op jit(solution)/shard_map/all_to_all | solution.py:113
  40.1 0.8 shard_map.28
  40.9 0.0 copy-start
  40.9 2.8 %copy-done = f32[512,3072]{1,0:T(8,128)S(1)} copy-done((f32[512,3072]{1,0:T(8,128)S(1)}, f32[512,3072]{1,0:T(8,128)}, u32[]{:S(2)}) %copy-start) | copy-done | bytes 6291480
  43.7 4.8 %shard_map.32 = (f32[256,768]{1,0:T(8,128)S(1)}, f32[256,768]{1,0:T(8,128)S(1)}) custom-call(s32[8]{0:T(128)S(1)} %stack.47.idx, bf16[512,1024]{1,0:T(8,128)(2,1)S(1)} %get-tuple-element.15.hi_ref, bf16[512,1024]{1,0:T(8,128)(2,1)S(1)} %get-tuple-element.16.lo_ref, f32[512,3072]{1,0:T(8,128)S(1)} %copy-done, f32[512,3072]{1,0:T(8,128)S(1)} %copy-done, ...), custom_call_target="tpu_custom_call" | custom-call | flops 2415919104 | bytes 6291456 | tf_op jit(solution)/shard_map/pallas_call | solution.py:93
  48.5 2.7 %collective-permute-start.13 = (f32[256,768]{1,0:T(8,128)S(1)}, f32[256,768]{1,0:T(8,128)S(1)}, u32[]{:S(2)}, u32[]{:S(2)}) collective-permute-start(f32[256,768]{1,0:T(8,128)S(1)} %get-tuple-element.24), channel_id=1, source_target_pairs={{0,24},{1,25},{2,26},{3,27},{4,28},{5,29},{6,30},{7,31},{8,16},{9,... | collective-permute-start | bytes 2359304 | tf_op jit(solution)/shard_map/ppermute | solution.py:27
  51.2 4.8 %shard_map.31 = (f32[256,768]{1,0:T(8,128)S(1)}, f32[256,768]{1,0:T(8,128)S(1)}) custom-call(s32[8]{0:T(128)S(1)} %stack.47.idx, bf16[512,1024]{1,0:T(8,128)(2,1)S(1)} %get-tuple-element.15.hi_ref, bf16[512,1024]{1,0:T(8,128)(2,1)S(1)} %get-tuple-element.16.lo_ref, f32[512,3072]{1,0:T(8,128)S(1)} %copy-done, f32[512,3072]{1,0:T(8,128)S(1)} %copy-done, ...), custom_call_target="tpu_custom_call" | custom-call | flops 2415919104 | bytes 6291456 | tf_op jit(solution)/shard_map/pallas_call | solution.py:93
  56.0 0.1 collective-permute-start.9
  56.1 4.8 %shard_map.30 = (f32[256,768]{1,0:T(8,128)S(1)}, f32[256,768]{1,0:T(8,128)S(1)}) custom-call(s32[8]{0:T(128)S(1)} %stack.47.idx, bf16[512,1024]{1,0:T(8,128)(2,1)S(1)} %get-tuple-element.15.hi_ref, bf16[512,1024]{1,0:T(8,128)(2,1)S(1)} %get-tuple-element.16.lo_ref, f32[512,3072]{1,0:T(8,128)S(1)} %copy-done, f32[512,3072]{1,0:T(8,128)S(1)} %copy-done, ...), custom_call_target="tpu_custom_call" | custom-call | flops 2415919104 | bytes 6291456 | tf_op jit(solution)/shard_map/pallas_call | solution.py:93
  60.9 2.1 %collective-permute-start.5 = (f32[256,768]{1,0:T(8,128)S(1)}, f32[256,768]{1,0:T(8,128)S(1)}, u32[]{:S(2)}, u32[]{:S(2)}) collective-permute-start(f32[256,768]{1,0:T(8,128)S(1)} %get-tuple-element.20), channel_id=1, source_target_pairs={{0,6},{1,7},{2,4},{3,5},{4,2},{5,3},{6,0},{7,1},{8,14},{9,15},{10,... | collective-permute-start | bytes 2359304 | tf_op jit(solution)/shard_map/ppermute | solution.py:27
  63.0 4.8 %shard_map.29 = (f32[256,768]{1,0:T(8,128)S(1)}, f32[256,768]{1,0:T(8,128)S(1)}) custom-call(s32[8]{0:T(128)S(1)} %stack.47.idx, bf16[512,1024]{1,0:T(8,128)(2,1)S(1)} %get-tuple-element.15.hi_ref, bf16[512,1024]{1,0:T(8,128)(2,1)S(1)} %get-tuple-element.16.lo_ref, f32[512,3072]{1,0:T(8,128)S(1)} %copy-done, f32[512,3072]{1,0:T(8,128)S(1)} %copy-done, ...), custom_call_target="tpu_custom_call" | custom-call | flops 2415919104 | bytes 6291456 | tf_op jit(solution)/shard_map/pallas_call | solution.py:93
  67.8 3.3 %collective-permute-start.1 = (f32[256,768]{1,0:T(8,128)S(1)}, f32[256,768]{1,0:T(8,128)S(1)}, u32[]{:S(2)}, u32[]{:S(2)}) collective-permute-start(f32[256,768]{1,0:T(8,128)S(1)} %get-tuple-element.18), channel_id=1, source_target_pairs={{0,2},{1,3},{2,0},{3,1},{4,6},{5,7},{6,4},{7,5},{8,10},{9,11},{10,... | collective-permute-start | bytes 2359304 | tf_op jit(solution)/shard_map/ppermute | solution.py:27
  71.0 0.0 collective-permute-done.13
  71.1 0.1 add.69
  71.2 1.0 collective-permute-start.14
  72.1 4.4 %collective-permute-done.9 = f32[256,768]{1,0:T(8,128)S(1)} collective-permute-done((f32[256,768]{1,0:T(8,128)S(1)}, f32[256,768]{1,0:T(8,128)S(1)}, u32[]{:S(2)}, u32[]{:S(2)}) %collective-permute-start.9) | collective-permute-done | bytes 786464 | tf_op jit(solution)/shard_map/ppermute | solution.py:27
  76.5 0.1 add.65
  76.7 0.7 collective-permute-start.10
  77.4 3.1 %collective-permute-done.5 = f32[256,768]{1,0:T(8,128)S(1)} collective-permute-done((f32[256,768]{1,0:T(8,128)S(1)}, f32[256,768]{1,0:T(8,128)S(1)}, u32[]{:S(2)}, u32[]{:S(2)}) %collective-permute-start.5) | collective-permute-done | bytes 786464 | tf_op jit(solution)/shard_map/ppermute | solution.py:27
  80.5 0.1 add.61
  80.6 4.4 %collective-permute-start.6 = (f32[128,768]{1,0:T(8,128)S(1)}, f32[128,768]{1,0:T(8,128)S(1)}, u32[]{:S(2)}, u32[]{:S(2)}) collective-permute-start(f32[128,768]{1,0:T(8,128)S(1)} %slice.119), channel_id=1, source_target_pairs={{0,2},{1,3},{2,0},{3,1},{4,6},{5,7},{6,4},{7,5},{8,10},{9,11},{10,... | collective-permute-start | bytes 1179656 | tf_op jit(solution)/shard_map/ppermute | solution.py:27
  85.0 4.5 %collective-permute-done.1 = f32[256,768]{1,0:T(8,128)S(1)} collective-permute-done((f32[256,768]{1,0:T(8,128)S(1)}, f32[256,768]{1,0:T(8,128)S(1)}, u32[]{:S(2)}, u32[]{:S(2)}) %collective-permute-start.1) | collective-permute-done | bytes 786464 | tf_op jit(solution)/shard_map/ppermute | solution.py:27
  89.5 0.1 add.57
  89.6 1.6 %collective-permute-start.2 = (f32[128,768]{1,0:T(8,128)S(1)}, f32[128,768]{1,0:T(8,128)S(1)}, u32[]{:S(2)}, u32[]{:S(2)}) collective-permute-start(f32[128,768]{1,0:T(8,128)S(1)} %slice.113), channel_id=1, source_target_pairs={{0,6},{1,7},{2,4},{3,5},{4,2},{5,3},{6,0},{7,1},{8,14},{9,15},{10,... | collective-permute-start | bytes 1179656 | tf_op jit(solution)/shard_map/ppermute | solution.py:27
  91.3 0.6 collective-permute-start.15
  92.0 3.3 %collective-permute-start.11 = (f32[64,768]{1,0:T(8,128)S(1)}, f32[64,768]{1,0:T(8,128)S(1)}, u32[]{:S(2)}, u32[]{:S(2)}) collective-permute-start(f32[64,768]{1,0:T(8,128)S(1)} %slice.127), channel_id=1, source_target_pairs={{0,2},{1,3},{2,0},{3,1},{4,6},{5,7},{6,4},{7,5},{8,10},{9,11},{10,... | collective-permute-start | bytes 589832 | tf_op jit(solution)/shard_map/ppermute | solution.py:27
  95.3 2.6 %collective-permute-done.6 = f32[128,768]{1,0:T(8,128)S(1)} collective-permute-done((f32[128,768]{1,0:T(8,128)S(1)}, f32[128,768]{1,0:T(8,128)S(1)}, u32[]{:S(2)}, u32[]{:S(2)}) %collective-permute-start.6) | collective-permute-done | bytes 393248 | tf_op jit(solution)/shard_map/ppermute | solution.py:27
  97.9 0.9 collective-permute-start.7
  98.9 0.0 collective-permute-done.2
  99.0 1.5 %collective-permute-start.3 = (f32[64,768]{1,0:T(8,128)S(1)}, f32[64,768]{1,0:T(8,128)S(1)}, u32[]{:S(2)}, u32[]{:S(2)}) collective-permute-start(f32[64,768]{1,0:T(8,128)S(1)} %slice.115), channel_id=1, source_target_pairs={{0,8},{1,9},{2,10},{3,11},{4,12},{5,13},{6,14},{7,15},{8,0},{9,1},... | collective-permute-start | bytes 589832 | tf_op jit(solution)/shard_map/ppermute | solution.py:27
  100.5 0.5 collective-permute-done.15
  101.0 2.5 %collective-permute-start.16 = (f32[32,768]{1,0:T(8,128)S(1)}, f32[32,768]{1,0:T(8,128)S(1)}, u32[]{:S(2)}, u32[]{:S(2)}) collective-permute-start(f32[32,768]{1,0:T(8,128)S(1)} %slice.135), channel_id=1, source_target_pairs={{0,2},{1,3},{2,0},{3,1},{4,6},{5,7},{6,4},{7,5},{8,10},{9,11},{10,... | collective-permute-start | bytes 294920 | tf_op jit(solution)/shard_map/ppermute | solution.py:27
  103.6 2.1 %collective-permute-start.12 = (f32[32,768]{1,0:T(8,128)S(1)}, f32[32,768]{1,0:T(8,128)S(1)}, u32[]{:S(2)}, u32[]{:S(2)}) collective-permute-start(f32[32,768]{1,0:T(8,128)S(1)} %slice.129), channel_id=1, source_target_pairs={{0,6},{1,7},{2,4},{3,5},{4,2},{5,3},{6,0},{7,1},{8,14},{9,15},{10,... | collective-permute-start | bytes 294920 | tf_op jit(solution)/shard_map/ppermute | solution.py:27
  105.7 1.5 %collective-permute-start.8 = (f32[32,768]{1,0:T(8,128)S(1)}, f32[32,768]{1,0:T(8,128)S(1)}, u32[]{:S(2)}, u32[]{:S(2)}) collective-permute-start(f32[32,768]{1,0:T(8,128)S(1)} %slice.123), channel_id=1, source_target_pairs={{0,8},{1,9},{2,10},{3,11},{4,12},{5,13},{6,14},{7,15},{8,0},{9,1},... | collective-permute-start | bytes 294920 | tf_op jit(solution)/shard_map/ppermute | solution.py:27
  107.3 1.8 %collective-permute-start.4 = (f32[32,768]{1,0:T(8,128)S(1)}, f32[32,768]{1,0:T(8,128)S(1)}, u32[]{:S(2)}, u32[]{:S(2)}) collective-permute-start(f32[32,768]{1,0:T(8,128)S(1)} %slice.117), channel_id=1, source_target_pairs={{0,24},{1,25},{2,26},{3,27},{4,28},{5,29},{6,30},{7,31},{8,16},{9,... | collective-permute-start | bytes 294920 | tf_op jit(solution)/shard_map/ppermute | solution.py:27
  109.2 2.0 %collective-permute-start.17 = (f32[32,1536]{1,0:T(8,128)S(1)}, f32[32,1536]{1,0:T(8,128)S(1)}, u32[]{:S(2)}, u32[]{:S(2)}) collective-permute-start(f32[32,1536]{1,0:T(8,128)S(1)} %pad_maximum_fusion), channel_id=1, source_target_pairs={{0,32},{1,33},{2,34},{3,35},{4,36},{5,37},{6,38},{7,39},{8,40},{9,... | collective-permute-start | bytes 589832 | tf_op jit(solution)/shard_map/ppermute | solution.py:27
  111.2 2.0 %collective-permute-done.4 = f32[32,768]{1,0:T(8,128)S(1)} collective-permute-done((f32[32,768]{1,0:T(8,128)S(1)}, f32[32,768]{1,0:T(8,128)S(1)}, u32[]{:S(2)}, u32[]{:S(2)}) %collective-permute-start.4) | collective-permute-done | bytes 98336 | tf_op jit(solution)/shard_map/ppermute | solution.py:27
  113.2 1.9 %collective-permute-done.17 = f32[32,1536]{1,0:T(8,128)S(1)} collective-permute-done((f32[32,1536]{1,0:T(8,128)S(1)}, f32[32,1536]{1,0:T(8,128)S(1)}, u32[]{:S(2)}, u32[]{:S(2)}) %collective-permute-start.17) | collective-permute-done | bytes 196640 | tf_op jit(solution)/shard_map/ppermute | solution.py:27
  115.2 3.1 %collective-permute-start.18 = (f32[32,768]{1,0:T(8,128)S(1)}, f32[32,768]{1,0:T(8,128)S(1)}, u32[]{:S(2)}, u32[]{:S(2)}) collective-permute-start(f32[32,768]{1,0:T(8,128)S(1)} %slice.137), channel_id=1, source_target_pairs={{0,64},{1,65},{2,66},{3,67},{4,68},{5,69},{6,70},{7,71},{8,72},{9,... | collective-permute-start | bytes 294920 | tf_op jit(solution)/shard_map/ppermute | solution.py:27
  118.3 2.6 %collective-permute-done.18 = f32[32,768]{1,0:T(8,128)S(1)} collective-permute-done((f32[32,768]{1,0:T(8,128)S(1)}, f32[32,768]{1,0:T(8,128)S(1)}, u32[]{:S(2)}, u32[]{:S(2)}) %collective-permute-start.18) | collective-permute-done | bytes 98336 | tf_op jit(solution)/shard_map/ppermute | solution.py:27
  120.9 8.5 %collective-permute-start.19 = (f32[32,384]{1,0:T(8,128)S(1)}, f32[32,384]{1,0:T(8,128)S(1)}, u32[]{:S(2)}, u32[]{:S(2)}) collective-permute-start(f32[32,384]{1,0:T(8,128)S(1)} %slice.139), channel_id=1, source_target_pairs={{0,128},{1,129},{2,130},{3,131},{4,132},{5,133},{6,134},{7,135},{8... | collective-permute-start | bytes 147464 | tf_op jit(solution)/shard_map/ppermute | solution.py:27
  129.4 2.1 %collective-permute-done.19 = f32[32,384]{1,0:T(8,128)S(1)} collective-permute-done((f32[32,384]{1,0:T(8,128)S(1)}, f32[32,384]{1,0:T(8,128)S(1)}, u32[]{:S(2)}, u32[]{:S(2)}) %collective-permute-start.19) | collective-permute-done | bytes 49184 | tf_op jit(solution)/shard_map/ppermute | solution.py:27
  131.5 0.6 fusion
  (38 shorter events, 0.6 us)
Async XLA Ops:
  0.0 40.9 %collective-permute-start = (f32[512,3072]{1,0:T(8,128)}, f32[512,3072]{1,0:T(8,128)}, u32[]{:S(2)}, u32[]{:S(2)}) collective-permute-start(f32[512,3072]{1,0:T(8,128)} %own1.7), channel_id=1, source_target_pairs={{0,1},{1,0},{2,3},{3,2},{4,5},{5,4},{6,7},{7,6},{8,9},{9,8},{10,11... | collective-permute-start | bytes 18874376 | tf_op jit(solution)/shard_map/ppermute | solution.py:27
  3.2 36.9 %all-to-all-start = ((f32[32,16,1024]{2,0,1:T(8,128)}), f32[32,16,1024]{2,0,1:T(8,128)S(1)}, u32[]{:S(2)}, u32[]{:S(2)}) async-start(f32[32,16,1024]{2,0,1:T(8,128)} %bitcast.19), calls=%async_computation | async-start | bytes 4194304 | tf_op jit(solution)/shard_map/all_to_all | solution.py:113
  40.9 2.8 %copy-start = (f32[512,3072]{1,0:T(8,128)S(1)}, f32[512,3072]{1,0:T(8,128)}, u32[]{:S(2)}) copy-start(f32[512,3072]{1,0:T(8,128)} %own1.7) | copy-start | bytes 18874372
  48.5 22.6 %collective-permute-start.13 = (f32[256,768]{1,0:T(8,128)S(1)}, f32[256,768]{1,0:T(8,128)S(1)}, u32[]{:S(2)}, u32[]{:S(2)}) collective-permute-start(f32[256,768]{1,0:T(8,128)S(1)} %get-tuple-element.24), channel_id=1, source_target_pairs={{0,24},{1,25},{2,26},{3,27},{4,28},{5,29},{6,30},{7,31},{8,16},{9,... | collective-permute-start | bytes 2359304 | tf_op jit(solution)/shard_map/ppermute | solution.py:27
  56.0 20.6 %collective-permute-start.9 = (f32[256,768]{1,0:T(8,128)S(1)}, f32[256,768]{1,0:T(8,128)S(1)}, u32[]{:S(2)}, u32[]{:S(2)}) collective-permute-start(f32[256,768]{1,0:T(8,128)S(1)} %get-tuple-element.22), channel_id=1, source_target_pairs={{0,8},{1,9},{2,10},{3,11},{4,12},{5,13},{6,14},{7,15},{8,0},{9,1},... | collective-permute-start | bytes 2359304 | tf_op jit(solution)/shard_map/ppermute | solution.py:27
  60.9 19.6 %collective-permute-start.5 = (f32[256,768]{1,0:T(8,128)S(1)}, f32[256,768]{1,0:T(8,128)S(1)}, u32[]{:S(2)}, u32[]{:S(2)}) collective-permute-start(f32[256,768]{1,0:T(8,128)S(1)} %get-tuple-element.20), channel_id=1, source_target_pairs={{0,6},{1,7},{2,4},{3,5},{4,2},{5,3},{6,0},{7,1},{8,14},{9,15},{10,... | collective-permute-start | bytes 2359304 | tf_op jit(solution)/shard_map/ppermute | solution.py:27
  67.8 21.7 %collective-permute-start.1 = (f32[256,768]{1,0:T(8,128)S(1)}, f32[256,768]{1,0:T(8,128)S(1)}, u32[]{:S(2)}, u32[]{:S(2)}) collective-permute-start(f32[256,768]{1,0:T(8,128)S(1)} %get-tuple-element.18), channel_id=1, source_target_pairs={{0,2},{1,3},{2,0},{3,1},{4,6},{5,7},{6,4},{7,5},{8,10},{9,11},{10,... | collective-permute-start | bytes 2359304 | tf_op jit(solution)/shard_map/ppermute | solution.py:27
  71.2 20.0 %collective-permute-start.14 = (f32[128,768]{1,0:T(8,128)S(1)}, f32[128,768]{1,0:T(8,128)S(1)}, u32[]{:S(2)}, u32[]{:S(2)}) collective-permute-start(f32[128,768]{1,0:T(8,128)S(1)} %slice.131), channel_id=1, source_target_pairs={{0,8},{1,9},{2,10},{3,11},{4,12},{5,13},{6,14},{7,15},{8,0},{9,1},... | collective-permute-start | bytes 1179656 | tf_op jit(solution)/shard_map/ppermute | solution.py:27
  76.7 15.2 %collective-permute-start.10 = (f32[128,768]{1,0:T(8,128)S(1)}, f32[128,768]{1,0:T(8,128)S(1)}, u32[]{:S(2)}, u32[]{:S(2)}) collective-permute-start(f32[128,768]{1,0:T(8,128)S(1)} %slice.125), channel_id=1, source_target_pairs={{0,24},{1,25},{2,26},{3,27},{4,28},{5,29},{6,30},{7,31},{8,16},{9,... | collective-permute-start | bytes 1179656 | tf_op jit(solution)/shard_map/ppermute | solution.py:27
  80.6 17.3 %collective-permute-start.6 = (f32[128,768]{1,0:T(8,128)S(1)}, f32[128,768]{1,0:T(8,128)S(1)}, u32[]{:S(2)}, u32[]{:S(2)}) collective-permute-start(f32[128,768]{1,0:T(8,128)S(1)} %slice.119), channel_id=1, source_target_pairs={{0,2},{1,3},{2,0},{3,1},{4,6},{5,7},{6,4},{7,5},{8,10},{9,11},{10,... | collective-permute-start | bytes 1179656 | tf_op jit(solution)/shard_map/ppermute | solution.py:27
  89.6 9.3 %collective-permute-start.2 = (f32[128,768]{1,0:T(8,128)S(1)}, f32[128,768]{1,0:T(8,128)S(1)}, u32[]{:S(2)}, u32[]{:S(2)}) collective-permute-start(f32[128,768]{1,0:T(8,128)S(1)} %slice.113), channel_id=1, source_target_pairs={{0,6},{1,7},{2,4},{3,5},{4,2},{5,3},{6,0},{7,1},{8,14},{9,15},{10,... | collective-permute-start | bytes 1179656 | tf_op jit(solution)/shard_map/ppermute | solution.py:27
  91.3 9.7 %collective-permute-start.15 = (f32[64,768]{1,0:T(8,128)S(1)}, f32[64,768]{1,0:T(8,128)S(1)}, u32[]{:S(2)}, u32[]{:S(2)}) collective-permute-start(f32[64,768]{1,0:T(8,128)S(1)} %slice.133), channel_id=1, source_target_pairs={{0,6},{1,7},{2,4},{3,5},{4,2},{5,3},{6,0},{7,1},{8,14},{9,15},{10,... | collective-permute-start | bytes 589832 | tf_op jit(solution)/shard_map/ppermute | solution.py:27
  92.0 11.5 %collective-permute-start.11 = (f32[64,768]{1,0:T(8,128)S(1)}, f32[64,768]{1,0:T(8,128)S(1)}, u32[]{:S(2)}, u32[]{:S(2)}) collective-permute-start(f32[64,768]{1,0:T(8,128)S(1)} %slice.127), channel_id=1, source_target_pairs={{0,2},{1,3},{2,0},{3,1},{4,6},{5,7},{6,4},{7,5},{8,10},{9,11},{10,... | collective-permute-start | bytes 589832 | tf_op jit(solution)/shard_map/ppermute | solution.py:27
  97.9 7.8 %collective-permute-start.7 = (f32[64,768]{1,0:T(8,128)S(1)}, f32[64,768]{1,0:T(8,128)S(1)}, u32[]{:S(2)}, u32[]{:S(2)}) collective-permute-start(f32[64,768]{1,0:T(8,128)S(1)} %slice.121), channel_id=1, source_target_pairs={{0,24},{1,25},{2,26},{3,27},{4,28},{5,29},{6,30},{7,31},{8,16},{9,... | collective-permute-start | bytes 589832 | tf_op jit(solution)/shard_map/ppermute | solution.py:27
  99.0 8.3 %collective-permute-start.3 = (f32[64,768]{1,0:T(8,128)S(1)}, f32[64,768]{1,0:T(8,128)S(1)}, u32[]{:S(2)}, u32[]{:S(2)}) collective-permute-start(f32[64,768]{1,0:T(8,128)S(1)} %slice.115), channel_id=1, source_target_pairs={{0,8},{1,9},{2,10},{3,11},{4,12},{5,13},{6,14},{7,15},{8,0},{9,1},... | collective-permute-start | bytes 589832 | tf_op jit(solution)/shard_map/ppermute | solution.py:27
  101.0 8.0 %collective-permute-start.16 = (f32[32,768]{1,0:T(8,128)S(1)}, f32[32,768]{1,0:T(8,128)S(1)}, u32[]{:S(2)}, u32[]{:S(2)}) collective-permute-start(f32[32,768]{1,0:T(8,128)S(1)} %slice.135), channel_id=1, source_target_pairs={{0,2},{1,3},{2,0},{3,1},{4,6},{5,7},{6,4},{7,5},{8,10},{9,11},{10,... | collective-permute-start | bytes 294920 | tf_op jit(solution)/shard_map/ppermute | solution.py:27
  103.6 5.5 %collective-permute-start.12 = (f32[32,768]{1,0:T(8,128)S(1)}, f32[32,768]{1,0:T(8,128)S(1)}, u32[]{:S(2)}, u32[]{:S(2)}) collective-permute-start(f32[32,768]{1,0:T(8,128)S(1)} %slice.129), channel_id=1, source_target_pairs={{0,6},{1,7},{2,4},{3,5},{4,2},{5,3},{6,0},{7,1},{8,14},{9,15},{10,... | collective-permute-start | bytes 294920 | tf_op jit(solution)/shard_map/ppermute | solution.py:27
  105.7 5.4 %collective-permute-start.8 = (f32[32,768]{1,0:T(8,128)S(1)}, f32[32,768]{1,0:T(8,128)S(1)}, u32[]{:S(2)}, u32[]{:S(2)}) collective-permute-start(f32[32,768]{1,0:T(8,128)S(1)} %slice.123), channel_id=1, source_target_pairs={{0,8},{1,9},{2,10},{3,11},{4,12},{5,13},{6,14},{7,15},{8,0},{9,1},... | collective-permute-start | bytes 294920 | tf_op jit(solution)/shard_map/ppermute | solution.py:27
  107.3 5.9 %collective-permute-start.4 = (f32[32,768]{1,0:T(8,128)S(1)}, f32[32,768]{1,0:T(8,128)S(1)}, u32[]{:S(2)}, u32[]{:S(2)}) collective-permute-start(f32[32,768]{1,0:T(8,128)S(1)} %slice.117), channel_id=1, source_target_pairs={{0,24},{1,25},{2,26},{3,27},{4,28},{5,29},{6,30},{7,31},{8,16},{9,... | collective-permute-start | bytes 294920 | tf_op jit(solution)/shard_map/ppermute | solution.py:27
  109.2 6.0 %collective-permute-start.17 = (f32[32,1536]{1,0:T(8,128)S(1)}, f32[32,1536]{1,0:T(8,128)S(1)}, u32[]{:S(2)}, u32[]{:S(2)}) collective-permute-start(f32[32,1536]{1,0:T(8,128)S(1)} %pad_maximum_fusion), channel_id=1, source_target_pairs={{0,32},{1,33},{2,34},{3,35},{4,36},{5,37},{6,38},{7,39},{8,40},{9,... | collective-permute-start | bytes 589832 | tf_op jit(solution)/shard_map/ppermute | solution.py:27
  115.2 5.7 %collective-permute-start.18 = (f32[32,768]{1,0:T(8,128)S(1)}, f32[32,768]{1,0:T(8,128)S(1)}, u32[]{:S(2)}, u32[]{:S(2)}) collective-permute-start(f32[32,768]{1,0:T(8,128)S(1)} %slice.137), channel_id=1, source_target_pairs={{0,64},{1,65},{2,66},{3,67},{4,68},{5,69},{6,70},{7,71},{8,72},{9,... | collective-permute-start | bytes 294920 | tf_op jit(solution)/shard_map/ppermute | solution.py:27
  120.9 10.6 %collective-permute-start.19 = (f32[32,384]{1,0:T(8,128)S(1)}, f32[32,384]{1,0:T(8,128)S(1)}, u32[]{:S(2)}, u32[]{:S(2)}) collective-permute-start(f32[32,384]{1,0:T(8,128)S(1)} %slice.139), channel_id=1, source_target_pairs={{0,128},{1,129},{2,130},{3,131},{4,132},{5,133},{6,134},{7,135},{8... | collective-permute-start | bytes 147464 | tf_op jit(solution)/shard_map/ppermute | solution.py:27

commit v2 on v1

--- a/solution.py
+++ b/solution.py
@@ -67,15 +67,34 @@
     )(where, a)
 
 
-def product_kernel(blocks, idx, hi_ref, lo_ref, own0, own1, oth0, oth1, send_ref, keep_ref, bhi, blo):
-    for col, (own, oth) in enumerate(((own0, oth0), (own1, oth1))):
-        at = pl.ds(col * WIDTH, WIDTH)
-        for half, ref in enumerate((own, oth)):
-            high, low = split(ref[...])
-            bhi[pl.ds(half * DEPTH, DEPTH), at] = high
-            blo[pl.ds(half * DEPTH, DEPTH), at] = low
+def integrals_kernel(idx, own_ref, oth_ref, hi_ref, lo_ref):
+    for half, ref in enumerate((own_ref, oth_ref)):
+        to = pl.ds(half * DEPTH, DEPTH)
+        hi_ref[to, :], lo_ref[to, :] = split(ref[...])
+
+
+def prepare_integrals(idx, own, oth):
+    shape = jax.ShapeDtypeStruct((2 * DEPTH, NZ * WIDTH), jnp.bfloat16)
+    block = pl.BlockSpec((DEPTH, WIDTH), lambda k, idx: (0, idx[k]))
+    out = pl.BlockSpec((2 * DEPTH, WIDTH), lambda k, idx: (0, k))
+    return pl.pallas_call(
+        integrals_kernel,
+        out_shape=(shape, shape),
+        grid_spec=pltpu.PrefetchScalarGridSpec(
+            num_scalar_prefetch=1, grid=(NZ,), in_specs=[block, block], out_specs=(out, out)
+        ),
+        compiler_params=pltpu.CompilerParams(vmem_limit_bytes=16 << 20),
+        cost_estimate=pl.CostEstimate(flops=20 << 20, bytes_accessed=24 << 20, transcendentals=0),
+    )(idx, own, oth)
+
+
+def product_kernel(group, hi_ref, lo_ref, bhi_ref, blo_ref, send_ref, keep_ref):
+    _, blocks = group_plan(group)
+    cols = pl.ds(group * 2 * WIDTH, 2 * WIDTH)
     dot = functools.partial(jnp.dot, preferred_element_type=jnp.float32)
-    total = dot(hi_ref[...], bhi[...]) + dot(lo_ref[...], bhi[...]) + dot(hi_ref[...], blo[...])
+    total = dot(hi_ref[...], bhi_ref[:, cols])
+    total += dot(lo_ref[...], bhi_ref[:, cols])
+    total += dot(hi_ref[...], blo_ref[:, cols])
     for i, q in enumerate(blocks):
         value = total[q * ROWS : (q + 1) * ROWS]
         if i < 8:
@@ -84,27 +103,19 @@
             keep_ref[pl.ds((i - 8) * ROWS, ROWS), :] = value
 
 
-def product(group, idx, hi, lo, own, oth):
-    _, blocks = group_plan(group)
+def product(group, hi, lo, bhi, blo):
     half = jax.ShapeDtypeStruct((8 * ROWS, 2 * WIDTH), jnp.float32)
-    whole = pl.BlockSpec((16 * ROWS, 2 * DEPTH), lambda i, idx: (0, 0))
-    col = lambda j: pl.BlockSpec((DEPTH, WIDTH), lambda i, idx: (0, idx[2 * group + j]))
-    out = pl.BlockSpec((8 * ROWS, 2 * WIDTH), lambda i, idx: (0, 0))
+    vmem = pl.BlockSpec(memory_space=pltpu.VMEM)
     return pl.pallas_call(
-        functools.partial(product_kernel, blocks),
+        functools.partial(product_kernel, group),
         out_shape=(half, half),
-        grid_spec=pltpu.PrefetchScalarGridSpec(
-            num_scalar_prefetch=1,
-            grid=(1,),
-            in_specs=[whole, whole, col(0), col(1), col(0), col(1)],
-            out_specs=(out, out),
-            scratch_shapes=[pltpu.VMEM((2 * DEPTH, 2 * WIDTH), jnp.bfloat16)] * 2,
-        ),
-        compiler_params=pltpu.CompilerParams(vmem_limit_bytes=40 << 20),
+        in_specs=[vmem] * 4,
+        out_specs=(vmem, vmem),
+        compiler_params=pltpu.CompilerParams(vmem_limit_bytes=32 << 20),
         cost_estimate=pl.CostEstimate(
             flops=6 * 16 * ROWS * 2 * DEPTH * 2 * WIDTH, bytes_accessed=6 << 20, transcendentals=0
         ),
-    )(idx, hi, lo, own, own, oth, oth)
+    )(hi, lo, bhi, blo)
 
 
 def body(amplitudes, integrals):
@@ -113,11 +124,12 @@
     mine = lax.all_to_all(amplitudes, ("y", "x"), split_axis=1, concat_axis=0, tiled=True)
     where = jnp.stack([y, x, core]).astype(jnp.int32)
     idx = jnp.stack([z ^ ((k >> 2) | (k & 2) | (k & 1) << 2) for k in range(NZ)]).astype(jnp.int32)
+    bhi, blo = prepare_integrals(idx, integrals, oth)
     hi, lo = prepare(where, mine)
     parts = []
     for group in range(GROUPS):
         steps, _ = group_plan(group)
-        send, keep = product(group, idx, hi, lo, integrals, oth)
+        send, keep = product(group, hi, lo, bhi, blo)
         for axis, mask in steps:
             total = keep + exchange(send, axis, mask)
             half = total.shape[0] // 2

time: 133 us -> 135 us (1.015)
  waiting for transfers between devices: 53 us -> 59.5 us
  starting transfers between devices: 51.3 us -> 46.8 us
    ppermute x20, waiting for transfers between devices: 23.7 us -> 30.3 us  [exchange(): return lax.ppermute(value, AXES, flip(axis, mask))]
    ppermute x20, starting transfers between devices: 43.8 us -> 39.3 us  [exchange(): return lax.ppermute(value, AXES, flip(axis, mask))]
    pallas_call x4 -> x5, Pallas kernels: 19.1 us -> 18.7 us  [the longest x4 10.5 us: product(): pl.pallas_call(functools.partial(product_kernel, group), out_shape=(half,...]
  transfers between devices with their start and end apart: 21 -> 21, of which waited for: 10 -> 13; matrix products, arithmetic and copies ran while one was open for 3% -> 3% of each run, Pallas kernels for 11% -> 4%
where the time goes in v2:
time: 135 us; the launch traced here: 134 us
  waiting for transfers between devices  59.5 us (44%)
  starting transfers between devices  46.8 us (35%)
  Pallas kernels  19.5 us (14%)
  local copies, waits for them, and re-layouts  6.32 us (5%)
  other arithmetic  1.42 us (1%)
    ppermute x20, starting transfers between devices, exchange(): return lax.ppermute(value, AXES, flip(axis, mask))  39.3 us
    ppermute x20, waiting for transfers between devices, exchange(): return lax.ppermute(value, AXES, flip(axis, mask))  30.3 us
    all_to_all x1, waiting for transfers between devices, body(): lax.all_to_all(amplitudes, ('y', 'x'), split_axis=1, concat_axis=0, tiled...  29.2 us
    pallas_call x4, Pallas kernels, product(): pl.pallas_call(functools.partial(product_kernel, group), out_shape=(half,...  10.5 us
    pallas_call x1, Pallas kernels, prepare_integrals(): pl.pallas_call(integrals_kernel, out_shape=(shape, shape), grid_spec=pltp...  8.23 us
    all_to_all x1, starting transfers between devices, body(): lax.all_to_all(amplitudes, ('y', 'x'), split_axis=1, concat_axis=0, tiled...  7.48 us
    all_to_all x1, local copies, waits for them, and re-layouts, body(): lax.all_to_all(amplitudes, ('y', 'x'), split_axis=1, concat_axis=0, tiled...  3.25 us
    unnamed x2, local copies, waits for them, and re-layouts  2.78 us
  transfers between devices with their start and end apart: 21, of which 13 were waited for; matrix products, arithmetic and copies ran while one was open for 3% of the time, Pallas kernels for 4%

profile of v2, /device:TPU:2, one launch (start us, length us, event | category | flops | bytes accessed | tf_op | source)
XLA Modules:
  0.0 133.8 jit_solution(6070484027226858243)
XLA Ops:
  0.0 3.2 %copy.6 = f32[4,16,8,1024]{3,2,0,1:T(8,128)} copy(f32[4,16,8,1024]{3,2,1,0:T(8,128)} %bitcast.20) | data formatting | bytes 4194304 | tf_op jit(solution)/shard_map/all_to_all | solution.py:124
  3.2 7.5 %all-to-all-start = ((f32[32,16,1024]{2,0,1:T(8,128)}), f32[32,16,1024]{2,0,1:T(8,128)S(1)}, u32[]{:S(2)}, u32[]{:S(2)}) async-start(f32[32,16,1024]{2,0,1:T(8,128)} %bitcast.19), calls=%async_computation | async-start | bytes 4194304 | tf_op jit(solution)/shard_map/all_to_all | solution.py:124
  10.7 0.1 stack.51.idx
  10.8 0.1 pad_add_fusion.where
  10.9 29.2 %all-to-all-done = f32[32,16,1024]{2,0,1:T(8,128)S(1)} async-done(((f32[32,16,1024]{2,0,1:T(8,128)}), f32[32,16,1024]{2,0,1:T(8,128)S(1)}, u32[]{:S(2)}, u32[]{:S(2)}) %all-to-all-start) | async-done | bytes 2097184 | tf_op jit(solution)/shard_map/all_to_all | solution.py:124
  40.1 0.8 shard_map.28
  40.9 0.0 copy-start
  41.0 2.8 %copy-done = f32[512,3072]{1,0:T(8,128)S(1)} copy-done((f32[512,3072]{1,0:T(8,128)S(1)}, f32[512,3072]{1,0:T(8,128)}, u32[]{:S(2)}) %copy-start) | copy-done | bytes 6291480
  43.7 8.2 %shard_map.29 = (bf16[1024,3072]{1,0:T(8,128)(2,1)S(1)}, bf16[1024,3072]{1,0:T(8,128)(2,1)S(1)}) custom-call(s32[8]{0:T(128)S(1)} %stack.51.idx, f32[512,3072]{1,0:T(8,128)S(1)} %copy-done, f32[512,3072]{1,0:T(8,128)} %collective-permute-done.oth_ref), custom_call_target="tpu_custom_call" | custom-call | flops 20971520 | bytes 25165824 | tf_op jit(solution)/shard_map/pallas_call | solution.py:80
  52.0 2.6 %shard_map.30 = (f32[256,768]{1,0:T(8,128)S(1)}, f32[256,768]{1,0:T(8,128)S(1)}) custom-call(bf16[512,1024]{1,0:T(8,128)(2,1)S(1)} %get-tuple-element.17.hi_ref, bf16[512,1024]{1,0:T(8,128)(2,1)S(1)} %get-tuple-element.18.lo_ref, bf16[1024,3072]{1,0:T(8,128)(2,1)S(1)} %get-tuple-element.19.bhi_ref, bf16[1024,3072]{1,0:T(8,128)(2,1)S(1)} %get-tuple-element.20.blo_ref), custom_call_target="tpu_custom_call" | custom-call | flops 2415919104 | bytes 6291456 | tf_op jit(solution)/shard_map/pallas_call | solution.py:109
  54.6 2.6 %shard_map.31 = (f32[256,768]{1,0:T(8,128)S(1)}, f32[256,768]{1,0:T(8,128)S(1)}) custom-call(bf16[512,1024]{1,0:T(8,128)(2,1)S(1)} %get-tuple-element.17.hi_ref, bf16[512,1024]{1,0:T(8,128)(2,1)S(1)} %get-tuple-element.18.lo_ref, bf16[1024,3072]{1,0:T(8,128)(2,1)S(1)} %get-tuple-element.19.bhi_ref, bf16[1024,3072]{1,0:T(8,128)(2,1)S(1)} %get-tuple-element.20.blo_ref), custom_call_target="tpu_custom_call" | custom-call | flops 2415919104 | bytes 6291456 | tf_op jit(solution)/shard_map/pallas_call | solution.py:109
  57.2 5.0 %collective-permute-start.1 = (f32[256,768]{1,0:T(8,128)S(1)}, f32[256,768]{1,0:T(8,128)S(1)}, u32[]{:S(2)}, u32[]{:S(2)}) collective-permute-start(f32[256,768]{1,0:T(8,128)S(1)} %get-tuple-element.22), channel_id=1, source_target_pairs={{0,2},{1,3},{2,0},{3,1},{4,6},{5,7},{6,4},{7,5},{8,10},{9,11},{10,... | collective-permute-start | bytes 2359304 | tf_op jit(solution)/shard_map/ppermute | solution.py:27
  62.2 2.6 %shard_map.32 = (f32[256,768]{1,0:T(8,128)S(1)}, f32[256,768]{1,0:T(8,128)S(1)}) custom-call(bf16[512,1024]{1,0:T(8,128)(2,1)S(1)} %get-tuple-element.17.hi_ref, bf16[512,1024]{1,0:T(8,128)(2,1)S(1)} %get-tuple-element.18.lo_ref, bf16[1024,3072]{1,0:T(8,128)(2,1)S(1)} %get-tuple-element.19.bhi_ref, bf16[1024,3072]{1,0:T(8,128)(2,1)S(1)} %get-tuple-element.20.blo_ref), custom_call_target="tpu_custom_call" | custom-call | flops 2415919104 | bytes 6291456 | tf_op jit(solution)/shard_map/pallas_call | solution.py:109
  64.9 0.3 collective-permute-start.9
  65.1 2.6 %shard_map.33 = (f32[256,768]{1,0:T(8,128)S(1)}, f32[256,768]{1,0:T(8,128)S(1)}) custom-call(bf16[512,1024]{1,0:T(8,128)(2,1)S(1)} %get-tuple-element.17.hi_ref, bf16[512,1024]{1,0:T(8,128)(2,1)S(1)} %get-tuple-element.18.lo_ref, bf16[1024,3072]{1,0:T(8,128)(2,1)S(1)} %get-tuple-element.19.bhi_ref, bf16[1024,3072]{1,0:T(8,128)(2,1)S(1)} %get-tuple-element.20.blo_ref), custom_call_target="tpu_custom_call" | custom-call | flops 2415919104 | bytes 6291456 | tf_op jit(solution)/shard_map/pallas_call | solution.py:109
  67.7 2.6 %collective-permute-start.13 = (f32[256,768]{1,0:T(8,128)S(1)}, f32[256,768]{1,0:T(8,128)S(1)}, u32[]{:S(2)}, u32[]{:S(2)}) collective-permute-start(f32[256,768]{1,0:T(8,128)S(1)} %get-tuple-element.28), channel_id=1, source_target_pairs={{0,24},{1,25},{2,26},{3,27},{4,28},{5,29},{6,30},{7,31},{8,16},{9,... | collective-permute-start | bytes 2359304 | tf_op jit(solution)/shard_map/ppermute | solution.py:27
  70.4 9.0 %collective-permute-done.1 = f32[256,768]{1,0:T(8,128)S(1)} collective-permute-done((f32[256,768]{1,0:T(8,128)S(1)}, f32[256,768]{1,0:T(8,128)S(1)}, u32[]{:S(2)}, u32[]{:S(2)}) %collective-permute-start.1) | collective-permute-done | bytes 786464 | tf_op jit(solution)/shard_map/ppermute | solution.py:27
  79.4 0.1 add.57
  79.5 0.1 collective-permute-start.2
  79.6 1.2 collective-permute-done.5
  80.8 0.1 add.61
  81.0 1.9 %collective-permute-start.6 = (f32[128,768]{1,0:T(8,128)S(1)}, f32[128,768]{1,0:T(8,128)S(1)}, u32[]{:S(2)}, u32[]{:S(2)}) collective-permute-start(f32[128,768]{1,0:T(8,128)S(1)} %slice.119), channel_id=1, source_target_pairs={{0,2},{1,3},{2,0},{3,1},{4,6},{5,7},{6,4},{7,5},{8,10},{9,11},{10,... | collective-permute-start | bytes 1179656 | tf_op jit(solution)/shard_map/ppermute | solution.py:27
  82.8 0.8 collective-permute-done.9
  83.6 0.1 add.65
  83.7 1.6 %collective-permute-start.10 = (f32[128,768]{1,0:T(8,128)S(1)}, f32[128,768]{1,0:T(8,128)S(1)}, u32[]{:S(2)}, u32[]{:S(2)}) collective-permute-start(f32[128,768]{1,0:T(8,128)S(1)} %slice.125), channel_id=1, source_target_pairs={{0,24},{1,25},{2,26},{3,27},{4,28},{5,29},{6,30},{7,31},{8,16},{9,... | collective-permute-start | bytes 1179656 | tf_op jit(solution)/shard_map/ppermute | solution.py:27
  85.3 3.8 %collective-permute-done.13 = f32[256,768]{1,0:T(8,128)S(1)} collective-permute-done((f32[256,768]{1,0:T(8,128)S(1)}, f32[256,768]{1,0:T(8,128)S(1)}, u32[]{:S(2)}, u32[]{:S(2)}) %collective-permute-start.13) | collective-permute-done | bytes 786464 | tf_op jit(solution)/shard_map/ppermute | solution.py:27
  89.1 0.1 add.69
  89.2 1.1 collective-permute-start.14
  90.5 1.1 collective-permute-start.3
  91.6 2.8 %collective-permute-start.7 = (f32[64,768]{1,0:T(8,128)S(1)}, f32[64,768]{1,0:T(8,128)S(1)}, u32[]{:S(2)}, u32[]{:S(2)}) collective-permute-start(f32[64,768]{1,0:T(8,128)S(1)} %slice.121), channel_id=1, source_target_pairs={{0,24},{1,25},{2,26},{3,27},{4,28},{5,29},{6,30},{7,31},{8,16},{9,... | collective-permute-start | bytes 589832 | tf_op jit(solution)/shard_map/ppermute | solution.py:27
  94.4 3.2 %collective-permute-done.10 = f32[128,768]{1,0:T(8,128)S(1)} collective-permute-done((f32[128,768]{1,0:T(8,128)S(1)}, f32[128,768]{1,0:T(8,128)S(1)}, u32[]{:S(2)}, u32[]{:S(2)}) %collective-permute-start.10) | collective-permute-done | bytes 393248 | tf_op jit(solution)/shard_map/ppermute | solution.py:27
  97.6 1.8 %collective-permute-start.11 = (f32[64,768]{1,0:T(8,128)S(1)}, f32[64,768]{1,0:T(8,128)S(1)}, u32[]{:S(2)}, u32[]{:S(2)}) collective-permute-start(f32[64,768]{1,0:T(8,128)S(1)} %slice.127), channel_id=1, source_target_pairs={{0,2},{1,3},{2,0},{3,1},{4,6},{5,7},{6,4},{7,5},{8,10},{9,11},{10,... | collective-permute-start | bytes 589832 | tf_op jit(solution)/shard_map/ppermute | solution.py:27
  99.5 1.1 collective-permute-start.15
  100.6 0.5 collective-permute-done.3
  101.1 1.7 %collective-permute-start.4 = (f32[32,768]{1,0:T(8,128)S(1)}, f32[32,768]{1,0:T(8,128)S(1)}, u32[]{:S(2)}, u32[]{:S(2)}) collective-permute-start(f32[32,768]{1,0:T(8,128)S(1)} %slice.117), channel_id=1, source_target_pairs={{0,24},{1,25},{2,26},{3,27},{4,28},{5,29},{6,30},{7,31},{8,16},{9,... | collective-permute-start | bytes 294920 | tf_op jit(solution)/shard_map/ppermute | solution.py:27
  102.9 0.1 collective-permute-start.8
  103.0 0.4 collective-permute-done.11
  103.4 2.7 %collective-permute-start.12 = (f32[32,768]{1,0:T(8,128)S(1)}, f32[32,768]{1,0:T(8,128)S(1)}, u32[]{:S(2)}, u32[]{:S(2)}) collective-permute-start(f32[32,768]{1,0:T(8,128)S(1)} %slice.129), channel_id=1, source_target_pairs={{0,6},{1,7},{2,4},{3,5},{4,2},{5,3},{6,0},{7,1},{8,14},{9,15},{10,... | collective-permute-start | bytes 294920 | tf_op jit(solution)/shard_map/ppermute | solution.py:27
  106.2 1.7 %collective-permute-start.16 = (f32[32,768]{1,0:T(8,128)S(1)}, f32[32,768]{1,0:T(8,128)S(1)}, u32[]{:S(2)}, u32[]{:S(2)}) collective-permute-start(f32[32,768]{1,0:T(8,128)S(1)} %slice.135), channel_id=1, source_target_pairs={{0,2},{1,3},{2,0},{3,1},{4,6},{5,7},{6,4},{7,5},{8,10},{9,11},{10,... | collective-permute-start | bytes 294920 | tf_op jit(solution)/shard_map/ppermute | solution.py:27
  107.9 0.9 collective-permute-done.12
  108.8 2.1 %collective-permute-done.16 = f32[32,768]{1,0:T(8,128)S(1)} collective-permute-done((f32[32,768]{1,0:T(8,128)S(1)}, f32[32,768]{1,0:T(8,128)S(1)}, u32[]{:S(2)}, u32[]{:S(2)}) %collective-permute-start.16) | collective-permute-done | bytes 98336 | tf_op jit(solution)/shard_map/ppermute | solution.py:27
  110.9 2.1 %collective-permute-start.17 = (f32[32,1536]{1,0:T(8,128)S(1)}, f32[32,1536]{1,0:T(8,128)S(1)}, u32[]{:S(2)}, u32[]{:S(2)}) collective-permute-start(f32[32,1536]{1,0:T(8,128)S(1)} %pad_maximum_fusion), channel_id=1, source_target_pairs={{0,32},{1,33},{2,34},{3,35},{4,36},{5,37},{6,38},{7,39},{8,40},{9,... | collective-permute-start | bytes 589832 | tf_op jit(solution)/shard_map/ppermute | solution.py:27
  113.1 3.8 %collective-permute-done.17 = f32[32,1536]{1,0:T(8,128)S(1)} collective-permute-done((f32[32,1536]{1,0:T(8,128)S(1)}, f32[32,1536]{1,0:T(8,128)S(1)}, u32[]{:S(2)}, u32[]{:S(2)}) %collective-permute-start.17) | collective-permute-done | bytes 196640 | tf_op jit(solution)/shard_map/ppermute | solution.py:27
  116.9 3.2 %collective-permute-start.18 = (f32[32,768]{1,0:T(8,128)S(1)}, f32[32,768]{1,0:T(8,128)S(1)}, u32[]{:S(2)}, u32[]{:S(2)}) collective-permute-start(f32[32,768]{1,0:T(8,128)S(1)} %slice.137), channel_id=1, source_target_pairs={{0,64},{1,65},{2,66},{3,67},{4,68},{5,69},{6,70},{7,71},{8,72},{9,... | collective-permute-start | bytes 294920 | tf_op jit(solution)/shard_map/ppermute | solution.py:27
  120.1 2.6 %collective-permute-done.18 = f32[32,768]{1,0:T(8,128)S(1)} collective-permute-done((f32[32,768]{1,0:T(8,128)S(1)}, f32[32,768]{1,0:T(8,128)S(1)}, u32[]{:S(2)}, u32[]{:S(2)}) %collective-permute-start.18) | collective-permute-done | bytes 98336 | tf_op jit(solution)/shard_map/ppermute | solution.py:27
  122.8 8.4 %collective-permute-start.19 = (f32[32,384]{1,0:T(8,128)S(1)}, f32[32,384]{1,0:T(8,128)S(1)}, u32[]{:S(2)}, u32[]{:S(2)}) collective-permute-start(f32[32,384]{1,0:T(8,128)S(1)} %slice.139), channel_id=1, source_target_pairs={{0,128},{1,129},{2,130},{3,131},{4,132},{5,133},{6,134},{7,135},{8... | collective-permute-start | bytes 147464 | tf_op jit(solution)/shard_map/ppermute | solution.py:27
  131.2 2.1 %collective-permute-done.19 = f32[32,384]{1,0:T(8,128)S(1)} collective-permute-done((f32[32,384]{1,0:T(8,128)S(1)}, f32[32,384]{1,0:T(8,128)S(1)}, u32[]{:S(2)}, u32[]{:S(2)}) %collective-permute-start.19) | collective-permute-done | bytes 49184 | tf_op jit(solution)/shard_map/ppermute | solution.py:27
  133.2 0.6 fusion
  (39 shorter events, 0.6 us)
Async XLA Ops:
  0.0 40.9 %collective-permute-start = (f32[512,3072]{1,0:T(8,128)}, f32[512,3072]{1,0:T(8,128)}, u32[]{:S(2)}, u32[]{:S(2)}) collective-permute-start(f32[512,3072]{1,0:T(8,128)} %own_ref.1), channel_id=1, source_target_pairs={{0,1},{1,0},{2,3},{3,2},{4,5},{5,4},{6,7},{7,6},{8,9},{9,8},{10,11... | collective-permute-start | bytes 18874376 | tf_op jit(solution)/shard_map/ppermute | solution.py:27
  3.2 36.9 %all-to-all-start = ((f32[32,16,1024]{2,0,1:T(8,128)}), f32[32,16,1024]{2,0,1:T(8,128)S(1)}, u32[]{:S(2)}, u32[]{:S(2)}) async-start(f32[32,16,1024]{2,0,1:T(8,128)} %bitcast.19), calls=%async_computation | async-start | bytes 4194304 | tf_op jit(solution)/shard_map/all_to_all | solution.py:124
  40.9 2.8 %copy-start = (f32[512,3072]{1,0:T(8,128)S(1)}, f32[512,3072]{1,0:T(8,128)}, u32[]{:S(2)}) copy-start(f32[512,3072]{1,0:T(8,128)} %own_ref.1) | copy-start | bytes 18874372
  57.2 22.2 %collective-permute-start.1 = (f32[256,768]{1,0:T(8,128)S(1)}, f32[256,768]{1,0:T(8,128)S(1)}, u32[]{:S(2)}, u32[]{:S(2)}) collective-permute-start(f32[256,768]{1,0:T(8,128)S(1)} %get-tuple-element.22), channel_id=1, source_target_pairs={{0,2},{1,3},{2,0},{3,1},{4,6},{5,7},{6,4},{7,5},{8,10},{9,11},{10,... | collective-permute-start | bytes 2359304 | tf_op jit(solution)/shard_map/ppermute | solution.py:27
  62.2 18.6 %collective-permute-start.5 = (f32[256,768]{1,0:T(8,128)S(1)}, f32[256,768]{1,0:T(8,128)S(1)}, u32[]{:S(2)}, u32[]{:S(2)}) collective-permute-start(f32[256,768]{1,0:T(8,128)S(1)} %get-tuple-element.24), channel_id=1, source_target_pairs={{0,6},{1,7},{2,4},{3,5},{4,2},{5,3},{6,0},{7,1},{8,14},{9,15},{10,... | collective-permute-start | bytes 2359304 | tf_op jit(solution)/shard_map/ppermute | solution.py:27
  64.9 18.7 %collective-permute-start.9 = (f32[256,768]{1,0:T(8,128)S(1)}, f32[256,768]{1,0:T(8,128)S(1)}, u32[]{:S(2)}, u32[]{:S(2)}) collective-permute-start(f32[256,768]{1,0:T(8,128)S(1)} %get-tuple-element.26), channel_id=1, source_target_pairs={{0,8},{1,9},{2,10},{3,11},{4,12},{5,13},{6,14},{7,15},{8,0},{9,1},... | collective-permute-start | bytes 2359304 | tf_op jit(solution)/shard_map/ppermute | solution.py:27
  67.7 21.4 %collective-permute-start.13 = (f32[256,768]{1,0:T(8,128)S(1)}, f32[256,768]{1,0:T(8,128)S(1)}, u32[]{:S(2)}, u32[]{:S(2)}) collective-permute-start(f32[256,768]{1,0:T(8,128)S(1)} %get-tuple-element.28), channel_id=1, source_target_pairs={{0,24},{1,25},{2,26},{3,27},{4,28},{5,29},{6,30},{7,31},{8,16},{9,... | collective-permute-start | bytes 2359304 | tf_op jit(solution)/shard_map/ppermute | solution.py:27
  79.5 10.9 %collective-permute-start.2 = (f32[128,768]{1,0:T(8,128)S(1)}, f32[128,768]{1,0:T(8,128)S(1)}, u32[]{:S(2)}, u32[]{:S(2)}) collective-permute-start(f32[128,768]{1,0:T(8,128)S(1)} %slice.113), channel_id=1, source_target_pairs={{0,6},{1,7},{2,4},{3,5},{4,2},{5,3},{6,0},{7,1},{8,14},{9,15},{10,... | collective-permute-start | bytes 1179656 | tf_op jit(solution)/shard_map/ppermute | solution.py:27
  81.0 10.5 %collective-permute-start.6 = (f32[128,768]{1,0:T(8,128)S(1)}, f32[128,768]{1,0:T(8,128)S(1)}, u32[]{:S(2)}, u32[]{:S(2)}) collective-permute-start(f32[128,768]{1,0:T(8,128)S(1)} %slice.119), channel_id=1, source_target_pairs={{0,2},{1,3},{2,0},{3,1},{4,6},{5,7},{6,4},{7,5},{8,10},{9,11},{10,... | collective-permute-start | bytes 1179656 | tf_op jit(solution)/shard_map/ppermute | solution.py:27
  83.7 13.8 %collective-permute-start.10 = (f32[128,768]{1,0:T(8,128)S(1)}, f32[128,768]{1,0:T(8,128)S(1)}, u32[]{:S(2)}, u32[]{:S(2)}) collective-permute-start(f32[128,768]{1,0:T(8,128)S(1)} %slice.125), channel_id=1, source_target_pairs={{0,24},{1,25},{2,26},{3,27},{4,28},{5,29},{6,30},{7,31},{8,16},{9,... | collective-permute-start | bytes 1179656 | tf_op jit(solution)/shard_map/ppermute | solution.py:27
  89.2 10.2 %collective-permute-start.14 = (f32[128,768]{1,0:T(8,128)S(1)}, f32[128,768]{1,0:T(8,128)S(1)}, u32[]{:S(2)}, u32[]{:S(2)}) collective-permute-start(f32[128,768]{1,0:T(8,128)S(1)} %slice.131), channel_id=1, source_target_pairs={{0,8},{1,9},{2,10},{3,11},{4,12},{5,13},{6,14},{7,15},{8,0},{9,1},... | collective-permute-start | bytes 1179656 | tf_op jit(solution)/shard_map/ppermute | solution.py:27
  90.5 10.6 %collective-permute-start.3 = (f32[64,768]{1,0:T(8,128)S(1)}, f32[64,768]{1,0:T(8,128)S(1)}, u32[]{:S(2)}, u32[]{:S(2)}) collective-permute-start(f32[64,768]{1,0:T(8,128)S(1)} %slice.115), channel_id=1, source_target_pairs={{0,8},{1,9},{2,10},{3,11},{4,12},{5,13},{6,14},{7,15},{8,0},{9,1},... | collective-permute-start | bytes 589832 | tf_op jit(solution)/shard_map/ppermute | solution.py:27
  91.6 11.3 %collective-permute-start.7 = (f32[64,768]{1,0:T(8,128)S(1)}, f32[64,768]{1,0:T(8,128)S(1)}, u32[]{:S(2)}, u32[]{:S(2)}) collective-permute-start(f32[64,768]{1,0:T(8,128)S(1)} %slice.121), channel_id=1, source_target_pairs={{0,24},{1,25},{2,26},{3,27},{4,28},{5,29},{6,30},{7,31},{8,16},{9,... | collective-permute-start | bytes 589832 | tf_op jit(solution)/shard_map/ppermute | solution.py:27
  97.6 5.8 %collective-permute-start.11 = (f32[64,768]{1,0:T(8,128)S(1)}, f32[64,768]{1,0:T(8,128)S(1)}, u32[]{:S(2)}, u32[]{:S(2)}) collective-permute-start(f32[64,768]{1,0:T(8,128)S(1)} %slice.127), channel_id=1, source_target_pairs={{0,2},{1,3},{2,0},{3,1},{4,6},{5,7},{6,4},{7,5},{8,10},{9,11},{10,... | collective-permute-start | bytes 589832 | tf_op jit(solution)/shard_map/ppermute | solution.py:27
  99.5 6.7 %collective-permute-start.15 = (f32[64,768]{1,0:T(8,128)S(1)}, f32[64,768]{1,0:T(8,128)S(1)}, u32[]{:S(2)}, u32[]{:S(2)}) collective-permute-start(f32[64,768]{1,0:T(8,128)S(1)} %slice.133), channel_id=1, source_target_pairs={{0,6},{1,7},{2,4},{3,5},{4,2},{5,3},{6,0},{7,1},{8,14},{9,15},{10,... | collective-permute-start | bytes 589832 | tf_op jit(solution)/shard_map/ppermute | solution.py:27
  101.1 12.0 %collective-permute-start.4 = (f32[32,768]{1,0:T(8,128)S(1)}, f32[32,768]{1,0:T(8,128)S(1)}, u32[]{:S(2)}, u32[]{:S(2)}) collective-permute-start(f32[32,768]{1,0:T(8,128)S(1)} %slice.117), channel_id=1, source_target_pairs={{0,24},{1,25},{2,26},{3,27},{4,28},{5,29},{6,30},{7,31},{8,16},{9,... | collective-permute-start | bytes 294920 | tf_op jit(solution)/shard_map/ppermute | solution.py:27
  102.9 10.2 %collective-permute-start.8 = (f32[32,768]{1,0:T(8,128)S(1)}, f32[32,768]{1,0:T(8,128)S(1)}, u32[]{:S(2)}, u32[]{:S(2)}) collective-permute-start(f32[32,768]{1,0:T(8,128)S(1)} %slice.123), channel_id=1, source_target_pairs={{0,8},{1,9},{2,10},{3,11},{4,12},{5,13},{6,14},{7,15},{8,0},{9,1},... | collective-permute-start | bytes 294920 | tf_op jit(solution)/shard_map/ppermute | solution.py:27
  103.4 5.3 %collective-permute-start.12 = (f32[32,768]{1,0:T(8,128)S(1)}, f32[32,768]{1,0:T(8,128)S(1)}, u32[]{:S(2)}, u32[]{:S(2)}) collective-permute-start(f32[32,768]{1,0:T(8,128)S(1)} %slice.129), channel_id=1, source_target_pairs={{0,6},{1,7},{2,4},{3,5},{4,2},{5,3},{6,0},{7,1},{8,14},{9,15},{10,... | collective-permute-start | bytes 294920 | tf_op jit(solution)/shard_map/ppermute | solution.py:27
  106.2 4.7 %collective-permute-start.16 = (f32[32,768]{1,0:T(8,128)S(1)}, f32[32,768]{1,0:T(8,128)S(1)}, u32[]{:S(2)}, u32[]{:S(2)}) collective-permute-start(f32[32,768]{1,0:T(8,128)S(1)} %slice.135), channel_id=1, source_target_pairs={{0,2},{1,3},{2,0},{3,1},{4,6},{5,7},{6,4},{7,5},{8,10},{9,11},{10,... | collective-permute-start | bytes 294920 | tf_op jit(solution)/shard_map/ppermute | solution.py:27
  110.9 6.0 %collective-permute-start.17 = (f32[32,1536]{1,0:T(8,128)S(1)}, f32[32,1536]{1,0:T(8,128)S(1)}, u32[]{:S(2)}, u32[]{:S(2)}) collective-permute-start(f32[32,1536]{1,0:T(8,128)S(1)} %pad_maximum_fusion), channel_id=1, source_target_pairs={{0,32},{1,33},{2,34},{3,35},{4,36},{5,37},{6,38},{7,39},{8,40},{9,... | collective-permute-start | bytes 589832 | tf_op jit(solution)/shard_map/ppermute | solution.py:27
  116.9 5.8 %collective-permute-start.18 = (f32[32,768]{1,0:T(8,128)S(1)}, f32[32,768]{1,0:T(8,128)S(1)}, u32[]{:S(2)}, u32[]{:S(2)}) collective-permute-start(f32[32,768]{1,0:T(8,128)S(1)} %slice.137), channel_id=1, source_target_pairs={{0,64},{1,65},{2,66},{3,67},{4,68},{5,69},{6,70},{7,71},{8,72},{9,... | collective-permute-start | bytes 294920 | tf_op jit(solution)/shard_map/ppermute | solution.py:27
  122.8 10.5 %collective-permute-start.19 = (f32[32,384]{1,0:T(8,128)S(1)}, f32[32,384]{1,0:T(8,128)S(1)}, u32[]{:S(2)}, u32[]{:S(2)}) collective-permute-start(f32[32,384]{1,0:T(8,128)S(1)} %slice.139), channel_id=1, source_target_pairs={{0,128},{1,129},{2,130},{3,131},{4,132},{5,133},{6,134},{7,135},{8... | collective-permute-start | bytes 147464 | tf_op jit(solution)/shard_map/ppermute | solution.py:27

commit v3 on v0

v3 whole, which is shorter than its diff:
```python
import functools

import jax
import jax.numpy as jnp
from jax import lax
from jax.experimental import pallas as pl
from jax.experimental.pallas import tpu as pltpu
from jax.sharding import Mesh, PartitionSpec as P

AXES = ("z", "y", "x", "core")
NZ, NY, NX = 8, 4, 4
ROWS, DEPTH, WIDTH = 32, 512, 384
GROUPS = 4
NEAR_FIRST, FAR_FIRST = (2, 1, 3, 0), (2, 3, 1, 0)
LAID = (1, 2, 3, 0, 1)
CHEAP = pl.CostEstimate(flops=1 << 20, bytes_accessed=1 << 16, transcendentals=0)
VMEM = pl.BlockSpec(memory_space=pltpu.VMEM)


def flip(axis, mask):
    pairs = []
    for i in range(NZ * NY * NX * 2):
        at = {"z": i // 32, "y": i // 8 % 4, "x": i // 2 % 4, "core": i % 2}
        at[axis] ^= mask
        pairs.append((i, ((at["z"] * 4 + at["y"]) * 4 + at["x"]) * 2 + at["core"]))
    return pairs


def exchange(value, axis, mask):
    return lax.ppermute(value, AXES, flip(axis, mask))


def split(value):
    high = value.astype(jnp.bfloat16)
    return high, (value - high.astype(jnp.float32)).astype(jnp.bfloat16)


def relayout_kernel(a_ref, out_ref):
    for i in range(NY * NX):
        out_ref[i] = a_ref[:, pl.ds(i * 2 * DEPTH, 2 * DEPTH)]


def relayout(a):
    return pl.pallas_call(
        relayout_kernel,
        out_shape=jax.ShapeDtypeStruct((NY * NX, ROWS, 2 * DEPTH), jnp.float32),
        in_specs=[VMEM],
        out_specs=VMEM,
        compiler_params=pltpu.CompilerParams(vmem_limit_bytes=4 << 20),
        cost_estimate=CHEAP,
    )(a)


def prepare_kernel(outer, where, a_ref, b_ref, hi_ref, lo_ref, b0_ref, b1_ref, sems):
    copies = []
    for i, to in enumerate((b0_ref, b1_ref)):
        group = i if outer == "x" else i + 2
        cols = pl.ds(group * 2 * WIDTH, 2 * WIDTH)
        copies.append(pltpu.make_async_copy(b_ref.at[:, cols], to, sems.at[i]))
        copies[i].start()
    own = pl.multiple_of(where[2] * DEPTH, DEPTH)
    other = pl.multiple_of((1 - where[2]) * DEPTH, DEPTH)
    for i in range(5 * 4):
        q = (LAID[i // 4], LAID[i % 4])
        qy, qx = q if outer == "y" else q[::-1]
        source = (where[0] ^ qy) * 4 + (where[1] ^ qx)
        rows = pl.ds(pl.multiple_of(source * ROWS, ROWS), ROWS)
        to = pl.ds(i * ROWS, ROWS)
        for half, start in enumerate((own, other)):
            high, low = split(a_ref[rows, pl.ds(start, DEPTH)])
            hi_ref[to, pl.ds(half * DEPTH, DEPTH)] = high
            lo_ref[to, pl.ds(half * DEPTH, DEPTH)] = low
    for copy in copies:
        copy.wait()


def prepare(outer, where, a, oth):
    part = jax.ShapeDtypeStruct((20 * ROWS, 2 * DEPTH), jnp.bfloat16)
    cols = jax.ShapeDtypeStruct((DEPTH, 2 * WIDTH), jnp.float32)
    hi, lo, *b = pl.pallas_call(
        functools.partial(prepare_kernel, outer),
        out_shape=(part, part, cols, cols),
        in_specs=[pl.BlockSpec(memory_space=pltpu.SMEM), VMEM, pl.BlockSpec(memory_space=pl.ANY)],
        out_specs=(VMEM,) * 4,
        scratch_shapes=[pltpu.SemaphoreType.DMA((2,))],
        compiler_params=pltpu.CompilerParams(vmem_limit_bytes=10 << 20),
        cost_estimate=CHEAP,
    )(where, a, oth)
    return (hi, lo), b


def product_kernel(group, first, order, hi_ref, lo_ref, own_ref, oth_ref, out_ref):
    rows = pl.ds(first * 4 * ROWS, 8 * ROWS)
    cols = pl.ds(group * 2 * WIDTH, 2 * WIDTH)
    dot = functools.partial(jnp.dot, preferred_element_type=jnp.float32)
    total = None
    for half, ref in enumerate((own_ref, oth_ref)):
        depth = pl.ds(half * DEPTH, DEPTH)
        a_hi, a_lo = hi_ref[rows, depth], lo_ref[rows, depth]
        b_hi, b_lo = split(ref[...] if half else ref[:, cols])
        part = dot(a_hi, b_hi) + dot(a_lo, b_hi) + dot(a_hi, b_lo)
        total = part if total is None else total + part
    for i, at in enumerate(order):
        out_ref[pl.ds(i * ROWS, ROWS), :] = total[at * ROWS : (at + 1) * ROWS]


def half_plan(group, half):
    blocks = (NEAR_FIRST, FAR_FIRST)[group % 2]
    outer = blocks[2 * half : 2 * half + 2]
    first = min(f for f in range(4) if set(LAID[f : f + 2]) == set(outer))
    laid = [(o, i) for o in LAID[first : first + 2] for i in LAID[:4]]
    return first, [laid.index((o, i)) for o in outer for i in blocks]


def product(group, half, a, own, oth):
    return pl.pallas_call(
        functools.partial(product_kernel, group, *half_plan(group, half)),
        out_shape=jax.ShapeDtypeStruct((8 * ROWS, 2 * WIDTH), jnp.float32),
        in_specs=[VMEM] * 4,
        out_specs=VMEM,
        compiler_params=pltpu.CompilerParams(vmem_limit_bytes=6 << 20),
        cost_estimate=CHEAP,
    )(*a, own, oth)


def body(amplitudes, integrals):
    z, y, x, core = (lax.axis_index(name) for name in AXES)
    oth = exchange(integrals, "core", 1)
    where = jnp.stack([y, x, core]).astype(jnp.int32)
    halves = [((z & 1) ^ v) * 4 * WIDTH for v in range(2)]
    blocks = [((z >> 1) ^ v) * WIDTH for v in range(4)]
    where, halves, blocks, laid = lax.optimization_barrier((where, halves, blocks, relayout(amplitudes)))
    mine = lax.all_to_all(laid, ("y", "x"), split_axis=0, concat_axis=0)
    mine = mine.reshape(NY * NX * ROWS, 2 * DEPTH)
    a_x, oth_x = prepare("x", where, mine, oth)
    a_y, oth_y = prepare("y", where, mine, oth)
    parts = []
    for group in range(GROUPS):
        a = a_x if group < 2 else a_y
        masks = ((1, 3), (3, 1))[group % 2]
        b = (oth_x + oth_y)[group]
        send = product(group, 0, a, integrals, b)
        keep = product(group, 1, a, integrals, b)
        for axis in ("x", "y") if group < 2 else ("y", "x"):
            for mask in masks:
                total = keep + exchange(send, axis, mask)
                half = total.shape[0] // 2
                send, keep = total[:half], total[half:]
        parts.append(total)
    cut = functools.partial(lax.dynamic_slice_in_dim, axis=1, allow_negative_indices=False)
    parts = [part[:, i * WIDTH : (i + 1) * WIDTH] for i in range(2) for part in parts]
    both = jnp.concatenate(parts, 1)
    keep, send = (cut(both, start, 4 * WIDTH) for start in halves)
    keep = keep + exchange(send, "z", 1)
    block = lambda v: cut(keep, blocks[v], WIDTH)
    far = [exchange(block(v), "z", 2 * v) for v in (2, 1, 3)]
    return 0.5 * (block(0) + far[0] + far[1] + far[2])


def solution(mesh):
    chips = Mesh(mesh.devices.reshape(NZ, NY, NX, 2), AXES)
    return jax.shard_map(
        body,
        mesh=chips,
        in_specs=(P(("y", "x", "core"), "z"), P(AXES, None)),
        out_specs=P(("y", "x", "core"), "z"),
        check_vma=False,
    )
```

time: 226 us -> 117 us (0.52)
  waiting for transfers between devices: 151 us -> 29.7 us
  starting transfers between devices: 0.04 us -> 30.7 us
  matrix products: 22.7 us -> 0 us
  Pallas kernels: 0 us -> 17.3 us
  between operations: 13.4 us -> 0.4 us
    reduce_scatter x2 -> x0, waiting for transfers between devices: 151 us -> none  [the longest x1 112 us: body(): lax.psum_scatter(jnp.dot(received, integrals, precision=lax.Precision.HIG...]
    ppermute x0 -> x21, starting transfers between devices: none -> 30.7 us  [exchange(): return lax.ppermute(value, AXES, flip(axis, mask))]
    ppermute x0 -> x21, waiting for transfers between devices: none -> 29.7 us  [exchange(): return lax.ppermute(value, AXES, flip(axis, mask))]
    dot_general x1 -> x0, matrix products: 22.7 us -> none  [body(): jnp.dot(received, integrals, precision=lax.Precision.HIGHEST, preferred_e...]
    pallas_call x0 -> x11, Pallas kernels: none -> 17.3 us  [the longest x8 12.2 us: product(): pl.pallas_call(functools.partial(product_kernel, group, *half_plan(group,...]
  transfers between devices with their start and end apart: 2 -> 21, of which waited for: 2 -> 10; matrix products, arithmetic and copies ran while one was open for 0% -> 1% of each run, Pallas kernels for 0% -> 11%
where the time goes in v3:
time: 117 us
  blocking collectives  35.4 us (30%)
  starting transfers between devices  30.7 us (26%)
  waiting for transfers between devices  29.7 us (25%)
  Pallas kernels  17.3 us (15%)
  local copies, waits for them, and re-layouts  2.08 us (2%)
  other arithmetic  1.64 us (1%)
    all_to_all x1, blocking collectives, body(): mine = lax.all_to_all(laid, ('y', 'x'), split_axis=0, concat_axis=0)  35.4 us
    ppermute x21, starting transfers between devices, exchange(): return lax.ppermute(value, AXES, flip(axis, mask))  30.7 us
    ppermute x21, waiting for transfers between devices, exchange(): return lax.ppermute(value, AXES, flip(axis, mask))  29.7 us
    pallas_call x8, Pallas kernels, product(): pl.pallas_call(functools.partial(product_kernel, group, *half_plan(group,...  12.2 us
    pallas_call x2, Pallas kernels, prepare(): pl.pallas_call(functools.partial(prepare_kernel, outer), out_shape=(part,...  4.98 us
  transfers between devices with their start and end apart: 21, of which 10 were waited for; matrix products, arithmetic and copies ran while one was open for 1% of the time, Pallas kernels for 11%

profile of v3, /device:TPU:2, one launch (start us, length us, event | category | flops | bytes accessed | tf_op | source)
XLA Modules:
  0.0 117.2 jit_solution(14223679862551329637)
XLA Ops:
  0.0 1.6 %copy-done = f32[32,16384]{1,0:T(8,128)S(1)} copy-done((f32[32,16384]{1,0:T(8,128)S(1)}, f32[32,16384]{1,0:T(8,128)}, u32[]{:S(2)}) %copy-start) | copy-done | bytes 2097176
  1.6 0.1 shard_map.28
  1.8 35.4 %all_to_all.5 = f32[16,32,1024]{2,1,0:T(8,128)S(1)} all-to-all(f32[16,32,1024]{2,1,0:T(8,128)S(1)} %shard_map.28), channel_id=1, replica_groups=mesh['z'=8,'y'=4,'x'=4,'core'=2] {'y','x'}, dimensions={0} | all-to-all | bytes 4194304 | tf_op jit(solution)/shard_map/all_to_all | solution.py:133
  37.2 2.5 %shard_map.29 = (bf16[640,1024]{1,0:T(8,128)(2,1)S(1)}, bf16[640,1024]{1,0:T(8,128)(2,1)S(1)}, f32[512,768]{1,0:T(8,128)S(1)}, f32[512,768]{1,0:T(8,128)S(1)}) custom-call(s32[3]{0:T(128)S(1)} %pad_add_fusion.where, f32[512,1024]{1,0:T(8,128)S(1)} %bitcast.6, f32[512,3072]{1,0:T(8,128)} %collective-permute-done.b_ref), custom_call_target="tpu_custom_call" | custom-call | flops 1048576 | bytes 65536 | tf_op jit(solution)/shard_map/pallas_call | solution.py:80
  39.7 1.5 %shard_map.31 = f32[256,768]{1,0:T(8,128)S(1)} custom-call(bf16[640,1024]{1,0:T(8,128)(2,1)S(1)} %get-tuple-element.23.hi_ref, bf16[640,1024]{1,0:T(8,128)(2,1)S(1)} %get-tuple-element.24.lo_ref, f32[512,3072]{1,0:T(8,128)S(1)} %bitcast.5, f32[512,768]{1,0:T(8,128)S(1)} %get-tuple-element.25.oth_ref), custom_call_target="tpu_custom_call" | custom-call | flops 1048576 | bytes 65536 | tf_op jit(solution)/shard_map/pallas_call | solution.py:116
  41.3 1.5 %collective-permute-start.1 = (f32[256,768]{1,0:T(8,128)S(1)}, f32[256,768]{1,0:T(8,128)S(1)}, u32[]{:S(2)}, u32[]{:S(2)}) collective-permute-start(f32[256,768]{1,0:T(8,128)S(1)} %shard_map.31), channel_id=1, source_target_pairs={{0,2},{1,3},{2,0},{3,1},{4,6},{5,7},{6,4},{7,5},{8,10},{9,11},{10,... | collective-permute-start | bytes 2359304 | tf_op jit(solution)/shard_map/ppermute | solution.py:30
  42.8 1.5 %shard_map.33 = f32[256,768]{1,0:T(8,128)S(1)} custom-call(bf16[640,1024]{1,0:T(8,128)(2,1)S(1)} %get-tuple-element.23.hi_ref, bf16[640,1024]{1,0:T(8,128)(2,1)S(1)} %get-tuple-element.24.lo_ref, f32[512,3072]{1,0:T(8,128)S(1)} %bitcast.5, f32[512,768]{1,0:T(8,128)S(1)} %get-tuple-element.26.oth_ref), custom_call_target="tpu_custom_call" | custom-call | flops 1048576 | bytes 65536 | tf_op jit(solution)/shard_map/pallas_call | solution.py:116
  44.3 0.1 collective-permute-start.5
  44.4 2.4 %shard_map.34 = (bf16[640,1024]{1,0:T(8,128)(2,1)S(1)}, bf16[640,1024]{1,0:T(8,128)(2,1)S(1)}, f32[512,768]{1,0:T(8,128)S(1)}, f32[512,768]{1,0:T(8,128)S(1)}) custom-call(s32[3]{0:T(128)S(1)} %pad_add_fusion.where, f32[512,1024]{1,0:T(8,128)S(1)} %bitcast.7, f32[512,3072]{1,0:T(8,128)} %collective-permute-done.b_ref), custom_call_target="tpu_custom_call" | custom-call | flops 1048576 | bytes 65536 | tf_op jit(solution)/shard_map/pallas_call | solution.py:80
  46.9 1.5 %shard_map.36 = f32[256,768]{1,0:T(8,128)S(1)} custom-call(bf16[640,1024]{1,0:T(8,128)(2,1)S(1)} %get-tuple-element.27.hi_ref, bf16[640,1024]{1,0:T(8,128)(2,1)S(1)} %get-tuple-element.28.lo_ref, f32[512,3072]{1,0:T(8,128)S(1)} %bitcast.5, f32[512,768]{1,0:T(8,128)S(1)} %get-tuple-element.29.oth_ref), custom_call_target="tpu_custom_call" | custom-call | flops 1048576 | bytes 65536 | tf_op jit(solution)/shard_map/pallas_call | solution.py:116
  48.4 0.6 collective-permute-start.9
  49.1 1.5 %shard_map.38 = f32[256,768]{1,0:T(8,128)S(1)} custom-call(bf16[640,1024]{1,0:T(8,128)(2,1)S(1)} %get-tuple-element.27.hi_ref, bf16[640,1024]{1,0:T(8,128)(2,1)S(1)} %get-tuple-element.28.lo_ref, f32[512,3072]{1,0:T(8,128)S(1)} %bitcast.5, f32[512,768]{1,0:T(8,128)S(1)} %get-tuple-element.30.oth_ref), custom_call_target="tpu_custom_call" | custom-call | flops 1048576 | bytes 65536 | tf_op jit(solution)/shard_map/pallas_call | solution.py:116
  50.6 1.5 %collective-permute-start.13 = (f32[256,768]{1,0:T(8,128)S(1)}, f32[256,768]{1,0:T(8,128)S(1)}, u32[]{:S(2)}, u32[]{:S(2)}) collective-permute-start(f32[256,768]{1,0:T(8,128)S(1)} %shard_map.38), channel_id=1, source_target_pairs={{0,24},{1,25},{2,26},{3,27},{4,28},{5,29},{6,30},{7,31},{8,16},{9,... | collective-permute-start | bytes 2359304 | tf_op jit(solution)/shard_map/ppermute | solution.py:30
  52.1 1.5 %shard_map.30 = f32[256,768]{1,0:T(8,128)S(1)} custom-call(bf16[640,1024]{1,0:T(8,128)(2,1)S(1)} %get-tuple-element.23.hi_ref, bf16[640,1024]{1,0:T(8,128)(2,1)S(1)} %get-tuple-element.24.lo_ref, f32[512,3072]{1,0:T(8,128)S(1)} %bitcast.5, f32[512,768]{1,0:T(8,128)S(1)} %get-tuple-element.25.oth_ref), custom_call_target="tpu_custom_call" | custom-call | flops 1048576 | bytes 65536 | tf_op jit(solution)/shard_map/pallas_call | solution.py:116
  53.7 6.3 %collective-permute-done.1 = f32[256,768]{1,0:T(8,128)S(1)} collective-permute-done((f32[256,768]{1,0:T(8,128)S(1)}, f32[256,768]{1,0:T(8,128)S(1)}, u32[]{:S(2)}, u32[]{:S(2)}) %collective-permute-start.1) | collective-permute-done | bytes 786464 | tf_op jit(solution)/shard_map/ppermute | solution.py:30
  60.1 1.1 collective-permute-start.2
  61.1 1.5 %shard_map.32 = f32[256,768]{1,0:T(8,128)S(1)} custom-call(bf16[640,1024]{1,0:T(8,128)(2,1)S(1)} %get-tuple-element.23.hi_ref, bf16[640,1024]{1,0:T(8,128)(2,1)S(1)} %get-tuple-element.24.lo_ref, f32[512,3072]{1,0:T(8,128)S(1)} %bitcast.5, f32[512,768]{1,0:T(8,128)S(1)} %get-tuple-element.26.oth_ref), custom_call_target="tpu_custom_call" | custom-call | flops 1048576 | bytes 65536 | tf_op jit(solution)/shard_map/pallas_call | solution.py:116
  62.7 1.5 %collective-permute-done.5 = f32[256,768]{1,0:T(8,128)S(1)} collective-permute-done((f32[256,768]{1,0:T(8,128)S(1)}, f32[256,768]{1,0:T(8,128)S(1)}, u32[]{:S(2)}, u32[]{:S(2)}) %collective-permute-start.5) | collective-permute-done | bytes 786464 | tf_op jit(solution)/shard_map/ppermute | solution.py:30
  64.3 1.4 %collective-permute-start.6 = (f32[128,768]{1,0:T(8,128)S(1)}, f32[128,768]{1,0:T(8,128)S(1)}, u32[]{:S(2)}, u32[]{:S(2)}) collective-permute-start(f32[128,768]{1,0:T(8,128)S(1)} %slice.136), channel_id=1, source_target_pairs={{0,2},{1,3},{2,0},{3,1},{4,6},{5,7},{6,4},{7,5},{8,10},{9,11},{10,... | collective-permute-start | bytes 1179656 | tf_op jit(solution)/shard_map/ppermute | solution.py:30
  65.7 1.5 %shard_map.35 = f32[256,768]{1,0:T(8,128)S(1)} custom-call(bf16[640,1024]{1,0:T(8,128)(2,1)S(1)} %get-tuple-element.27.hi_ref, bf16[640,1024]{1,0:T(8,128)(2,1)S(1)} %get-tuple-element.28.lo_ref, f32[512,3072]{1,0:T(8,128)S(1)} %bitcast.5, f32[512,768]{1,0:T(8,128)S(1)} %get-tuple-element.29.oth_ref), custom_call_target="tpu_custom_call" | custom-call | flops 1048576 | bytes 65536 | tf_op jit(solution)/shard_map/pallas_call | solution.py:116
  67.3 1.5 %shard_map.37 = f32[256,768]{1,0:T(8,128)S(1)} custom-call(bf16[640,1024]{1,0:T(8,128)(2,1)S(1)} %get-tuple-element.27.hi_ref, bf16[640,1024]{1,0:T(8,128)(2,1)S(1)} %get-tuple-element.28.lo_ref, f32[512,3072]{1,0:T(8,128)S(1)} %bitcast.5, f32[512,768]{1,0:T(8,128)S(1)} %get-tuple-element.30.oth_ref), custom_call_target="tpu_custom_call" | custom-call | flops 1048576 | bytes 65536 | tf_op jit(solution)/shard_map/pallas_call | solution.py:116
  68.8 0.1 add.68
  68.9 0.9 collective-permute-start.10
  69.9 0.1 add.72
  70.0 2.1 %collective-permute-start.14 = (f32[128,768]{1,0:T(8,128)S(1)}, f32[128,768]{1,0:T(8,128)S(1)}, u32[]{:S(2)}, u32[]{:S(2)}) collective-permute-start(f32[128,768]{1,0:T(8,128)S(1)} %slice.150), channel_id=1, source_target_pairs={{0,8},{1,9},{2,10},{3,11},{4,12},{5,13},{6,14},{7,15},{8,0},{9,1},... | collective-permute-start | bytes 1179656 | tf_op jit(solution)/shard_map/ppermute | solution.py:30
  72.2 0.1 collective-permute-start.3
  72.3 0.7 collective-permute-done.6
  73.1 1.8 %collective-permute-start.7 = (f32[64,768]{1,0:T(8,128)S(1)}, f32[64,768]{1,0:T(8,128)S(1)}, u32[]{:S(2)}, u32[]{:S(2)}) collective-permute-start(f32[64,768]{1,0:T(8,128)S(1)} %slice.138), channel_id=1, source_target_pairs={{0,24},{1,25},{2,26},{3,27},{4,28},{5,29},{6,30},{7,31},{8,16},{9,... | collective-permute-start | bytes 589832 | tf_op jit(solution)/shard_map/ppermute | solution.py:30
  74.9 5.3 %collective-permute-done.10 = f32[128,768]{1,0:T(8,128)S(1)} collective-permute-done((f32[128,768]{1,0:T(8,128)S(1)}, f32[128,768]{1,0:T(8,128)S(1)}, u32[]{:S(2)}, u32[]{:S(2)}) %collective-permute-start.10) | collective-permute-done | bytes 393248 | tf_op jit(solution)/shard_map/ppermute | solution.py:30
  80.2 2.0 %collective-permute-start.11 = (f32[64,768]{1,0:T(8,128)S(1)}, f32[64,768]{1,0:T(8,128)S(1)}, u32[]{:S(2)}, u32[]{:S(2)}) collective-permute-start(f32[64,768]{1,0:T(8,128)S(1)} %slice.145), channel_id=1, source_target_pairs={{0,2},{1,3},{2,0},{3,1},{4,6},{5,7},{6,4},{7,5},{8,10},{9,11},{10,... | collective-permute-start | bytes 589832 | tf_op jit(solution)/shard_map/ppermute | solution.py:30
  82.3 1.1 collective-permute-start.15
  83.5 1.2 collective-permute-start.4
  84.8 2.2 %collective-permute-done.11 = f32[64,768]{1,0:T(8,128)S(1)} collective-permute-done((f32[64,768]{1,0:T(8,128)S(1)}, f32[64,768]{1,0:T(8,128)S(1)}, u32[]{:S(2)}, u32[]{:S(2)}) %collective-permute-start.11) | collective-permute-done | bytes 196640 | tf_op jit(solution)/shard_map/ppermute | solution.py:30
  87.0 2.2 %collective-permute-start.12 = (f32[32,768]{1,0:T(8,128)S(1)}, f32[32,768]{1,0:T(8,128)S(1)}, u32[]{:S(2)}, u32[]{:S(2)}) collective-permute-start(f32[32,768]{1,0:T(8,128)S(1)} %slice.147), channel_id=1, source_target_pairs={{0,6},{1,7},{2,4},{3,5},{4,2},{5,3},{6,0},{7,1},{8,14},{9,15},{10,... | collective-permute-start | bytes 294920 | tf_op jit(solution)/shard_map/ppermute | solution.py:30
  89.2 1.5 %collective-permute-start.16 = (f32[32,768]{1,0:T(8,128)S(1)}, f32[32,768]{1,0:T(8,128)S(1)}, u32[]{:S(2)}, u32[]{:S(2)}) collective-permute-start(f32[32,768]{1,0:T(8,128)S(1)} %slice.154), channel_id=1, source_target_pairs={{0,2},{1,3},{2,0},{3,1},{4,6},{5,7},{6,4},{7,5},{8,10},{9,11},{10,... | collective-permute-start | bytes 294920 | tf_op jit(solution)/shard_map/ppermute | solution.py:30
  90.8 1.0 collective-permute-done.12
  91.8 2.1 %collective-permute-done.16 = f32[32,768]{1,0:T(8,128)S(1)} collective-permute-done((f32[32,768]{1,0:T(8,128)S(1)}, f32[32,768]{1,0:T(8,128)S(1)}, u32[]{:S(2)}, u32[]{:S(2)}) %collective-permute-start.16) | collective-permute-done | bytes 98336 | tf_op jit(solution)/shard_map/ppermute | solution.py:30
  94.0 0.1 constant_dynamic-slice_fusion.3
  94.1 2.0 %collective-permute-start.17 = (f32[32,1536]{1,0:T(8,128)S(1)}, f32[32,1536]{1,0:T(8,128)S(1)}, u32[]{:S(2)}, u32[]{:S(2)}) collective-permute-start(f32[32,1536]{1,0:T(8,128)S(1)} %constant_dynamic-slice_fusion.3), channel_id=1, source_target_pairs={{0,32},{1,33},{2,34},{3,35},{4,36},{5,37},{6,38},{7,39},{8,40},{9,... | collective-permute-start | bytes 589832 | tf_op jit(solution)/shard_map/ppermute | solution.py:30
  96.1 3.8 %collective-permute-done.17 = f32[32,1536]{1,0:T(8,128)S(1)} collective-permute-done((f32[32,1536]{1,0:T(8,128)S(1)}, f32[32,1536]{1,0:T(8,128)S(1)}, u32[]{:S(2)}, u32[]{:S(2)}) %collective-permute-start.17) | collective-permute-done | bytes 196640 | tf_op jit(solution)/shard_map/ppermute | solution.py:30
  99.9 0.1 dynamic-slice_add_fusion
  100.0 0.1 constant_dynamic-slice_fusion.2
  100.1 7.0 %collective-permute-start.20 = (f32[32,384]{1,0:T(8,128)S(1)}, f32[32,384]{1,0:T(8,128)S(1)}, u32[]{:S(2)}, u32[]{:S(2)}) collective-permute-start(f32[32,384]{1,0:T(8,128)S(1)} %get-tuple-element.38), channel_id=1, source_target_pairs={{0,192},{1,193},{2,194},{3,195},{4,196},{5,197},{6,198},{7,199},{8... | collective-permute-start | bytes 147464 | tf_op jit(solution)/shard_map/ppermute | solution.py:30
  107.1 0.8 collective-permute-start.19
  107.9 1.6 %collective-permute-start.18 = (f32[32,384]{1,0:T(8,128)S(1)}, f32[32,384]{1,0:T(8,128)S(1)}, u32[]{:S(2)}, u32[]{:S(2)}) collective-permute-start(f32[32,384]{1,0:T(8,128)S(1)} %get-tuple-element.37), channel_id=1, source_target_pairs={{0,128},{1,129},{2,130},{3,131},{4,132},{5,133},{6,134},{7,135},{8... | collective-permute-start | bytes 147464 | tf_op jit(solution)/shard_map/ppermute | solution.py:30
  109.6 2.9 %collective-permute-done.19 = f32[32,384]{1,0:T(8,128)S(1)} collective-permute-done((f32[32,384]{1,0:T(8,128)S(1)}, f32[32,384]{1,0:T(8,128)S(1)}, u32[]{:S(2)}, u32[]{:S(2)}) %collective-permute-start.19) | collective-permute-done | bytes 49184 | tf_op jit(solution)/shard_map/ppermute | solution.py:30
  112.5 4.0 %collective-permute-done.18 = f32[32,384]{1,0:T(8,128)S(1)} collective-permute-done((f32[32,384]{1,0:T(8,128)S(1)}, f32[32,384]{1,0:T(8,128)S(1)}, u32[]{:S(2)}, u32[]{:S(2)}) %collective-permute-start.18) | collective-permute-done | bytes 49184 | tf_op jit(solution)/shard_map/ppermute | solution.py:30
  116.5 0.7 add_multiply_fusion
  (54 shorter events, 1.0 us)
Async XLA Ops:
  0.0 37.2 %collective-permute-start = (f32[512,3072]{1,0:T(8,128)}, f32[512,3072]{1,0:T(8,128)}, u32[]{:S(2)}, u32[]{:S(2)}) collective-permute-start(f32[512,3072]{1,0:T(8,128)} %own_ref.15), channel_id=1, source_target_pairs={{0,1},{1,0},{2,3},{3,2},{4,5},{5,4},{6,7},{7,6},{8,9},{9,8},{10,11... | collective-permute-start | bytes 18874376 | tf_op jit(solution)/shard_map/ppermute | solution.py:30
  0.0 1.6 %copy-start = (f32[32,16384]{1,0:T(8,128)S(1)}, f32[32,16384]{1,0:T(8,128)}, u32[]{:S(2)}) copy-start(f32[32,16384]{1,0:T(8,128)} %a_ref.1) | copy-start | bytes 6291460
  1.8 37.9 %slice-start = ((s8[6291456]{0:T(1024)(128)(4,1)}), s8[4194304]{0:T(1024)(128)(4,1)S(1)}, s32[]{:S(2)}) async-start(s8[6291456]{0:T(1024)(128)(4,1)} %bitcast.4), calls=%async_computation.1 | async-start | bytes 8388608
  37.2 2.6 %slice-start.1 = ((s8[6291456]{0:T(1024)(128)(4,1)}), s8[2097152]{0:T(1024)(128)(4,1)S(1)}, s32[]{:S(2)}) async-start(s8[6291456]{0:T(1024)(128)(4,1)} %bitcast.4), calls=%async_computation.2 | async-start | bytes 4194304
  41.3 18.6 %collective-permute-start.1 = (f32[256,768]{1,0:T(8,128)S(1)}, f32[256,768]{1,0:T(8,128)S(1)}, u32[]{:S(2)}, u32[]{:S(2)}) collective-permute-start(f32[256,768]{1,0:T(8,128)S(1)} %shard_map.31), channel_id=1, source_target_pairs={{0,2},{1,3},{2,0},{3,1},{4,6},{5,7},{6,4},{7,5},{8,10},{9,11},{10,... | collective-permute-start | bytes 2359304 | tf_op jit(solution)/shard_map/ppermute | solution.py:30
  44.3 19.8 %collective-permute-start.5 = (f32[256,768]{1,0:T(8,128)S(1)}, f32[256,768]{1,0:T(8,128)S(1)}, u32[]{:S(2)}, u32[]{:S(2)}) collective-permute-start(f32[256,768]{1,0:T(8,128)S(1)} %shard_map.33), channel_id=1, source_target_pairs={{0,6},{1,7},{2,4},{3,5},{4,2},{5,3},{6,0},{7,1},{8,14},{9,15},{10,... | collective-permute-start | bytes 2359304 | tf_op jit(solution)/shard_map/ppermute | solution.py:30
  48.4 20.4 %collective-permute-start.9 = (f32[256,768]{1,0:T(8,128)S(1)}, f32[256,768]{1,0:T(8,128)S(1)}, u32[]{:S(2)}, u32[]{:S(2)}) collective-permute-start(f32[256,768]{1,0:T(8,128)S(1)} %shard_map.36), channel_id=1, source_target_pairs={{0,8},{1,9},{2,10},{3,11},{4,12},{5,13},{6,14},{7,15},{8,0},{9,1},... | collective-permute-start | bytes 2359304 | tf_op jit(solution)/shard_map/ppermute | solution.py:30
  50.6 19.3 %collective-permute-start.13 = (f32[256,768]{1,0:T(8,128)S(1)}, f32[256,768]{1,0:T(8,128)S(1)}, u32[]{:S(2)}, u32[]{:S(2)}) collective-permute-start(f32[256,768]{1,0:T(8,128)S(1)} %shard_map.38), channel_id=1, source_target_pairs={{0,24},{1,25},{2,26},{3,27},{4,28},{5,29},{6,30},{7,31},{8,16},{9,... | collective-permute-start | bytes 2359304 | tf_op jit(solution)/shard_map/ppermute | solution.py:30
  60.1 12.1 %collective-permute-start.2 = (f32[128,768]{1,0:T(8,128)S(1)}, f32[128,768]{1,0:T(8,128)S(1)}, u32[]{:S(2)}, u32[]{:S(2)}) collective-permute-start(f32[128,768]{1,0:T(8,128)S(1)} %slice.129), channel_id=1, source_target_pairs={{0,6},{1,7},{2,4},{3,5},{4,2},{5,3},{6,0},{7,1},{8,14},{9,15},{10,... | collective-permute-start | bytes 1179656 | tf_op jit(solution)/shard_map/ppermute | solution.py:30
  64.3 8.7 %collective-permute-start.6 = (f32[128,768]{1,0:T(8,128)S(1)}, f32[128,768]{1,0:T(8,128)S(1)}, u32[]{:S(2)}, u32[]{:S(2)}) collective-permute-start(f32[128,768]{1,0:T(8,128)S(1)} %slice.136), channel_id=1, source_target_pairs={{0,2},{1,3},{2,0},{3,1},{4,6},{5,7},{6,4},{7,5},{8,10},{9,11},{10,... | collective-permute-start | bytes 1179656 | tf_op jit(solution)/shard_map/ppermute | solution.py:30
  68.9 11.2 %collective-permute-start.10 = (f32[128,768]{1,0:T(8,128)S(1)}, f32[128,768]{1,0:T(8,128)S(1)}, u32[]{:S(2)}, u32[]{:S(2)}) collective-permute-start(f32[128,768]{1,0:T(8,128)S(1)} %slice.143), channel_id=1, source_target_pairs={{0,24},{1,25},{2,26},{3,27},{4,28},{5,29},{6,30},{7,31},{8,16},{9,... | collective-permute-start | bytes 1179656 | tf_op jit(solution)/shard_map/ppermute | solution.py:30
  70.0 12.2 %collective-permute-start.14 = (f32[128,768]{1,0:T(8,128)S(1)}, f32[128,768]{1,0:T(8,128)S(1)}, u32[]{:S(2)}, u32[]{:S(2)}) collective-permute-start(f32[128,768]{1,0:T(8,128)S(1)} %slice.150), channel_id=1, source_target_pairs={{0,8},{1,9},{2,10},{3,11},{4,12},{5,13},{6,14},{7,15},{8,0},{9,1},... | collective-permute-start | bytes 1179656 | tf_op jit(solution)/shard_map/ppermute | solution.py:30
  72.2 11.2 %collective-permute-start.3 = (f32[64,768]{1,0:T(8,128)S(1)}, f32[64,768]{1,0:T(8,128)S(1)}, u32[]{:S(2)}, u32[]{:S(2)}) collective-permute-start(f32[64,768]{1,0:T(8,128)S(1)} %slice.131), channel_id=1, source_target_pairs={{0,8},{1,9},{2,10},{3,11},{4,12},{5,13},{6,14},{7,15},{8,0},{9,1},... | collective-permute-start | bytes 589832 | tf_op jit(solution)/shard_map/ppermute | solution.py:30
  73.1 11.6 %collective-permute-start.7 = (f32[64,768]{1,0:T(8,128)S(1)}, f32[64,768]{1,0:T(8,128)S(1)}, u32[]{:S(2)}, u32[]{:S(2)}) collective-permute-start(f32[64,768]{1,0:T(8,128)S(1)} %slice.138), channel_id=1, source_target_pairs={{0,24},{1,25},{2,26},{3,27},{4,28},{5,29},{6,30},{7,31},{8,16},{9,... | collective-permute-start | bytes 589832 | tf_op jit(solution)/shard_map/ppermute | solution.py:30
  80.2 6.7 %collective-permute-start.11 = (f32[64,768]{1,0:T(8,128)S(1)}, f32[64,768]{1,0:T(8,128)S(1)}, u32[]{:S(2)}, u32[]{:S(2)}) collective-permute-start(f32[64,768]{1,0:T(8,128)S(1)} %slice.145), channel_id=1, source_target_pairs={{0,2},{1,3},{2,0},{3,1},{4,6},{5,7},{6,4},{7,5},{8,10},{9,11},{10,... | collective-permute-start | bytes 589832 | tf_op jit(solution)/shard_map/ppermute | solution.py:30
  82.3 6.9 %collective-permute-start.15 = (f32[64,768]{1,0:T(8,128)S(1)}, f32[64,768]{1,0:T(8,128)S(1)}, u32[]{:S(2)}, u32[]{:S(2)}) collective-permute-start(f32[64,768]{1,0:T(8,128)S(1)} %slice.152), channel_id=1, source_target_pairs={{0,6},{1,7},{2,4},{3,5},{4,2},{5,3},{6,0},{7,1},{8,14},{9,15},{10,... | collective-permute-start | bytes 589832 | tf_op jit(solution)/shard_map/ppermute | solution.py:30
  83.5 7.2 %collective-permute-start.4 = (f32[32,768]{1,0:T(8,128)S(1)}, f32[32,768]{1,0:T(8,128)S(1)}, u32[]{:S(2)}, u32[]{:S(2)}) collective-permute-start(f32[32,768]{1,0:T(8,128)S(1)} %slice.133), channel_id=1, source_target_pairs={{0,24},{1,25},{2,26},{3,27},{4,28},{5,29},{6,30},{7,31},{8,16},{9,... | collective-permute-start | bytes 294920 | tf_op jit(solution)/shard_map/ppermute | solution.py:30
  84.7 6.1 %collective-permute-start.8 = (f32[32,768]{1,0:T(8,128)S(1)}, f32[32,768]{1,0:T(8,128)S(1)}, u32[]{:S(2)}, u32[]{:S(2)}) collective-permute-start(f32[32,768]{1,0:T(8,128)S(1)} %slice.140), channel_id=1, source_target_pairs={{0,8},{1,9},{2,10},{3,11},{4,12},{5,13},{6,14},{7,15},{8,0},{9,1},... | collective-permute-start | bytes 294920 | tf_op jit(solution)/shard_map/ppermute | solution.py:30
  87.0 4.8 %collective-permute-start.12 = (f32[32,768]{1,0:T(8,128)S(1)}, f32[32,768]{1,0:T(8,128)S(1)}, u32[]{:S(2)}, u32[]{:S(2)}) collective-permute-start(f32[32,768]{1,0:T(8,128)S(1)} %slice.147), channel_id=1, source_target_pairs={{0,6},{1,7},{2,4},{3,5},{4,2},{5,3},{6,0},{7,1},{8,14},{9,15},{10,... | collective-permute-start | bytes 294920 | tf_op jit(solution)/shard_map/ppermute | solution.py:30
  89.2 4.7 %collective-permute-start.16 = (f32[32,768]{1,0:T(8,128)S(1)}, f32[32,768]{1,0:T(8,128)S(1)}, u32[]{:S(2)}, u32[]{:S(2)}) collective-permute-start(f32[32,768]{1,0:T(8,128)S(1)} %slice.154), channel_id=1, source_target_pairs={{0,2},{1,3},{2,0},{3,1},{4,6},{5,7},{6,4},{7,5},{8,10},{9,11},{10,... | collective-permute-start | bytes 294920 | tf_op jit(solution)/shard_map/ppermute | solution.py:30
  94.1 5.8 %collective-permute-start.17 = (f32[32,1536]{1,0:T(8,128)S(1)}, f32[32,1536]{1,0:T(8,128)S(1)}, u32[]{:S(2)}, u32[]{:S(2)}) collective-permute-start(f32[32,1536]{1,0:T(8,128)S(1)} %constant_dynamic-slice_fusion.3), channel_id=1, source_target_pairs={{0,32},{1,33},{2,34},{3,35},{4,36},{5,37},{6,38},{7,39},{8,40},{9,... | collective-permute-start | bytes 589832 | tf_op jit(solution)/shard_map/ppermute | solution.py:30
  100.1 9.4 %collective-permute-start.20 = (f32[32,384]{1,0:T(8,128)S(1)}, f32[32,384]{1,0:T(8,128)S(1)}, u32[]{:S(2)}, u32[]{:S(2)}) collective-permute-start(f32[32,384]{1,0:T(8,128)S(1)} %get-tuple-element.38), channel_id=1, source_target_pairs={{0,192},{1,193},{2,194},{3,195},{4,196},{5,197},{6,198},{7,199},{8... | collective-permute-start | bytes 147464 | tf_op jit(solution)/shard_map/ppermute | solution.py:30
  107.1 5.4 %collective-permute-start.19 = (f32[32,384]{1,0:T(8,128)S(1)}, f32[32,384]{1,0:T(8,128)S(1)}, u32[]{:S(2)}, u32[]{:S(2)}) collective-permute-start(f32[32,384]{1,0:T(8,128)S(1)} %get-tuple-element.39), channel_id=1, source_target_pairs={{0,64},{1,65},{2,66},{3,67},{4,68},{5,69},{6,70},{7,71},{8,72},{9,... | collective-permute-start | bytes 147464 | tf_op jit(solution)/shard_map/ppermute | solution.py:30
  107.9 8.5 %collective-permute-start.18 = (f32[32,384]{1,0:T(8,128)S(1)}, f32[32,384]{1,0:T(8,128)S(1)}, u32[]{:S(2)}, u32[]{:S(2)}) collective-permute-start(f32[32,384]{1,0:T(8,128)S(1)} %get-tuple-element.37), channel_id=1, source_target_pairs={{0,128},{1,129},{2,130},{3,131},{4,132},{5,133},{6,134},{7,135},{8... | collective-permute-start | bytes 147464 | tf_op jit(solution)/shard_map/ppermute | solution.py:30

commit v4 on v0

v4 whole, which is shorter than its diff:
```python
import functools

import jax
import jax.numpy as jnp
from jax import lax
from jax.experimental import pallas as pl
from jax.experimental.pallas import tpu as pltpu
from jax.sharding import Mesh, PartitionSpec as P

AXES = ("z", "y", "x", "core")
NZ, NY, NX = 8, 4, 4
ROWS, DEPTH, WIDTH = 32, 512, 384
GROUPS = 4
NEAR_FIRST, FAR_FIRST = (2, 1, 3, 0), (2, 3, 1, 0)
SECOND = (1, 3, 2, 0)
CHEAP = pl.CostEstimate(flops=1 << 20, bytes_accessed=1 << 16, transcendentals=0)
VMEM = pl.BlockSpec(memory_space=pltpu.VMEM)


def flip(axis, mask):
    pairs = []
    for i in range(NZ * NY * NX * 2):
        at = {"z": i // 32, "y": i // 8 % 4, "x": i // 2 % 4, "core": i % 2}
        at[axis] ^= mask
        pairs.append((i, ((at["z"] * 4 + at["y"]) * 4 + at["x"]) * 2 + at["core"]))
    return pairs


def exchange(value, axis, mask):
    return lax.ppermute(value, AXES, flip(axis, mask))


def split(value):
    high = value.astype(jnp.bfloat16)
    return high, (value - high.astype(jnp.float32)).astype(jnp.bfloat16)


def relayout_kernel(a_ref, out_ref):
    for i in range(NY * NX):
        out_ref[i] = a_ref[:, pl.ds(i * 2 * DEPTH, 2 * DEPTH)]


def relayout(a):
    return pl.pallas_call(
        relayout_kernel,
        out_shape=jax.ShapeDtypeStruct((NY * NX, ROWS, 2 * DEPTH), jnp.float32),
        in_specs=[VMEM],
        out_specs=VMEM,
        compiler_params=pltpu.CompilerParams(vmem_limit_bytes=4 << 20),
        cost_estimate=CHEAP,
    )(a)


def after(value, *earlier):
    return lax.optimization_barrier((value, *earlier))[0]


def columns(group):
    return pl.ds(group * 2 * WIDTH, 2 * WIDTH)


def multiply(group, half, other, hi_ref, lo_ref, b):
    blocks = (NEAR_FIRST, FAR_FIRST)[group % 2]
    order = [(outer, inner) for outer in blocks[2 * half : 2 * half + 2] for inner in SECOND]
    order = [qy * 4 + qx if group < 2 else qx * 4 + qy for qx, qy in order]
    depth = pl.ds(other * DEPTH, DEPTH)
    a_hi, a_lo = (
        jnp.concatenate([ref[q * ROWS : (q + 1) * ROWS, depth] for q in order], 0)
        for ref in (hi_ref, lo_ref)
    )
    b_hi, b_lo = split(b)
    dot = functools.partial(jnp.dot, preferred_element_type=jnp.float32)
    return dot(a_hi, b_hi) + dot(a_lo, b_hi) + dot(a_hi, b_lo)


def whole(group, half, hi_ref, lo_ref, own_ref, oth_ref):
    total = multiply(group, half, 0, hi_ref, lo_ref, own_ref[:, columns(group)])
    return total + multiply(group, half, 1, hi_ref, lo_ref, oth_ref[:, columns(group)])


def sent_kernel(where, a_ref, own_ref, oth_ref, *refs):
    *outs, hi_ref, lo_ref = refs
    for q in range(NY * NX):
        source = (where[0] ^ (q // 4)) * 4 + (where[1] ^ (q % 4))
        rows = pl.ds(pl.multiple_of(source * ROWS, ROWS), ROWS)
        to = pl.ds(q * ROWS, ROWS)
        for other in range(2):
            depth = pl.ds(pl.multiple_of((where[2] ^ other) * DEPTH, DEPTH), DEPTH)
            high, low = split(a_ref[rows, depth])
            hi_ref[to, pl.ds(other * DEPTH, DEPTH)] = high
            lo_ref[to, pl.ds(other * DEPTH, DEPTH)] = low
    for group, out_ref in enumerate(outs):
        out_ref[...] = whole(group, 0, hi_ref, lo_ref, own_ref, oth_ref)


def kept_kernel(group, *refs):
    *refs, out_ref = refs
    out_ref[...] = whole(group, 1, *refs)


def call(kernel, out_shape, in_specs, limit):
    return pl.pallas_call(
        kernel,
        out_shape=out_shape,
        in_specs=in_specs,
        out_specs=jax.tree.map(lambda _: VMEM, out_shape),
        compiler_params=pltpu.CompilerParams(vmem_limit_bytes=limit << 20),
        cost_estimate=CHEAP,
    )


def products(where, a, own, oth):
    out = jax.ShapeDtypeStruct((8 * ROWS, 2 * WIDTH), jnp.float32)
    part = jax.ShapeDtypeStruct((NY * NX * ROWS, 2 * DEPTH), jnp.bfloat16)
    smem = pl.BlockSpec(memory_space=pltpu.SMEM)
    *sends, hi, lo = call(
        sent_kernel, (out,) * GROUPS + (part, part), [smem, VMEM, VMEM, VMEM], 6
    )(where, a, own, oth)
    keeps = [
        call(functools.partial(kept_kernel, group), out, [VMEM] * 4, 6)(hi, lo, own, oth)
        for group in range(GROUPS)
    ]
    return sends, keeps


def body(amplitudes, integrals):
    z, y, x, core = (lax.axis_index(name) for name in AXES)
    where = jnp.stack([y, x, core]).astype(jnp.int32)
    halves = [((z & 1) ^ v) * 4 * WIDTH for v in range(2)]
    blocks = [((z >> 1) ^ v) * WIDTH for v in range(4)]
    scalars = (where, halves, blocks)
    scalars, amplitudes, integrals = lax.optimization_barrier((scalars, amplitudes, integrals))
    where, halves, blocks = scalars
    oth = exchange(integrals, "core", 1)
    laid = relayout(amplitudes)
    mine = lax.all_to_all(laid, ("y", "x"), split_axis=0, concat_axis=0)
    mine = mine.reshape(NY * NX * ROWS, 2 * DEPTH)
    sends, parts = products(where, mine, integrals, oth)
    parts[0] = after(parts[0], *parts[1:])
    last = None
    for step in range(2):
        for group in range(GROUPS):
            keep = parts[group] if last is None else after(parts[group], last)
            mask = ((1, 3), (3, 1))[group % 2][step]
            last = keep + exchange(sends[group], "xxyy"[group], mask)
            if step == 0:
                sends[group], parts[group] = last[: 4 * ROWS], last[4 * ROWS :]
            else:
                parts[group] = last
    pairs = []
    for first, axis in ((0, "y"), (2, "x")):
        pair = [
            jnp.concatenate([part[i * ROWS : (i + 1) * ROWS] for part in parts[first : first + 2]], 1)
            for i in range(4)
        ]
        pairs.append(pair[3] + sum(exchange(pair[i], axis, SECOND[i]) for i in range(3)))
    cut = functools.partial(lax.dynamic_slice_in_dim, axis=1, allow_negative_indices=False)
    order = [(pair, i) for parity in range(2) for pair in pairs for i in (parity, parity + 2)]
    both = jnp.concatenate([pair[:, i * WIDTH : (i + 1) * WIDTH] for pair, i in order], 1)
    keep, send = (cut(both, start, 4 * WIDTH) for start in halves)
    keep = keep + exchange(send, "z", 1)
    block = lambda v: cut(keep, blocks[v], WIDTH)
    far = [exchange(block(v), "z", 2 * v) for v in (2, 1, 3)]
    return 0.5 * (block(0) + far[0] + far[1] + far[2])


def solution(mesh):
    chips = Mesh(mesh.devices.reshape(NZ, NY, NX, 2), AXES)
    return jax.shard_map(
        body,
        mesh=chips,
        in_specs=(P(("y", "x", "core"), "z"), P(AXES, None)),
        out_specs=P(("y", "x", "core"), "z"),
        check_vma=False,
    )
```

time: 226 us -> 110 us (0.49)
  waiting for transfers between devices: 151 us -> 31.3 us
  starting transfers between devices: 0.04 us -> 27.2 us
  matrix products: 22.7 us -> 0 us
  between operations: 13.4 us -> 0.33 us
  Pallas kernels: 0 us -> 11.9 us
    reduce_scatter x2 -> x0, waiting for transfers between devices: 151 us -> none  [the longest x1 112 us: body(): lax.psum_scatter(jnp.dot(received, integrals, precision=lax.Precision.HIG...]
    ppermute x0 -> x19, waiting for transfers between devices: none -> 31.3 us  [exchange(): return lax.ppermute(value, AXES, flip(axis, mask))]
    ppermute x0 -> x19, starting transfers between devices: none -> 27.2 us  [exchange(): return lax.ppermute(value, AXES, flip(axis, mask))]
    dot_general x1 -> x0, matrix products: 22.7 us -> none  [body(): jnp.dot(received, integrals, precision=lax.Precision.HIGHEST, preferred_e...]
    pallas_call x0 -> x6, Pallas kernels: none -> 11.9 us  [the longest x1 5.9 us: products(): call(sent_kernel, (out,) * GROUPS + (part, part), [smem, VMEM, VMEM, VMEM...]
  transfers between devices with their start and end apart: 2 -> 19, of which waited for: 2 -> 11; matrix products, arithmetic and copies ran while one was open for 0% -> 1% of each run, Pallas kernels for 0% -> 5%
where the time goes in v4:
time: 110 us
  blocking collectives  35.3 us (32%)
  waiting for transfers between devices  31.3 us (28%)
  starting transfers between devices  27.2 us (25%)
  Pallas kernels  11.9 us (11%)
  local copies, waits for them, and re-layouts  2.2 us (2%)
  other arithmetic  1.67 us (2%)
    all_to_all x1, blocking collectives, body(): mine = lax.all_to_all(laid, ('y', 'x'), split_axis=0, concat_axis=0)  35.3 us
    ppermute x19, waiting for transfers between devices, exchange(): return lax.ppermute(value, AXES, flip(axis, mask))  31.3 us
    ppermute x19, starting transfers between devices, exchange(): return lax.ppermute(value, AXES, flip(axis, mask))  27.2 us
    pallas_call x1, Pallas kernels, products(): call(sent_kernel, (out,) * GROUPS + (part, part), [smem, VMEM, VMEM, VMEM...  5.9 us
    pallas_call x4, Pallas kernels, products(): call(functools.partial(kept_kernel, group), out, [VMEM] * 4, 6)  5.86 us
  transfers between devices with their start and end apart: 19, of which 11 were waited for; matrix products, arithmetic and copies ran while one was open for 1% of the time, Pallas kernels for 5%

profile of v4, /device:TPU:2, one launch (start us, length us, event | category | flops | bytes accessed | tf_op | source)
XLA Modules:
  0.0 110.0 jit_solution(1575299262975179211)
XLA Ops:
  0.0 0.1 pad_add_fusion.where
  0.1 1.6 %copy-done.1 = f32[32,16384]{1,0:T(8,128)S(1)} copy-done((f32[32,16384]{1,0:T(8,128)S(1)}, f32[32,16384]{1,0:T(8,128)}, u32[]{:S(2)}) %copy-start.1) | copy-done | bytes 2097176
  1.7 0.1 shard_map.28
  1.9 35.3 %all_to_all.5 = f32[16,32,1024]{2,1,0:T(8,128)S(1)} all-to-all(f32[16,32,1024]{2,1,0:T(8,128)S(1)} %shard_map.28), channel_id=1, replica_groups=mesh['z'=8,'y'=4,'x'=4,'core'=2] {'y','x'}, dimensions={0} | all-to-all | bytes 4194304 | tf_op jit(solution)/shard_map/all_to_all | solution.py:136
  37.2 5.9 %shard_map.29 = (f32[256,768]{1,0:T(8,128)S(1)}, f32[256,768]{1,0:T(8,128)S(1)}, f32[256,768]{1,0:T(8,128)S(1)}, f32[256,768]{1,0:T(8,128)S(1)}, bf16[512,1024]{...) custom-call(s32[3]{0:T(128)S(1)} %pad_add_fusion.where, f32[512,1024]{1,0:T(8,128)S(1)} %bitcast.4, ...), custom_call_target="tpu_custom_call" | custom-call | flops 1048576 | bytes 65536 | tf_op jit(solution)/shard_map/pallas_call | solution.py:116
  43.1 1.5 %collective-permute-start.1 = (f32[256,768]{1,0:T(8,128)S(1)}, f32[256,768]{1,0:T(8,128)S(1)}, u32[]{:S(2)}, u32[]{:S(2)}) collective-permute-start(f32[256,768]{1,0:T(8,128)S(1)} %get-tuple-element.34), channel_id=1, source_target_pairs={{0,2},{1,3},{2,0},{3,1},{4,6},{5,7},{6,4},{7,5},{8,10},{9,11},{10,... | collective-permute-start | bytes 2359304 | tf_op jit(solution)/shard_map/ppermute | solution.py:30
  44.7 0.5 collective-permute-start.3
  45.2 1.4 %collective-permute-start.4 = (f32[256,768]{1,0:T(8,128)S(1)}, f32[256,768]{1,0:T(8,128)S(1)}, u32[]{:S(2)}, u32[]{:S(2)}) collective-permute-start(f32[256,768]{1,0:T(8,128)S(1)} %get-tuple-element.40), channel_id=1, source_target_pairs={{0,24},{1,25},{2,26},{3,27},{4,28},{5,29},{6,30},{7,31},{8,16},{9,... | collective-permute-start | bytes 2359304 | tf_op jit(solution)/shard_map/ppermute | solution.py:30
  46.6 1.5 %shard_map.33 = f32[256,768]{1,0:T(8,128)S(1)} custom-call(bf16[512,1024]{1,0:T(8,128)(2,1)S(1)} %get-tuple-element.31.refs_0_, bf16[512,1024]{1,0:T(8,128)(2,1)S(1)} %get-tuple-element.32.refs_1_, f32[512,3072]{1,0:T(8,128)S(1)} %copy-done, f32[512,3072]{1,0:T(8,128)S(1)} %collective-permute-done.oth_ref.refs_3_), custom_call_target="tpu_custom_call" | custom-call | flops 1048576 | bytes 65536 | tf_op jit(solution)/shard_map/pallas_call | solution.py:120
  48.1 1.5 %shard_map.32 = f32[256,768]{1,0:T(8,128)S(1)} custom-call(bf16[512,1024]{1,0:T(8,128)(2,1)S(1)} %get-tuple-element.31.refs_0_, bf16[512,1024]{1,0:T(8,128)(2,1)S(1)} %get-tuple-element.32.refs_1_, f32[512,3072]{1,0:T(8,128)S(1)} %copy-done, f32[512,3072]{1,0:T(8,128)S(1)} %collective-permute-done.oth_ref.refs_3_), custom_call_target="tpu_custom_call" | custom-call | flops 1048576 | bytes 65536 | tf_op jit(solution)/shard_map/pallas_call | solution.py:120
  49.6 1.5 %shard_map.31 = f32[256,768]{1,0:T(8,128)S(1)} custom-call(bf16[512,1024]{1,0:T(8,128)(2,1)S(1)} %get-tuple-element.31.refs_0_, bf16[512,1024]{1,0:T(8,128)(2,1)S(1)} %get-tuple-element.32.refs_1_, f32[512,3072]{1,0:T(8,128)S(1)} %copy-done, f32[512,3072]{1,0:T(8,128)S(1)} %collective-permute-done.oth_ref.refs_3_), custom_call_target="tpu_custom_call" | custom-call | flops 1048576 | bytes 65536 | tf_op jit(solution)/shard_map/pallas_call | solution.py:120
  51.1 1.5 %shard_map.30 = f32[256,768]{1,0:T(8,128)S(1)} custom-call(bf16[512,1024]{1,0:T(8,128)(2,1)S(1)} %get-tuple-element.31.refs_0_, bf16[512,1024]{1,0:T(8,128)(2,1)S(1)} %get-tuple-element.32.refs_1_, f32[512,3072]{1,0:T(8,128)S(1)} %copy-done, f32[512,3072]{1,0:T(8,128)S(1)} %collective-permute-done.oth_ref.refs_3_), custom_call_target="tpu_custom_call" | custom-call | flops 1048576 | bytes 65536 | tf_op jit(solution)/shard_map/pallas_call | solution.py:120
  52.5 9.2 %collective-permute-done.1 = f32[256,768]{1,0:T(8,128)S(1)} collective-permute-done((f32[256,768]{1,0:T(8,128)S(1)}, f32[256,768]{1,0:T(8,128)S(1)}, u32[]{:S(2)}, u32[]{:S(2)}) %collective-permute-start.1) | collective-permute-done | bytes 786464 | tf_op jit(solution)/shard_map/ppermute | solution.py:30
  61.7 0.1 add.54
  61.8 0.1 fusion.3
  61.9 1.1 %collective-permute-start.5 = (f32[128,768]{1,0:T(8,128)S(1)}, f32[128,768]{1,0:T(8,128)S(1)}, u32[]{:S(2)}, u32[]{:S(2)}) collective-permute-start(f32[128,768]{1,0:T(8,128)S(1)} %get-tuple-element.57), channel_id=1, source_target_pairs={{0,6},{1,7},{2,4},{3,5},{4,2},{5,3},{6,0},{7,1},{8,14},{9,15},{10,... | collective-permute-start | bytes 1179656 | tf_op jit(solution)/shard_map/ppermute | solution.py:30
  63.0 0.1 add.55
  63.1 0.1 fusion.2
  63.2 1.8 %collective-permute-start.6 = (f32[128,768]{1,0:T(8,128)S(1)}, f32[128,768]{1,0:T(8,128)S(1)}, u32[]{:S(2)}, u32[]{:S(2)}) collective-permute-start(f32[128,768]{1,0:T(8,128)S(1)} %get-tuple-element.55), channel_id=1, source_target_pairs={{0,2},{1,3},{2,0},{3,1},{4,6},{5,7},{6,4},{7,5},{8,10},{9,11},{10,... | collective-permute-start | bytes 1179656 | tf_op jit(solution)/shard_map/ppermute | solution.py:30
  65.0 0.1 add.56
  65.1 0.1 fusion.1
  65.1 0.9 collective-permute-start.10
  66.1 0.1 add.57
  66.2 0.1 fusion
  66.2 0.1 collective-permute-start.11
  66.3 5.1 %collective-permute-done.5 = f32[128,768]{1,0:T(8,128)S(1)} collective-permute-done((f32[128,768]{1,0:T(8,128)S(1)}, f32[128,768]{1,0:T(8,128)S(1)}, u32[]{:S(2)}, u32[]{:S(2)}) %collective-permute-start.5) | collective-permute-done | bytes 393248 | tf_op jit(solution)/shard_map/ppermute | solution.py:30
  71.6 1.6 %collective-permute-done.6 = f32[128,768]{1,0:T(8,128)S(1)} collective-permute-done((f32[128,768]{1,0:T(8,128)S(1)}, f32[128,768]{1,0:T(8,128)S(1)}, u32[]{:S(2)}, u32[]{:S(2)}) %collective-permute-start.6) | collective-permute-done | bytes 393248 | tf_op jit(solution)/shard_map/ppermute | solution.py:30
  73.3 0.1 collective-permute-start.7
  73.4 1.9 %collective-permute-start.9 = (f32[32,1536]{1,0:T(8,128)S(1)}, f32[32,1536]{1,0:T(8,128)S(1)}, u32[]{:S(2)}, u32[]{:S(2)}) collective-permute-start(f32[32,1536]{1,0:T(8,128)S(1)} %pad_maximum_fusion.2), channel_id=1, source_target_pairs={{0,16},{1,17},{2,18},{3,19},{4,20},{5,21},{6,22},{7,23},{8,24},{9,... | collective-permute-start | bytes 589832 | tf_op jit(solution)/shard_map/ppermute | solution.py:30
  75.4 2.9 %collective-permute-start.8 = (f32[32,1536]{1,0:T(8,128)S(1)}, f32[32,1536]{1,0:T(8,128)S(1)}, u32[]{:S(2)}, u32[]{:S(2)}) collective-permute-start(f32[32,1536]{1,0:T(8,128)S(1)} %pad_maximum_fusion.1), channel_id=1, source_target_pairs={{0,24},{1,25},{2,26},{3,27},{4,28},{5,29},{6,30},{7,31},{8,16},{9,... | collective-permute-start | bytes 589832 | tf_op jit(solution)/shard_map/ppermute | solution.py:30
  78.5 0.8 collective-permute-start.12
  79.4 1.7 %collective-permute-start.14 = (f32[32,1536]{1,0:T(8,128)S(1)}, f32[32,1536]{1,0:T(8,128)S(1)}, u32[]{:S(2)}, u32[]{:S(2)}) collective-permute-start(f32[32,1536]{1,0:T(8,128)S(1)} %pad_maximum_fusion.5), channel_id=1, source_target_pairs={{0,4},{1,5},{2,6},{3,7},{4,0},{5,1},{6,2},{7,3},{8,12},{9,13},{10,... | collective-permute-start | bytes 589832 | tf_op jit(solution)/shard_map/ppermute | solution.py:30
  81.1 0.1 collective-permute-done.7
  81.2 1.1 collective-permute-start.13
  82.3 2.7 %collective-permute-done.9 = f32[32,1536]{1,0:T(8,128)S(1)} collective-permute-done((f32[32,1536]{1,0:T(8,128)S(1)}, f32[32,1536]{1,0:T(8,128)S(1)}, u32[]{:S(2)}, u32[]{:S(2)}) %collective-permute-start.9) | collective-permute-done | bytes 196640 | tf_op jit(solution)/shard_map/ppermute | solution.py:30
  85.0 0.2 collective-permute-done.8
  85.3 1.8 %collective-permute-done.14 = f32[32,1536]{1,0:T(8,128)S(1)} collective-permute-done((f32[32,1536]{1,0:T(8,128)S(1)}, f32[32,1536]{1,0:T(8,128)S(1)}, u32[]{:S(2)}, u32[]{:S(2)}) %collective-permute-start.14) | collective-permute-done | bytes 196640 | tf_op jit(solution)/shard_map/ppermute | solution.py:30
  87.1 1.9 %collective-permute-done.13 = f32[32,1536]{1,0:T(8,128)S(1)} collective-permute-done((f32[32,1536]{1,0:T(8,128)S(1)}, f32[32,1536]{1,0:T(8,128)S(1)}, u32[]{:S(2)}, u32[]{:S(2)}) %collective-permute-start.13) | collective-permute-done | bytes 196640 | tf_op jit(solution)/shard_map/ppermute | solution.py:30
  89.1 0.1 constant_dynamic-slice_fusion.3
  89.3 2.0 %collective-permute-start.15 = (f32[32,1536]{1,0:T(8,128)S(1)}, f32[32,1536]{1,0:T(8,128)S(1)}, u32[]{:S(2)}, u32[]{:S(2)}) collective-permute-start(f32[32,1536]{1,0:T(8,128)S(1)} %constant_dynamic-slice_fusion.3), channel_id=1, source_target_pairs={{0,32},{1,33},{2,34},{3,35},{4,36},{5,37},{6,38},{7,39},{8,40},{9,... | collective-permute-start | bytes 589832 | tf_op jit(solution)/shard_map/ppermute | solution.py:30
  91.3 3.7 %collective-permute-done.15 = f32[32,1536]{1,0:T(8,128)S(1)} collective-permute-done((f32[32,1536]{1,0:T(8,128)S(1)}, f32[32,1536]{1,0:T(8,128)S(1)}, u32[]{:S(2)}, u32[]{:S(2)}) %collective-permute-start.15) | collective-permute-done | bytes 196640 | tf_op jit(solution)/shard_map/ppermute | solution.py:30
  95.0 0.1 dynamic-slice_add_fusion
  95.1 0.1 constant_dynamic-slice_fusion.2
  95.3 7.8 %collective-permute-start.16 = (f32[32,384]{1,0:T(8,128)S(1)}, f32[32,384]{1,0:T(8,128)S(1)}, u32[]{:S(2)}, u32[]{:S(2)}) collective-permute-start(f32[32,384]{1,0:T(8,128)S(1)} %get-tuple-element.75), channel_id=1, source_target_pairs={{0,128},{1,129},{2,130},{3,131},{4,132},{5,133},{6,134},{7,135},{8... | collective-permute-start | bytes 147464 | tf_op jit(solution)/shard_map/ppermute | solution.py:30
  103.1 1.4 %collective-permute-start.17 = (f32[32,384]{1,0:T(8,128)S(1)}, f32[32,384]{1,0:T(8,128)S(1)}, u32[]{:S(2)}, u32[]{:S(2)}) collective-permute-start(f32[32,384]{1,0:T(8,128)S(1)} %get-tuple-element.77), channel_id=1, source_target_pairs={{0,64},{1,65},{2,66},{3,67},{4,68},{5,69},{6,70},{7,71},{8,72},{9,... | collective-permute-start | bytes 147464 | tf_op jit(solution)/shard_map/ppermute | solution.py:30
  104.4 0.7 collective-permute-done.16
  105.1 4.1 %collective-permute-done.18 = f32[32,384]{1,0:T(8,128)S(1)} collective-permute-done((f32[32,384]{1,0:T(8,128)S(1)}, f32[32,384]{1,0:T(8,128)S(1)}, u32[]{:S(2)}, u32[]{:S(2)}) %collective-permute-start.18) | collective-permute-done | bytes 49184 | tf_op jit(solution)/shard_map/ppermute | solution.py:30
  109.3 0.7 add_multiply_fusion
  (38 shorter events, 0.6 us)
Async XLA Ops:
  0.1 37.1 %collective-permute-start = (f32[512,3072]{1,0:T(8,128)}, f32[512,3072]{1,0:T(8,128)S(1)}, u32[]{:S(2)}, u32[]{:S(2)}) collective-permute-start(f32[512,3072]{1,0:T(8,128)} %refs_2_.3), channel_id=1, source_target_pairs={{0,1},{1,0},{2,3},{3,2},{4,5},{5,4},{6,7},{7,6},{8,9},{9,8},{10,11... | collective-permute-start | bytes 18874376 | tf_op jit(solution)/shard_map/ppermute | solution.py:30
  0.1 1.6 %copy-start.1 = (f32[32,16384]{1,0:T(8,128)S(1)}, f32[32,16384]{1,0:T(8,128)}, u32[]{:S(2)}) copy-start(f32[32,16384]{1,0:T(8,128)} %a_ref) | copy-start | bytes 6291460
  1.7 35.5 %copy-start = (f32[512,3072]{1,0:T(8,128)S(1)}, f32[512,3072]{1,0:T(8,128)}, u32[]{:S(2)}) copy-start(f32[512,3072]{1,0:T(8,128)} %refs_2_.3) | copy-start | bytes 18874372
  43.1 18.6 %collective-permute-start.1 = (f32[256,768]{1,0:T(8,128)S(1)}, f32[256,768]{1,0:T(8,128)S(1)}, u32[]{:S(2)}, u32[]{:S(2)}) collective-permute-start(f32[256,768]{1,0:T(8,128)S(1)} %get-tuple-element.34), channel_id=1, source_target_pairs={{0,2},{1,3},{2,0},{3,1},{4,6},{5,7},{6,4},{7,5},{8,10},{9,11},{10,... | collective-permute-start | bytes 2359304 | tf_op jit(solution)/shard_map/ppermute | solution.py:30
  44.7 18.4 %collective-permute-start.2 = (f32[256,768]{1,0:T(8,128)S(1)}, f32[256,768]{1,0:T(8,128)S(1)}, u32[]{:S(2)}, u32[]{:S(2)}) collective-permute-start(f32[256,768]{1,0:T(8,128)S(1)} %get-tuple-element.36), channel_id=1, source_target_pairs={{0,6},{1,7},{2,4},{3,5},{4,2},{5,3},{6,0},{7,1},{8,14},{9,15},{10,... | collective-permute-start | bytes 2359304 | tf_op jit(solution)/shard_map/ppermute | solution.py:30
  44.7 20.3 %collective-permute-start.3 = (f32[256,768]{1,0:T(8,128)S(1)}, f32[256,768]{1,0:T(8,128)S(1)}, u32[]{:S(2)}, u32[]{:S(2)}) collective-permute-start(f32[256,768]{1,0:T(8,128)S(1)} %get-tuple-element.38), channel_id=1, source_target_pairs={{0,8},{1,9},{2,10},{3,11},{4,12},{5,13},{6,14},{7,15},{8,0},{9,1},... | collective-permute-start | bytes 2359304 | tf_op jit(solution)/shard_map/ppermute | solution.py:30
  45.2 20.9 %collective-permute-start.4 = (f32[256,768]{1,0:T(8,128)S(1)}, f32[256,768]{1,0:T(8,128)S(1)}, u32[]{:S(2)}, u32[]{:S(2)}) collective-permute-start(f32[256,768]{1,0:T(8,128)S(1)} %get-tuple-element.40), channel_id=1, source_target_pairs={{0,24},{1,25},{2,26},{3,27},{4,28},{5,29},{6,30},{7,31},{8,16},{9,... | collective-permute-start | bytes 2359304 | tf_op jit(solution)/shard_map/ppermute | solution.py:30
  61.9 9.6 %collective-permute-start.5 = (f32[128,768]{1,0:T(8,128)S(1)}, f32[128,768]{1,0:T(8,128)S(1)}, u32[]{:S(2)}, u32[]{:S(2)}) collective-permute-start(f32[128,768]{1,0:T(8,128)S(1)} %get-tuple-element.57), channel_id=1, source_target_pairs={{0,6},{1,7},{2,4},{3,5},{4,2},{5,3},{6,0},{7,1},{8,14},{9,15},{10,... | collective-permute-start | bytes 1179656 | tf_op jit(solution)/shard_map/ppermute | solution.py:30
  63.2 10.0 %collective-permute-start.6 = (f32[128,768]{1,0:T(8,128)S(1)}, f32[128,768]{1,0:T(8,128)S(1)}, u32[]{:S(2)}, u32[]{:S(2)}) collective-permute-start(f32[128,768]{1,0:T(8,128)S(1)} %get-tuple-element.55), channel_id=1, source_target_pairs={{0,2},{1,3},{2,0},{3,1},{4,6},{5,7},{6,4},{7,5},{8,10},{9,11},{10,... | collective-permute-start | bytes 1179656 | tf_op jit(solution)/shard_map/ppermute | solution.py:30
  65.1 13.2 %collective-permute-start.10 = (f32[128,768]{1,0:T(8,128)S(1)}, f32[128,768]{1,0:T(8,128)S(1)}, u32[]{:S(2)}, u32[]{:S(2)}) collective-permute-start(f32[128,768]{1,0:T(8,128)S(1)} %get-tuple-element.53), channel_id=1, source_target_pairs={{0,24},{1,25},{2,26},{3,27},{4,28},{5,29},{6,30},{7,31},{8,16},{9,... | collective-permute-start | bytes 1179656 | tf_op jit(solution)/shard_map/ppermute | solution.py:30
  66.2 12.2 %collective-permute-start.11 = (f32[128,768]{1,0:T(8,128)S(1)}, f32[128,768]{1,0:T(8,128)S(1)}, u32[]{:S(2)}, u32[]{:S(2)}) collective-permute-start(f32[128,768]{1,0:T(8,128)S(1)} %get-tuple-element.51), channel_id=1, source_target_pairs={{0,8},{1,9},{2,10},{3,11},{4,12},{5,13},{6,14},{7,15},{8,0},{9,1},... | collective-permute-start | bytes 1179656 | tf_op jit(solution)/shard_map/ppermute | solution.py:30
  73.3 7.9 %collective-permute-start.7 = (f32[32,1536]{1,0:T(8,128)S(1)}, f32[32,1536]{1,0:T(8,128)S(1)}, u32[]{:S(2)}, u32[]{:S(2)}) collective-permute-start(f32[32,1536]{1,0:T(8,128)S(1)} %pad_maximum_fusion), channel_id=1, source_target_pairs={{0,8},{1,9},{2,10},{3,11},{4,12},{5,13},{6,14},{7,15},{8,0},{9,1},... | collective-permute-start | bytes 589832 | tf_op jit(solution)/shard_map/ppermute | solution.py:30
  73.4 11.6 %collective-permute-start.9 = (f32[32,1536]{1,0:T(8,128)S(1)}, f32[32,1536]{1,0:T(8,128)S(1)}, u32[]{:S(2)}, u32[]{:S(2)}) collective-permute-start(f32[32,1536]{1,0:T(8,128)S(1)} %pad_maximum_fusion.2), channel_id=1, source_target_pairs={{0,16},{1,17},{2,18},{3,19},{4,20},{5,21},{6,22},{7,23},{8,24},{9,... | collective-permute-start | bytes 589832 | tf_op jit(solution)/shard_map/ppermute | solution.py:30
  75.4 9.9 %collective-permute-start.8 = (f32[32,1536]{1,0:T(8,128)S(1)}, f32[32,1536]{1,0:T(8,128)S(1)}, u32[]{:S(2)}, u32[]{:S(2)}) collective-permute-start(f32[32,1536]{1,0:T(8,128)S(1)} %pad_maximum_fusion.1), channel_id=1, source_target_pairs={{0,24},{1,25},{2,26},{3,27},{4,28},{5,29},{6,30},{7,31},{8,16},{9,... | collective-permute-start | bytes 589832 | tf_op jit(solution)/shard_map/ppermute | solution.py:30
  78.5 6.8 %collective-permute-start.12 = (f32[32,1536]{1,0:T(8,128)S(1)}, f32[32,1536]{1,0:T(8,128)S(1)}, u32[]{:S(2)}, u32[]{:S(2)}) collective-permute-start(f32[32,1536]{1,0:T(8,128)S(1)} %pad_maximum_fusion.3), channel_id=1, source_target_pairs={{0,2},{1,3},{2,0},{3,1},{4,6},{5,7},{6,4},{7,5},{8,10},{9,11},{10,... | collective-permute-start | bytes 589832 | tf_op jit(solution)/shard_map/ppermute | solution.py:30
  79.4 7.8 %collective-permute-start.14 = (f32[32,1536]{1,0:T(8,128)S(1)}, f32[32,1536]{1,0:T(8,128)S(1)}, u32[]{:S(2)}, u32[]{:S(2)}) collective-permute-start(f32[32,1536]{1,0:T(8,128)S(1)} %pad_maximum_fusion.5), channel_id=1, source_target_pairs={{0,4},{1,5},{2,6},{3,7},{4,0},{5,1},{6,2},{7,3},{8,12},{9,13},{10,... | collective-permute-start | bytes 589832 | tf_op jit(solution)/shard_map/ppermute | solution.py:30
  81.2 7.8 %collective-permute-start.13 = (f32[32,1536]{1,0:T(8,128)S(1)}, f32[32,1536]{1,0:T(8,128)S(1)}, u32[]{:S(2)}, u32[]{:S(2)}) collective-permute-start(f32[32,1536]{1,0:T(8,128)S(1)} %pad_maximum_fusion.4), channel_id=1, source_target_pairs={{0,6},{1,7},{2,4},{3,5},{4,2},{5,3},{6,0},{7,1},{8,14},{9,15},{10,... | collective-permute-start | bytes 589832 | tf_op jit(solution)/shard_map/ppermute | solution.py:30
  89.3 5.8 %collective-permute-start.15 = (f32[32,1536]{1,0:T(8,128)S(1)}, f32[32,1536]{1,0:T(8,128)S(1)}, u32[]{:S(2)}, u32[]{:S(2)}) collective-permute-start(f32[32,1536]{1,0:T(8,128)S(1)} %constant_dynamic-slice_fusion.3), channel_id=1, source_target_pairs={{0,32},{1,33},{2,34},{3,35},{4,36},{5,37},{6,38},{7,39},{8,40},{9,... | collective-permute-start | bytes 589832 | tf_op jit(solution)/shard_map/ppermute | solution.py:30
  95.3 9.9 %collective-permute-start.16 = (f32[32,384]{1,0:T(8,128)S(1)}, f32[32,384]{1,0:T(8,128)S(1)}, u32[]{:S(2)}, u32[]{:S(2)}) collective-permute-start(f32[32,384]{1,0:T(8,128)S(1)} %get-tuple-element.75), channel_id=1, source_target_pairs={{0,128},{1,129},{2,130},{3,131},{4,132},{5,133},{6,134},{7,135},{8... | collective-permute-start | bytes 147464 | tf_op jit(solution)/shard_map/ppermute | solution.py:30
  103.1 6.2 %collective-permute-start.18 = (f32[32,384]{1,0:T(8,128)S(1)}, f32[32,384]{1,0:T(8,128)S(1)}, u32[]{:S(2)}, u32[]{:S(2)}) collective-permute-start(f32[32,384]{1,0:T(8,128)S(1)} %get-tuple-element.76), channel_id=1, source_target_pairs={{0,192},{1,193},{2,194},{3,195},{4,196},{5,197},{6,198},{7,199},{8... | collective-permute-start | bytes 147464 | tf_op jit(solution)/shard_map/ppermute | solution.py:30
  103.1 6.2 %collective-permute-start.17 = (f32[32,384]{1,0:T(8,128)S(1)}, f32[32,384]{1,0:T(8,128)S(1)}, u32[]{:S(2)}, u32[]{:S(2)}) collective-permute-start(f32[32,384]{1,0:T(8,128)S(1)} %get-tuple-element.77), channel_id=1, source_target_pairs={{0,64},{1,65},{2,66},{3,67},{4,68},{5,69},{6,70},{7,71},{8,72},{9,... | collective-permute-start | bytes 147464 | tf_op jit(solution)/shard_map/ppermute | solution.py:30

commit v5 on v4

--- a/solution.py
+++ b/solution.py
@@ -78,7 +78,7 @@
     return total + multiply(group, half, 1, hi_ref, lo_ref, oth_ref[:, columns(group)])
 
 
-def sent_kernel(where, a_ref, own_ref, oth_ref, *refs):
+def first_kernel(where, a_ref, own_ref, oth_ref, *refs):
     *outs, hi_ref, lo_ref = refs
     for q in range(NY * NX):
         source = (where[0] ^ (q // 4)) * 4 + (where[1] ^ (q % 4))
@@ -93,9 +93,9 @@
         out_ref[...] = whole(group, 0, hi_ref, lo_ref, own_ref, oth_ref)
 
 
-def kept_kernel(group, *refs):
-    *refs, out_ref = refs
-    out_ref[...] = whole(group, 1, *refs)
+def product_kernel(groups, half, *refs):
+    for group, out_ref in zip(groups, refs[4:]):
+        out_ref[...] = whole(group, half, *refs[:4])
 
 
 def call(kernel, out_shape, in_specs, limit):
@@ -114,12 +114,15 @@
     part = jax.ShapeDtypeStruct((NY * NX * ROWS, 2 * DEPTH), jnp.bfloat16)
     smem = pl.BlockSpec(memory_space=pltpu.SMEM)
     *sends, hi, lo = call(
-        sent_kernel, (out,) * GROUPS + (part, part), [smem, VMEM, VMEM, VMEM], 6
+        first_kernel, (out,) * 2 + (part, part), [smem, VMEM, VMEM, VMEM], 6
     )(where, a, own, oth)
-    keeps = [
-        call(functools.partial(kept_kernel, group), out, [VMEM] * 4, 6)(hi, lo, own, oth)
-        for group in range(GROUPS)
-    ]
+    later = functools.partial(product_kernel, (2, 3), 0)
+    sends += call(later, (out,) * 2, [VMEM] * 4, 6)(hi, lo, own, oth)
+    hi = after(hi, sends[-1])
+    keeps = []
+    for group in range(GROUPS):
+        kernel = functools.partial(product_kernel, (group,), 1)
+        keeps += call(kernel, (out,), [VMEM] * 4, 6)(hi, lo, own, oth)
     return sends, keeps
 
 

time: 110 us -> 110 us (level)
  waiting for transfers between devices: 31.3 us -> 28.5 us
  starting transfers between devices: 27.2 us -> 28.9 us
    ppermute x19, waiting for transfers between devices: 31.3 us -> 28.5 us  [exchange(): return lax.ppermute(value, AXES, flip(axis, mask))]
    ppermute x19, starting transfers between devices: 27.2 us -> 28.9 us  [exchange(): return lax.ppermute(value, AXES, flip(axis, mask))]
    pallas_call x5 -> x6, Pallas kernels: 11.8 us -> 12 us  [the longest x4 5.86 us: products(): keeps += call(kernel, (out,), [VMEM] * 4, 6)(hi, lo, own, oth)]
  transfers between devices with their start and end apart: 19 -> 19, of which waited for: 11 -> 9; matrix products, arithmetic and copies ran while one was open for 1% -> 1% of each run, Pallas kernels for 5% -> 8%
where the time goes in v5:
time: 110 us; the launch traced here: 109 us
  blocking collectives  35.3 us (32%)
  starting transfers between devices  28.9 us (26%)
  waiting for transfers between devices  28.5 us (26%)
  Pallas kernels  12.1 us (11%)
  local copies, waits for them, and re-layouts  2.2 us (2%)
  other arithmetic  1.69 us (2%)
    all_to_all x1, blocking collectives, body(): mine = lax.all_to_all(laid, ('y', 'x'), split_axis=0, concat_axis=0)  35.3 us
    ppermute x19, starting transfers between devices, exchange(): return lax.ppermute(value, AXES, flip(axis, mask))  28.9 us
    ppermute x19, waiting for transfers between devices, exchange(): return lax.ppermute(value, AXES, flip(axis, mask))  28.5 us
    pallas_call x4, Pallas kernels, products(): keeps += call(kernel, (out,), [VMEM] * 4, 6)(hi, lo, own, oth)  5.86 us
    pallas_call x1, Pallas kernels, products(): call(first_kernel, (out,) * 2 + (part, part), [smem, VMEM, VMEM, VMEM], 6)  3.39 us
    pallas_call x1, Pallas kernels, products(): sends += call(later, (out,) * 2, [VMEM] * 4, 6)(hi, lo, own, oth)  2.73 us
  transfers between devices with their start and end apart: 19, of which 9 were waited for; matrix products, arithmetic and copies ran while one was open for 1% of the time, Pallas kernels for 8%

profile of v5, /device:TPU:2, one launch (start us, length us, event | category | flops | bytes accessed | tf_op | source)
XLA Modules:
  0.0 109.2 jit_solution(17760565124581048613)
XLA Ops:
  0.0 0.1 pad_add_fusion.where
  0.1 1.6 %copy-done.1 = f32[32,16384]{1,0:T(8,128)S(1)} copy-done((f32[32,16384]{1,0:T(8,128)S(1)}, f32[32,16384]{1,0:T(8,128)}, u32[]{:S(2)}) %copy-start.1) | copy-done | bytes 2097176
  1.7 0.1 shard_map.28
  1.9 35.3 %all_to_all.5 = f32[16,32,1024]{2,1,0:T(8,128)S(1)} all-to-all(f32[16,32,1024]{2,1,0:T(8,128)S(1)} %shard_map.28), channel_id=1, replica_groups=mesh['z'=8,'y'=4,'x'=4,'core'=2] {'y','x'}, dimensions={0} | all-to-all | bytes 4194304 | tf_op jit(solution)/shard_map/all_to_all | solution.py:139
  37.2 3.4 %shard_map.29 = (f32[256,768]{1,0:T(8,128)S(1)}, f32[256,768]{1,0:T(8,128)S(1)}, bf16[512,1024]{1,0:T(8,128)(2,1)S(1)}, bf16[512,1024]{1,0:T(8,128)(2,1)S(1)}) custom-call(s32[3]{0:T(128)S(1)} %pad_add_fusion.where, f32[512,1024]{1,0:T(8,128)S(1)} %bitcast.4, f32[512,3072]{1,0:T(8,128)S(1)} %copy-done, f32[512,3072]{1,0:T(8,128)S(1)} %collective-permute-done.oth_ref.refs_3_), custom_call_target="tpu_custom_call" | custom-call | flops 1048576 | bytes 65536 | tf_op jit(solution)/shard_map/pallas_call | solution.py:116
  40.6 1.5 %collective-permute-start.1 = (f32[256,768]{1,0:T(8,128)S(1)}, f32[256,768]{1,0:T(8,128)S(1)}, u32[]{:S(2)}, u32[]{:S(2)}) collective-permute-start(f32[256,768]{1,0:T(8,128)S(1)} %get-tuple-element.37), channel_id=1, source_target_pairs={{0,2},{1,3},{2,0},{3,1},{4,6},{5,7},{6,4},{7,5},{8,10},{9,11},{10,... | collective-permute-start | bytes 2359304 | tf_op jit(solution)/shard_map/ppermute | solution.py:30
  42.2 2.7 %shard_map.30 = (f32[256,768]{1,0:T(8,128)S(1)}, f32[256,768]{1,0:T(8,128)S(1)}) custom-call(bf16[512,1024]{1,0:T(8,128)(2,1)S(1)} %get-tuple-element.35.refs_0_, bf16[512,1024]{1,0:T(8,128)(2,1)S(1)} %get-tuple-element.33.refs_1_, f32[512,3072]{1,0:T(8,128)S(1)} %copy-done, f32[512,3072]{1,0:T(8,128)S(1)} %collective-permute-done.oth_ref.refs_3_), custom_call_target="tpu_custom_call" | custom-call | flops 1048576 | bytes 65536 | tf_op jit(solution)/shard_map/pallas_call | solution.py:120
  44.9 0.6 collective-permute-start.3
  45.5 1.4 %collective-permute-start.4 = (f32[256,768]{1,0:T(8,128)S(1)}, f32[256,768]{1,0:T(8,128)S(1)}, u32[]{:S(2)}, u32[]{:S(2)}) collective-permute-start(f32[256,768]{1,0:T(8,128)S(1)} %get-tuple-element.34), channel_id=1, source_target_pairs={{0,24},{1,25},{2,26},{3,27},{4,28},{5,29},{6,30},{7,31},{8,16},{9,... | collective-permute-start | bytes 2359304 | tf_op jit(solution)/shard_map/ppermute | solution.py:30
  47.0 1.5 %shard_map.34 = f32[256,768]{1,0:T(8,128)S(1)} custom-call(bf16[512,1024]{1,0:T(8,128)(2,1)S(1)} %get-tuple-element.35.refs_0_, bf16[512,1024]{1,0:T(8,128)(2,1)S(1)} %get-tuple-element.33.refs_1_, f32[512,3072]{1,0:T(8,128)S(1)} %copy-done, f32[512,3072]{1,0:T(8,128)S(1)} %collective-permute-done.oth_ref.refs_3_), custom_call_target="tpu_custom_call" | custom-call | flops 1048576 | bytes 65536 | tf_op jit(solution)/shard_map/pallas_call | solution.py:125
  48.4 1.5 %shard_map.33 = f32[256,768]{1,0:T(8,128)S(1)} custom-call(bf16[512,1024]{1,0:T(8,128)(2,1)S(1)} %get-tuple-element.35.refs_0_, bf16[512,1024]{1,0:T(8,128)(2,1)S(1)} %get-tuple-element.33.refs_1_, f32[512,3072]{1,0:T(8,128)S(1)} %copy-done, f32[512,3072]{1,0:T(8,128)S(1)} %collective-permute-done.oth_ref.refs_3_), custom_call_target="tpu_custom_call" | custom-call | flops 1048576 | bytes 65536 | tf_op jit(solution)/shard_map/pallas_call | solution.py:125
  49.9 1.5 %shard_map.32 = f32[256,768]{1,0:T(8,128)S(1)} custom-call(bf16[512,1024]{1,0:T(8,128)(2,1)S(1)} %get-tuple-element.35.refs_0_, bf16[512,1024]{1,0:T(8,128)(2,1)S(1)} %get-tuple-element.33.refs_1_, f32[512,3072]{1,0:T(8,128)S(1)} %copy-done, f32[512,3072]{1,0:T(8,128)S(1)} %collective-permute-done.oth_ref.refs_3_), custom_call_target="tpu_custom_call" | custom-call | flops 1048576 | bytes 65536 | tf_op jit(solution)/shard_map/pallas_call | solution.py:125
  51.4 1.5 %shard_map.31 = f32[256,768]{1,0:T(8,128)S(1)} custom-call(bf16[512,1024]{1,0:T(8,128)(2,1)S(1)} %get-tuple-element.35.refs_0_, bf16[512,1024]{1,0:T(8,128)(2,1)S(1)} %get-tuple-element.33.refs_1_, f32[512,3072]{1,0:T(8,128)S(1)} %copy-done, f32[512,3072]{1,0:T(8,128)S(1)} %collective-permute-done.oth_ref.refs_3_), custom_call_target="tpu_custom_call" | custom-call | flops 1048576 | bytes 65536 | tf_op jit(solution)/shard_map/pallas_call | solution.py:125
  52.9 6.4 %collective-permute-done.1 = f32[256,768]{1,0:T(8,128)S(1)} collective-permute-done((f32[256,768]{1,0:T(8,128)S(1)}, f32[256,768]{1,0:T(8,128)S(1)}, u32[]{:S(2)}, u32[]{:S(2)}) %collective-permute-start.1) | collective-permute-done | bytes 786464 | tf_op jit(solution)/shard_map/ppermute | solution.py:30
  59.2 0.1 add.54
  59.3 1.1 collective-permute-done.2
  60.4 0.1 add.55
  60.5 0.1 fusion.2
  60.6 1.9 %collective-permute-start.6 = (f32[128,768]{1,0:T(8,128)S(1)}, f32[128,768]{1,0:T(8,128)S(1)}, u32[]{:S(2)}, u32[]{:S(2)}) collective-permute-start(f32[128,768]{1,0:T(8,128)S(1)} %get-tuple-element.57), channel_id=1, source_target_pairs={{0,2},{1,3},{2,0},{3,1},{4,6},{5,7},{6,4},{7,5},{8,10},{9,11},{10,... | collective-permute-start | bytes 1179656 | tf_op jit(solution)/shard_map/ppermute | solution.py:30
  62.5 1.1 %collective-permute-start.5 = (f32[128,768]{1,0:T(8,128)S(1)}, f32[128,768]{1,0:T(8,128)S(1)}, u32[]{:S(2)}, u32[]{:S(2)}) collective-permute-start(f32[128,768]{1,0:T(8,128)S(1)} %get-tuple-element.59), channel_id=1, source_target_pairs={{0,6},{1,7},{2,4},{3,5},{4,2},{5,3},{6,0},{7,1},{8,14},{9,15},{10,... | collective-permute-start | bytes 1179656 | tf_op jit(solution)/shard_map/ppermute | solution.py:30
  63.6 0.1 add.56
  63.7 0.1 fusion.1
  63.8 0.9 collective-permute-start.10
  64.7 0.1 add.57
  64.8 0.1 fusion
  64.9 1.0 collective-permute-start.11
  65.8 5.6 %collective-permute-done.5 = f32[128,768]{1,0:T(8,128)S(1)} collective-permute-done((f32[128,768]{1,0:T(8,128)S(1)}, f32[128,768]{1,0:T(8,128)S(1)}, u32[]{:S(2)}, u32[]{:S(2)}) %collective-permute-start.5) | collective-permute-done | bytes 393248 | tf_op jit(solution)/shard_map/ppermute | solution.py:30
  71.7 0.1 collective-permute-start.7
  71.8 2.1 %collective-permute-start.9 = (f32[32,1536]{1,0:T(8,128)S(1)}, f32[32,1536]{1,0:T(8,128)S(1)}, u32[]{:S(2)}, u32[]{:S(2)}) collective-permute-start(f32[32,1536]{1,0:T(8,128)S(1)} %pad_maximum_fusion.2), channel_id=1, source_target_pairs={{0,16},{1,17},{2,18},{3,19},{4,20},{5,21},{6,22},{7,23},{8,24},{9,... | collective-permute-start | bytes 589832 | tf_op jit(solution)/shard_map/ppermute | solution.py:30
  73.9 2.7 %collective-permute-start.8 = (f32[32,1536]{1,0:T(8,128)S(1)}, f32[32,1536]{1,0:T(8,128)S(1)}, u32[]{:S(2)}, u32[]{:S(2)}) collective-permute-start(f32[32,1536]{1,0:T(8,128)S(1)} %pad_maximum_fusion.1), channel_id=1, source_target_pairs={{0,24},{1,25},{2,26},{3,27},{4,28},{5,29},{6,30},{7,31},{8,16},{9,... | collective-permute-start | bytes 589832 | tf_op jit(solution)/shard_map/ppermute | solution.py:30
  76.9 2.2 %collective-permute-start.12 = (f32[32,1536]{1,0:T(8,128)S(1)}, f32[32,1536]{1,0:T(8,128)S(1)}, u32[]{:S(2)}, u32[]{:S(2)}) collective-permute-start(f32[32,1536]{1,0:T(8,128)S(1)} %pad_maximum_fusion.3), channel_id=1, source_target_pairs={{0,2},{1,3},{2,0},{3,1},{4,6},{5,7},{6,4},{7,5},{8,10},{9,11},{10,... | collective-permute-start | bytes 589832 | tf_op jit(solution)/shard_map/ppermute | solution.py:30
  79.1 1.1 %collective-permute-start.14 = (f32[32,1536]{1,0:T(8,128)S(1)}, f32[32,1536]{1,0:T(8,128)S(1)}, u32[]{:S(2)}, u32[]{:S(2)}) collective-permute-start(f32[32,1536]{1,0:T(8,128)S(1)} %pad_maximum_fusion.5), channel_id=1, source_target_pairs={{0,4},{1,5},{2,6},{3,7},{4,0},{5,1},{6,2},{7,3},{8,12},{9,13},{10,... | collective-permute-start | bytes 589832 | tf_op jit(solution)/shard_map/ppermute | solution.py:30
  80.3 1.0 collective-permute-start.13
  81.4 2.9 %collective-permute-done.9 = f32[32,1536]{1,0:T(8,128)S(1)} collective-permute-done((f32[32,1536]{1,0:T(8,128)S(1)}, f32[32,1536]{1,0:T(8,128)S(1)}, u32[]{:S(2)}, u32[]{:S(2)}) %collective-permute-start.9) | collective-permute-done | bytes 196640 | tf_op jit(solution)/shard_map/ppermute | solution.py:30
  84.3 0.1 maximum_add_fusion
  84.4 2.1 %collective-permute-done.14 = f32[32,1536]{1,0:T(8,128)S(1)} collective-permute-done((f32[32,1536]{1,0:T(8,128)S(1)}, f32[32,1536]{1,0:T(8,128)S(1)}, u32[]{:S(2)}, u32[]{:S(2)}) %collective-permute-start.14) | collective-permute-done | bytes 196640 | tf_op jit(solution)/shard_map/ppermute | solution.py:30
  86.5 1.7 %collective-permute-done.13 = f32[32,1536]{1,0:T(8,128)S(1)} collective-permute-done((f32[32,1536]{1,0:T(8,128)S(1)}, f32[32,1536]{1,0:T(8,128)S(1)}, u32[]{:S(2)}, u32[]{:S(2)}) %collective-permute-start.13) | collective-permute-done | bytes 196640 | tf_op jit(solution)/shard_map/ppermute | solution.py:30
  88.2 0.1 maximum_add_fusion.1
  88.3 0.1 constant_dynamic-slice_fusion.3
  88.4 2.0 %collective-permute-start.15 = (f32[32,1536]{1,0:T(8,128)S(1)}, f32[32,1536]{1,0:T(8,128)S(1)}, u32[]{:S(2)}, u32[]{:S(2)}) collective-permute-start(f32[32,1536]{1,0:T(8,128)S(1)} %constant_dynamic-slice_fusion.3), channel_id=1, source_target_pairs={{0,32},{1,33},{2,34},{3,35},{4,36},{5,37},{6,38},{7,39},{8,40},{9,... | collective-permute-start | bytes 589832 | tf_op jit(solution)/shard_map/ppermute | solution.py:30
  90.4 3.8 %collective-permute-done.15 = f32[32,1536]{1,0:T(8,128)S(1)} collective-permute-done((f32[32,1536]{1,0:T(8,128)S(1)}, f32[32,1536]{1,0:T(8,128)S(1)}, u32[]{:S(2)}, u32[]{:S(2)}) %collective-permute-start.15) | collective-permute-done | bytes 196640 | tf_op jit(solution)/shard_map/ppermute | solution.py:30
  94.2 0.1 dynamic-slice_add_fusion
  94.3 0.1 constant_dynamic-slice_fusion.2
  94.4 7.8 %collective-permute-start.16 = (f32[32,384]{1,0:T(8,128)S(1)}, f32[32,384]{1,0:T(8,128)S(1)}, u32[]{:S(2)}, u32[]{:S(2)}) collective-permute-start(f32[32,384]{1,0:T(8,128)S(1)} %get-tuple-element.77), channel_id=1, source_target_pairs={{0,128},{1,129},{2,130},{3,131},{4,132},{5,133},{6,134},{7,135},{8... | collective-permute-start | bytes 147464 | tf_op jit(solution)/shard_map/ppermute | solution.py:30
  102.2 1.3 %collective-permute-start.17 = (f32[32,384]{1,0:T(8,128)S(1)}, f32[32,384]{1,0:T(8,128)S(1)}, u32[]{:S(2)}, u32[]{:S(2)}) collective-permute-start(f32[32,384]{1,0:T(8,128)S(1)} %get-tuple-element.79), channel_id=1, source_target_pairs={{0,64},{1,65},{2,66},{3,67},{4,68},{5,69},{6,70},{7,71},{8,72},{9,... | collective-permute-start | bytes 147464 | tf_op jit(solution)/shard_map/ppermute | solution.py:30
  103.5 0.8 collective-permute-done.16
  104.3 4.1 %collective-permute-done.18 = f32[32,384]{1,0:T(8,128)S(1)} collective-permute-done((f32[32,384]{1,0:T(8,128)S(1)}, f32[32,384]{1,0:T(8,128)S(1)}, u32[]{:S(2)}, u32[]{:S(2)}) %collective-permute-start.18) | collective-permute-done | bytes 49184 | tf_op jit(solution)/shard_map/ppermute | solution.py:30
  108.4 0.7 add_multiply_fusion
  (39 shorter events, 0.6 us)
Async XLA Ops:
  0.1 37.1 %collective-permute-start = (f32[512,3072]{1,0:T(8,128)}, f32[512,3072]{1,0:T(8,128)S(1)}, u32[]{:S(2)}, u32[]{:S(2)}) collective-permute-start(f32[512,3072]{1,0:T(8,128)} %refs_2_.4), channel_id=1, source_target_pairs={{0,1},{1,0},{2,3},{3,2},{4,5},{5,4},{6,7},{7,6},{8,9},{9,8},{10,11... | collective-permute-start | bytes 18874376 | tf_op jit(solution)/shard_map/ppermute | solution.py:30
  0.1 1.6 %copy-start.1 = (f32[32,16384]{1,0:T(8,128)S(1)}, f32[32,16384]{1,0:T(8,128)}, u32[]{:S(2)}) copy-start(f32[32,16384]{1,0:T(8,128)} %a_ref) | copy-start | bytes 6291460
  1.7 35.5 %copy-start = (f32[512,3072]{1,0:T(8,128)S(1)}, f32[512,3072]{1,0:T(8,128)}, u32[]{:S(2)}) copy-start(f32[512,3072]{1,0:T(8,128)} %refs_2_.4) | copy-start | bytes 18874372
  40.6 18.6 %collective-permute-start.1 = (f32[256,768]{1,0:T(8,128)S(1)}, f32[256,768]{1,0:T(8,128)S(1)}, u32[]{:S(2)}, u32[]{:S(2)}) collective-permute-start(f32[256,768]{1,0:T(8,128)S(1)} %get-tuple-element.37), channel_id=1, source_target_pairs={{0,2},{1,3},{2,0},{3,1},{4,6},{5,7},{6,4},{7,5},{8,10},{9,11},{10,... | collective-permute-start | bytes 2359304 | tf_op jit(solution)/shard_map/ppermute | solution.py:30
  42.2 18.3 %collective-permute-start.2 = (f32[256,768]{1,0:T(8,128)S(1)}, f32[256,768]{1,0:T(8,128)S(1)}, u32[]{:S(2)}, u32[]{:S(2)}) collective-permute-start(f32[256,768]{1,0:T(8,128)S(1)} %get-tuple-element.39), channel_id=1, source_target_pairs={{0,6},{1,7},{2,4},{3,5},{4,2},{5,3},{6,0},{7,1},{8,14},{9,15},{10,... | collective-permute-start | bytes 2359304 | tf_op jit(solution)/shard_map/ppermute | solution.py:30
  44.9 18.7 %collective-permute-start.3 = (f32[256,768]{1,0:T(8,128)S(1)}, f32[256,768]{1,0:T(8,128)S(1)}, u32[]{:S(2)}, u32[]{:S(2)}) collective-permute-start(f32[256,768]{1,0:T(8,128)S(1)} %get-tuple-element.41), channel_id=1, source_target_pairs={{0,8},{1,9},{2,10},{3,11},{4,12},{5,13},{6,14},{7,15},{8,0},{9,1},... | collective-permute-start | bytes 2359304 | tf_op jit(solution)/shard_map/ppermute | solution.py:30
  45.5 19.2 %collective-permute-start.4 = (f32[256,768]{1,0:T(8,128)S(1)}, f32[256,768]{1,0:T(8,128)S(1)}, u32[]{:S(2)}, u32[]{:S(2)}) collective-permute-start(f32[256,768]{1,0:T(8,128)S(1)} %get-tuple-element.34), channel_id=1, source_target_pairs={{0,24},{1,25},{2,26},{3,27},{4,28},{5,29},{6,30},{7,31},{8,16},{9,... | collective-permute-start | bytes 2359304 | tf_op jit(solution)/shard_map/ppermute | solution.py:30
  60.6 11.0 %collective-permute-start.6 = (f32[128,768]{1,0:T(8,128)S(1)}, f32[128,768]{1,0:T(8,128)S(1)}, u32[]{:S(2)}, u32[]{:S(2)}) collective-permute-start(f32[128,768]{1,0:T(8,128)S(1)} %get-tuple-element.57), channel_id=1, source_target_pairs={{0,2},{1,3},{2,0},{3,1},{4,6},{5,7},{6,4},{7,5},{8,10},{9,11},{10,... | collective-permute-start | bytes 1179656 | tf_op jit(solution)/shard_map/ppermute | solution.py:30
  62.5 9.0 %collective-permute-start.5 = (f32[128,768]{1,0:T(8,128)S(1)}, f32[128,768]{1,0:T(8,128)S(1)}, u32[]{:S(2)}, u32[]{:S(2)}) collective-permute-start(f32[128,768]{1,0:T(8,128)S(1)} %get-tuple-element.59), channel_id=1, source_target_pairs={{0,6},{1,7},{2,4},{3,5},{4,2},{5,3},{6,0},{7,1},{8,14},{9,15},{10,... | collective-permute-start | bytes 1179656 | tf_op jit(solution)/shard_map/ppermute | solution.py:30
  63.8 12.9 %collective-permute-start.10 = (f32[128,768]{1,0:T(8,128)S(1)}, f32[128,768]{1,0:T(8,128)S(1)}, u32[]{:S(2)}, u32[]{:S(2)}) collective-permute-start(f32[128,768]{1,0:T(8,128)S(1)} %get-tuple-element.55), channel_id=1, source_target_pairs={{0,24},{1,25},{2,26},{3,27},{4,28},{5,29},{6,30},{7,31},{8,16},{9,... | collective-permute-start | bytes 1179656 | tf_op jit(solution)/shard_map/ppermute | solution.py:30
  64.9 11.9 %collective-permute-start.11 = (f32[128,768]{1,0:T(8,128)S(1)}, f32[128,768]{1,0:T(8,128)S(1)}, u32[]{:S(2)}, u32[]{:S(2)}) collective-permute-start(f32[128,768]{1,0:T(8,128)S(1)} %get-tuple-element.53), channel_id=1, source_target_pairs={{0,8},{1,9},{2,10},{3,11},{4,12},{5,13},{6,14},{7,15},{8,0},{9,1},... | collective-permute-start | bytes 1179656 | tf_op jit(solution)/shard_map/ppermute | solution.py:30
  71.7 8.6 %collective-permute-start.7 = (f32[32,1536]{1,0:T(8,128)S(1)}, f32[32,1536]{1,0:T(8,128)S(1)}, u32[]{:S(2)}, u32[]{:S(2)}) collective-permute-start(f32[32,1536]{1,0:T(8,128)S(1)} %pad_maximum_fusion), channel_id=1, source_target_pairs={{0,8},{1,9},{2,10},{3,11},{4,12},{5,13},{6,14},{7,15},{8,0},{9,1},... | collective-permute-start | bytes 589832 | tf_op jit(solution)/shard_map/ppermute | solution.py:30
  71.8 12.5 %collective-permute-start.9 = (f32[32,1536]{1,0:T(8,128)S(1)}, f32[32,1536]{1,0:T(8,128)S(1)}, u32[]{:S(2)}, u32[]{:S(2)}) collective-permute-start(f32[32,1536]{1,0:T(8,128)S(1)} %pad_maximum_fusion.2), channel_id=1, source_target_pairs={{0,16},{1,17},{2,18},{3,19},{4,20},{5,21},{6,22},{7,23},{8,24},{9,... | collective-permute-start | bytes 589832 | tf_op jit(solution)/shard_map/ppermute | solution.py:30
  73.9 10.3 %collective-permute-start.8 = (f32[32,1536]{1,0:T(8,128)S(1)}, f32[32,1536]{1,0:T(8,128)S(1)}, u32[]{:S(2)}, u32[]{:S(2)}) collective-permute-start(f32[32,1536]{1,0:T(8,128)S(1)} %pad_maximum_fusion.1), channel_id=1, source_target_pairs={{0,24},{1,25},{2,26},{3,27},{4,28},{5,29},{6,30},{7,31},{8,16},{9,... | collective-permute-start | bytes 589832 | tf_op jit(solution)/shard_map/ppermute | solution.py:30
  76.9 7.5 %collective-permute-start.12 = (f32[32,1536]{1,0:T(8,128)S(1)}, f32[32,1536]{1,0:T(8,128)S(1)}, u32[]{:S(2)}, u32[]{:S(2)}) collective-permute-start(f32[32,1536]{1,0:T(8,128)S(1)} %pad_maximum_fusion.3), channel_id=1, source_target_pairs={{0,2},{1,3},{2,0},{3,1},{4,6},{5,7},{6,4},{7,5},{8,10},{9,11},{10,... | collective-permute-start | bytes 589832 | tf_op jit(solution)/shard_map/ppermute | solution.py:30
  79.1 7.4 %collective-permute-start.14 = (f32[32,1536]{1,0:T(8,128)S(1)}, f32[32,1536]{1,0:T(8,128)S(1)}, u32[]{:S(2)}, u32[]{:S(2)}) collective-permute-start(f32[32,1536]{1,0:T(8,128)S(1)} %pad_maximum_fusion.5), channel_id=1, source_target_pairs={{0,4},{1,5},{2,6},{3,7},{4,0},{5,1},{6,2},{7,3},{8,12},{9,13},{10,... | collective-permute-start | bytes 589832 | tf_op jit(solution)/shard_map/ppermute | solution.py:30
  80.3 7.9 %collective-permute-start.13 = (f32[32,1536]{1,0:T(8,128)S(1)}, f32[32,1536]{1,0:T(8,128)S(1)}, u32[]{:S(2)}, u32[]{:S(2)}) collective-permute-start(f32[32,1536]{1,0:T(8,128)S(1)} %pad_maximum_fusion.4), channel_id=1, source_target_pairs={{0,6},{1,7},{2,4},{3,5},{4,2},{5,3},{6,0},{7,1},{8,14},{9,15},{10,... | collective-permute-start | bytes 589832 | tf_op jit(solution)/shard_map/ppermute | solution.py:30
  88.4 5.8 %collective-permute-start.15 = (f32[32,1536]{1,0:T(8,128)S(1)}, f32[32,1536]{1,0:T(8,128)S(1)}, u32[]{:S(2)}, u32[]{:S(2)}) collective-permute-start(f32[32,1536]{1,0:T(8,128)S(1)} %constant_dynamic-slice_fusion.3), channel_id=1, source_target_pairs={{0,32},{1,33},{2,34},{3,35},{4,36},{5,37},{6,38},{7,39},{8,40},{9,... | collective-permute-start | bytes 589832 | tf_op jit(solution)/shard_map/ppermute | solution.py:30
  94.4 9.9 %collective-permute-start.16 = (f32[32,384]{1,0:T(8,128)S(1)}, f32[32,384]{1,0:T(8,128)S(1)}, u32[]{:S(2)}, u32[]{:S(2)}) collective-permute-start(f32[32,384]{1,0:T(8,128)S(1)} %get-tuple-element.77), channel_id=1, source_target_pairs={{0,128},{1,129},{2,130},{3,131},{4,132},{5,133},{6,134},{7,135},{8... | collective-permute-start | bytes 147464 | tf_op jit(solution)/shard_map/ppermute | solution.py:30
  102.2 6.2 %collective-permute-start.18 = (f32[32,384]{1,0:T(8,128)S(1)}, f32[32,384]{1,0:T(8,128)S(1)}, u32[]{:S(2)}, u32[]{:S(2)}) collective-permute-start(f32[32,384]{1,0:T(8,128)S(1)} %get-tuple-element.78), channel_id=1, source_target_pairs={{0,192},{1,193},{2,194},{3,195},{4,196},{5,197},{6,198},{7,199},{8... | collective-permute-start | bytes 147464 | tf_op jit(solution)/shard_map/ppermute | solution.py:30
  102.2 6.2 %collective-permute-start.17 = (f32[32,384]{1,0:T(8,128)S(1)}, f32[32,384]{1,0:T(8,128)S(1)}, u32[]{:S(2)}, u32[]{:S(2)}) collective-permute-start(f32[32,384]{1,0:T(8,128)S(1)} %get-tuple-element.79), channel_id=1, source_target_pairs={{0,64},{1,65},{2,66},{3,67},{4,68},{5,69},{6,70},{7,71},{8,72},{9,... | collective-permute-start | bytes 147464 | tf_op jit(solution)/shard_map/ppermute | solution.py:30

commit v6 on v5

--- a/solution.py
+++ b/solution.py
@@ -12,7 +12,7 @@
 ROWS, DEPTH, WIDTH = 32, 512, 384
 GROUPS = 4
 NEAR_FIRST, FAR_FIRST = (2, 1, 3, 0), (2, 3, 1, 0)
-SECOND = (1, 3, 2, 0)
+SECOND = (2, 1, 3, 0)
 CHEAP = pl.CostEstimate(flops=1 << 20, bytes_accessed=1 << 16, transcendentals=0)
 VMEM = pl.BlockSpec(memory_space=pltpu.VMEM)
 

time: 110 us -> 109 us (level)
  transfers between devices with their start and end apart: 19 -> 19, of which waited for: 9 -> 11; matrix products, arithmetic and copies ran while one was open for 1% -> 1% of each run, Pallas kernels for 8% -> 8%
where the time goes in v6:
time: 109 us
  blocking collectives  35.3 us (32%)
  waiting for transfers between devices  28.9 us (27%)
  starting transfers between devices  28.4 us (26%)
  Pallas kernels  12.1 us (11%)
  local copies, waits for them, and re-layouts  2.2 us (2%)
  other arithmetic  1.69 us (2%)
    all_to_all x1, blocking collectives, body(): mine = lax.all_to_all(laid, ('y', 'x'), split_axis=0, concat_axis=0)  35.3 us
    ppermute x19, waiting for transfers between devices, exchange(): return lax.ppermute(value, AXES, flip(axis, mask))  28.9 us
    ppermute x19, starting transfers between devices, exchange(): return lax.ppermute(value, AXES, flip(axis, mask))  28.4 us
    pallas_call x4, Pallas kernels, products(): keeps += call(kernel, (out,), [VMEM] * 4, 6)(hi, lo, own, oth)  5.86 us
    pallas_call x1, Pallas kernels, products(): call(first_kernel, (out,) * 2 + (part, part), [smem, VMEM, VMEM, VMEM], 6)  3.39 us
    pallas_call x1, Pallas kernels, products(): sends += call(later, (out,) * 2, [VMEM] * 4, 6)(hi, lo, own, oth)  2.73 us
  transfers between devices with their start and end apart: 19, of which 11 were waited for; matrix products, arithmetic and copies ran while one was open for 1% of the time, Pallas kernels for 8%

profile of v6, /device:TPU:2, one launch (start us, length us, event | category | flops | bytes accessed | tf_op | source)
XLA Modules:
  0.0 108.9 jit_solution(9105421000185119815)
XLA Ops:
  0.0 0.1 pad_add_fusion.where
  0.1 1.6 %copy-done.1 = f32[32,16384]{1,0:T(8,128)S(1)} copy-done((f32[32,16384]{1,0:T(8,128)S(1)}, f32[32,16384]{1,0:T(8,128)}, u32[]{:S(2)}) %copy-start.1) | copy-done | bytes 2097176
  1.7 0.1 shard_map.28
  1.9 35.3 %all_to_all.5 = f32[16,32,1024]{2,1,0:T(8,128)S(1)} all-to-all(f32[16,32,1024]{2,1,0:T(8,128)S(1)} %shard_map.28), channel_id=1, replica_groups=mesh['z'=8,'y'=4,'x'=4,'core'=2] {'y','x'}, dimensions={0} | all-to-all | bytes 4194304 | tf_op jit(solution)/shard_map/all_to_all | solution.py:139
  37.2 3.4 %shard_map.29 = (f32[256,768]{1,0:T(8,128)S(1)}, f32[256,768]{1,0:T(8,128)S(1)}, bf16[512,1024]{1,0:T(8,128)(2,1)S(1)}, bf16[512,1024]{1,0:T(8,128)(2,1)S(1)}) custom-call(s32[3]{0:T(128)S(1)} %pad_add_fusion.where, f32[512,1024]{1,0:T(8,128)S(1)} %bitcast.4, f32[512,3072]{1,0:T(8,128)S(1)} %copy-done, f32[512,3072]{1,0:T(8,128)S(1)} %collective-permute-done.oth_ref.refs_3_), custom_call_target="tpu_custom_call" | custom-call | flops 1048576 | bytes 65536 | tf_op jit(solution)/shard_map/pallas_call | solution.py:116
  40.6 1.5 %collective-permute-start.1 = (f32[256,768]{1,0:T(8,128)S(1)}, f32[256,768]{1,0:T(8,128)S(1)}, u32[]{:S(2)}, u32[]{:S(2)}) collective-permute-start(f32[256,768]{1,0:T(8,128)S(1)} %get-tuple-element.37), channel_id=1, source_target_pairs={{0,2},{1,3},{2,0},{3,1},{4,6},{5,7},{6,4},{7,5},{8,10},{9,11},{10,... | collective-permute-start | bytes 2359304 | tf_op jit(solution)/shard_map/ppermute | solution.py:30
  42.2 2.7 %shard_map.30 = (f32[256,768]{1,0:T(8,128)S(1)}, f32[256,768]{1,0:T(8,128)S(1)}) custom-call(bf16[512,1024]{1,0:T(8,128)(2,1)S(1)} %get-tuple-element.35.refs_0_, bf16[512,1024]{1,0:T(8,128)(2,1)S(1)} %get-tuple-element.33.refs_1_, f32[512,3072]{1,0:T(8,128)S(1)} %copy-done, f32[512,3072]{1,0:T(8,128)S(1)} %collective-permute-done.oth_ref.refs_3_), custom_call_target="tpu_custom_call" | custom-call | flops 1048576 | bytes 65536 | tf_op jit(solution)/shard_map/pallas_call | solution.py:120
  44.9 0.6 collective-permute-start.3
  45.5 1.4 %collective-permute-start.4 = (f32[256,768]{1,0:T(8,128)S(1)}, f32[256,768]{1,0:T(8,128)S(1)}, u32[]{:S(2)}, u32[]{:S(2)}) collective-permute-start(f32[256,768]{1,0:T(8,128)S(1)} %get-tuple-element.34), channel_id=1, source_target_pairs={{0,24},{1,25},{2,26},{3,27},{4,28},{5,29},{6,30},{7,31},{8,16},{9,... | collective-permute-start | bytes 2359304 | tf_op jit(solution)/shard_map/ppermute | solution.py:30
  47.0 1.5 %shard_map.34 = f32[256,768]{1,0:T(8,128)S(1)} custom-call(bf16[512,1024]{1,0:T(8,128)(2,1)S(1)} %get-tuple-element.35.refs_0_, bf16[512,1024]{1,0:T(8,128)(2,1)S(1)} %get-tuple-element.33.refs_1_, f32[512,3072]{1,0:T(8,128)S(1)} %copy-done, f32[512,3072]{1,0:T(8,128)S(1)} %collective-permute-done.oth_ref.refs_3_), custom_call_target="tpu_custom_call" | custom-call | flops 1048576 | bytes 65536 | tf_op jit(solution)/shard_map/pallas_call | solution.py:125
  48.4 1.5 %shard_map.33 = f32[256,768]{1,0:T(8,128)S(1)} custom-call(bf16[512,1024]{1,0:T(8,128)(2,1)S(1)} %get-tuple-element.35.refs_0_, bf16[512,1024]{1,0:T(8,128)(2,1)S(1)} %get-tuple-element.33.refs_1_, f32[512,3072]{1,0:T(8,128)S(1)} %copy-done, f32[512,3072]{1,0:T(8,128)S(1)} %collective-permute-done.oth_ref.refs_3_), custom_call_target="tpu_custom_call" | custom-call | flops 1048576 | bytes 65536 | tf_op jit(solution)/shard_map/pallas_call | solution.py:125
  49.9 1.5 %shard_map.32 = f32[256,768]{1,0:T(8,128)S(1)} custom-call(bf16[512,1024]{1,0:T(8,128)(2,1)S(1)} %get-tuple-element.35.refs_0_, bf16[512,1024]{1,0:T(8,128)(2,1)S(1)} %get-tuple-element.33.refs_1_, f32[512,3072]{1,0:T(8,128)S(1)} %copy-done, f32[512,3072]{1,0:T(8,128)S(1)} %collective-permute-done.oth_ref.refs_3_), custom_call_target="tpu_custom_call" | custom-call | flops 1048576 | bytes 65536 | tf_op jit(solution)/shard_map/pallas_call | solution.py:125
  51.4 1.5 %shard_map.31 = f32[256,768]{1,0:T(8,128)S(1)} custom-call(bf16[512,1024]{1,0:T(8,128)(2,1)S(1)} %get-tuple-element.35.refs_0_, bf16[512,1024]{1,0:T(8,128)(2,1)S(1)} %get-tuple-element.33.refs_1_, f32[512,3072]{1,0:T(8,128)S(1)} %copy-done, f32[512,3072]{1,0:T(8,128)S(1)} %collective-permute-done.oth_ref.refs_3_), custom_call_target="tpu_custom_call" | custom-call | flops 1048576 | bytes 65536 | tf_op jit(solution)/shard_map/pallas_call | solution.py:125
  52.9 6.4 %collective-permute-done.1 = f32[256,768]{1,0:T(8,128)S(1)} collective-permute-done((f32[256,768]{1,0:T(8,128)S(1)}, f32[256,768]{1,0:T(8,128)S(1)}, u32[]{:S(2)}, u32[]{:S(2)}) %collective-permute-start.1) | collective-permute-done | bytes 786464 | tf_op jit(solution)/shard_map/ppermute | solution.py:30
  59.2 0.1 add.54
  59.3 1.1 collective-permute-done.2
  60.4 0.1 add.55
  60.6 1.9 %collective-permute-start.6 = (f32[128,768]{1,0:T(8,128)S(1)}, f32[128,768]{1,0:T(8,128)S(1)}, u32[]{:S(2)}, u32[]{:S(2)}) collective-permute-start(f32[128,768]{1,0:T(8,128)S(1)} %get-tuple-element.57), channel_id=1, source_target_pairs={{0,2},{1,3},{2,0},{3,1},{4,6},{5,7},{6,4},{7,5},{8,10},{9,11},{10,... | collective-permute-start | bytes 1179656 | tf_op jit(solution)/shard_map/ppermute | solution.py:30
  62.5 1.1 %collective-permute-start.5 = (f32[128,768]{1,0:T(8,128)S(1)}, f32[128,768]{1,0:T(8,128)S(1)}, u32[]{:S(2)}, u32[]{:S(2)}) collective-permute-start(f32[128,768]{1,0:T(8,128)S(1)} %get-tuple-element.59), channel_id=1, source_target_pairs={{0,6},{1,7},{2,4},{3,5},{4,2},{5,3},{6,0},{7,1},{8,14},{9,15},{10,... | collective-permute-start | bytes 1179656 | tf_op jit(solution)/shard_map/ppermute | solution.py:30
  63.6 0.1 add.56
  63.7 0.1 fusion.1
  63.8 0.9 collective-permute-start.10
  64.7 0.1 add.57
  64.8 0.1 fusion
  64.9 1.0 collective-permute-start.11
  65.8 5.6 %collective-permute-done.5 = f32[128,768]{1,0:T(8,128)S(1)} collective-permute-done((f32[128,768]{1,0:T(8,128)S(1)}, f32[128,768]{1,0:T(8,128)S(1)}, u32[]{:S(2)}, u32[]{:S(2)}) %collective-permute-start.5) | collective-permute-done | bytes 393248 | tf_op jit(solution)/shard_map/ppermute | solution.py:30
  71.7 0.7 collective-permute-start.7
  72.4 1.8 %collective-permute-start.9 = (f32[32,1536]{1,0:T(8,128)S(1)}, f32[32,1536]{1,0:T(8,128)S(1)}, u32[]{:S(2)}, u32[]{:S(2)}) collective-permute-start(f32[32,1536]{1,0:T(8,128)S(1)} %pad_maximum_fusion.2), channel_id=1, source_target_pairs={{0,24},{1,25},{2,26},{3,27},{4,28},{5,29},{6,30},{7,31},{8,16},{9,... | collective-permute-start | bytes 589832 | tf_op jit(solution)/shard_map/ppermute | solution.py:30
  74.2 1.2 %collective-permute-start.8 = (f32[32,1536]{1,0:T(8,128)S(1)}, f32[32,1536]{1,0:T(8,128)S(1)}, u32[]{:S(2)}, u32[]{:S(2)}) collective-permute-start(f32[32,1536]{1,0:T(8,128)S(1)} %pad_maximum_fusion.1), channel_id=1, source_target_pairs={{0,8},{1,9},{2,10},{3,11},{4,12},{5,13},{6,14},{7,15},{8,0},{9,1},... | collective-permute-start | bytes 589832 | tf_op jit(solution)/shard_map/ppermute | solution.py:30
  75.5 2.7 %collective-permute-done.10 = f32[128,768]{1,0:T(8,128)S(1)} collective-permute-done((f32[128,768]{1,0:T(8,128)S(1)}, f32[128,768]{1,0:T(8,128)S(1)}, u32[]{:S(2)}, u32[]{:S(2)}) %collective-permute-start.10) | collective-permute-done | bytes 393248 | tf_op jit(solution)/shard_map/ppermute | solution.py:30
  78.4 0.1 collective-permute-start.12
  78.5 3.5 %collective-permute-start.14 = (f32[32,1536]{1,0:T(8,128)S(1)}, f32[32,1536]{1,0:T(8,128)S(1)}, u32[]{:S(2)}, u32[]{:S(2)}) collective-permute-start(f32[32,1536]{1,0:T(8,128)S(1)} %pad_maximum_fusion.5), channel_id=1, source_target_pairs={{0,6},{1,7},{2,4},{3,5},{4,2},{5,3},{6,0},{7,1},{8,14},{9,15},{10,... | collective-permute-start | bytes 589832 | tf_op jit(solution)/shard_map/ppermute | solution.py:30
  82.1 0.2 collective-permute-done.7
  82.3 1.8 %collective-permute-start.13 = (f32[32,1536]{1,0:T(8,128)S(1)}, f32[32,1536]{1,0:T(8,128)S(1)}, u32[]{:S(2)}, u32[]{:S(2)}) collective-permute-start(f32[32,1536]{1,0:T(8,128)S(1)} %pad_maximum_fusion.4), channel_id=1, source_target_pairs={{0,2},{1,3},{2,0},{3,1},{4,6},{5,7},{6,4},{7,5},{8,10},{9,11},{10,... | collective-permute-start | bytes 589832 | tf_op jit(solution)/shard_map/ppermute | solution.py:30
  84.1 1.6 %collective-permute-done.12 = f32[32,1536]{1,0:T(8,128)S(1)} collective-permute-done((f32[32,1536]{1,0:T(8,128)S(1)}, f32[32,1536]{1,0:T(8,128)S(1)}, u32[]{:S(2)}, u32[]{:S(2)}) %collective-permute-start.12) | collective-permute-done | bytes 196640 | tf_op jit(solution)/shard_map/ppermute | solution.py:30
  85.8 2.0 %collective-permute-done.14 = f32[32,1536]{1,0:T(8,128)S(1)} collective-permute-done((f32[32,1536]{1,0:T(8,128)S(1)}, f32[32,1536]{1,0:T(8,128)S(1)}, u32[]{:S(2)}, u32[]{:S(2)}) %collective-permute-start.14) | collective-permute-done | bytes 196640 | tf_op jit(solution)/shard_map/ppermute | solution.py:30
  87.8 0.2 collective-permute-done.13
  87.9 0.1 maximum_add_fusion.1
  88.1 0.1 constant_dynamic-slice_fusion.3
  88.2 2.0 %collective-permute-start.15 = (f32[32,1536]{1,0:T(8,128)S(1)}, f32[32,1536]{1,0:T(8,128)S(1)}, u32[]{:S(2)}, u32[]{:S(2)}) collective-permute-start(f32[32,1536]{1,0:T(8,128)S(1)} %constant_dynamic-slice_fusion.3), channel_id=1, source_target_pairs={{0,32},{1,33},{2,34},{3,35},{4,36},{5,37},{6,38},{7,39},{8,40},{9,... | collective-permute-start | bytes 589832 | tf_op jit(solution)/shard_map/ppermute | solution.py:30
  90.2 3.8 %collective-permute-done.15 = f32[32,1536]{1,0:T(8,128)S(1)} collective-permute-done((f32[32,1536]{1,0:T(8,128)S(1)}, f32[32,1536]{1,0:T(8,128)S(1)}, u32[]{:S(2)}, u32[]{:S(2)}) %collective-permute-start.15) | collective-permute-done | bytes 196640 | tf_op jit(solution)/shard_map/ppermute | solution.py:30
  94.0 0.1 dynamic-slice_add_fusion
  94.1 0.1 constant_dynamic-slice_fusion.2
  94.2 7.8 %collective-permute-start.16 = (f32[32,384]{1,0:T(8,128)S(1)}, f32[32,384]{1,0:T(8,128)S(1)}, u32[]{:S(2)}, u32[]{:S(2)}) collective-permute-start(f32[32,384]{1,0:T(8,128)S(1)} %get-tuple-element.77), channel_id=1, source_target_pairs={{0,128},{1,129},{2,130},{3,131},{4,132},{5,133},{6,134},{7,135},{8... | collective-permute-start | bytes 147464 | tf_op jit(solution)/shard_map/ppermute | solution.py:30
  102.0 1.0 collective-permute-start.17
  103.0 1.1 %collective-permute-done.16 = f32[32,384]{1,0:T(8,128)S(1)} collective-permute-done((f32[32,384]{1,0:T(8,128)S(1)}, f32[32,384]{1,0:T(8,128)S(1)}, u32[]{:S(2)}, u32[]{:S(2)}) %collective-permute-start.16) | collective-permute-done | bytes 49184 | tf_op jit(solution)/shard_map/ppermute | solution.py:30
  104.1 4.1 %collective-permute-done.18 = f32[32,384]{1,0:T(8,128)S(1)} collective-permute-done((f32[32,384]{1,0:T(8,128)S(1)}, f32[32,384]{1,0:T(8,128)S(1)}, u32[]{:S(2)}, u32[]{:S(2)}) %collective-permute-start.18) | collective-permute-done | bytes 49184 | tf_op jit(solution)/shard_map/ppermute | solution.py:30
  108.2 0.7 add_multiply_fusion
  (39 shorter events, 0.7 us)
Async XLA Ops:
  0.1 37.1 %collective-permute-start = (f32[512,3072]{1,0:T(8,128)}, f32[512,3072]{1,0:T(8,128)S(1)}, u32[]{:S(2)}, u32[]{:S(2)}) collective-permute-start(f32[512,3072]{1,0:T(8,128)} %refs_2_.4), channel_id=1, source_target_pairs={{0,1},{1,0},{2,3},{3,2},{4,5},{5,4},{6,7},{7,6},{8,9},{9,8},{10,11... | collective-permute-start | bytes 18874376 | tf_op jit(solution)/shard_map/ppermute | solution.py:30
  0.1 1.6 %copy-start.1 = (f32[32,16384]{1,0:T(8,128)S(1)}, f32[32,16384]{1,0:T(8,128)}, u32[]{:S(2)}) copy-start(f32[32,16384]{1,0:T(8,128)} %a_ref) | copy-start | bytes 6291460
  1.7 35.5 %copy-start = (f32[512,3072]{1,0:T(8,128)S(1)}, f32[512,3072]{1,0:T(8,128)}, u32[]{:S(2)}) copy-start(f32[512,3072]{1,0:T(8,128)} %refs_2_.4) | copy-start | bytes 18874372
  40.6 18.6 %collective-permute-start.1 = (f32[256,768]{1,0:T(8,128)S(1)}, f32[256,768]{1,0:T(8,128)S(1)}, u32[]{:S(2)}, u32[]{:S(2)}) collective-permute-start(f32[256,768]{1,0:T(8,128)S(1)} %get-tuple-element.37), channel_id=1, source_target_pairs={{0,2},{1,3},{2,0},{3,1},{4,6},{5,7},{6,4},{7,5},{8,10},{9,11},{10,... | collective-permute-start | bytes 2359304 | tf_op jit(solution)/shard_map/ppermute | solution.py:30
  42.2 18.3 %collective-permute-start.2 = (f32[256,768]{1,0:T(8,128)S(1)}, f32[256,768]{1,0:T(8,128)S(1)}, u32[]{:S(2)}, u32[]{:S(2)}) collective-permute-start(f32[256,768]{1,0:T(8,128)S(1)} %get-tuple-element.39), channel_id=1, source_target_pairs={{0,6},{1,7},{2,4},{3,5},{4,2},{5,3},{6,0},{7,1},{8,14},{9,15},{10,... | collective-permute-start | bytes 2359304 | tf_op jit(solution)/shard_map/ppermute | solution.py:30
  44.9 18.7 %collective-permute-start.3 = (f32[256,768]{1,0:T(8,128)S(1)}, f32[256,768]{1,0:T(8,128)S(1)}, u32[]{:S(2)}, u32[]{:S(2)}) collective-permute-start(f32[256,768]{1,0:T(8,128)S(1)} %get-tuple-element.41), channel_id=1, source_target_pairs={{0,8},{1,9},{2,10},{3,11},{4,12},{5,13},{6,14},{7,15},{8,0},{9,1},... | collective-permute-start | bytes 2359304 | tf_op jit(solution)/shard_map/ppermute | solution.py:30
  45.5 19.2 %collective-permute-start.4 = (f32[256,768]{1,0:T(8,128)S(1)}, f32[256,768]{1,0:T(8,128)S(1)}, u32[]{:S(2)}, u32[]{:S(2)}) collective-permute-start(f32[256,768]{1,0:T(8,128)S(1)} %get-tuple-element.34), channel_id=1, source_target_pairs={{0,24},{1,25},{2,26},{3,27},{4,28},{5,29},{6,30},{7,31},{8,16},{9,... | collective-permute-start | bytes 2359304 | tf_op jit(solution)/shard_map/ppermute | solution.py:30
  60.6 11.0 %collective-permute-start.6 = (f32[128,768]{1,0:T(8,128)S(1)}, f32[128,768]{1,0:T(8,128)S(1)}, u32[]{:S(2)}, u32[]{:S(2)}) collective-permute-start(f32[128,768]{1,0:T(8,128)S(1)} %get-tuple-element.57), channel_id=1, source_target_pairs={{0,2},{1,3},{2,0},{3,1},{4,6},{5,7},{6,4},{7,5},{8,10},{9,11},{10,... | collective-permute-start | bytes 1179656 | tf_op jit(solution)/shard_map/ppermute | solution.py:30
  62.5 9.0 %collective-permute-start.5 = (f32[128,768]{1,0:T(8,128)S(1)}, f32[128,768]{1,0:T(8,128)S(1)}, u32[]{:S(2)}, u32[]{:S(2)}) collective-permute-start(f32[128,768]{1,0:T(8,128)S(1)} %get-tuple-element.59), channel_id=1, source_target_pairs={{0,6},{1,7},{2,4},{3,5},{4,2},{5,3},{6,0},{7,1},{8,14},{9,15},{10,... | collective-permute-start | bytes 1179656 | tf_op jit(solution)/shard_map/ppermute | solution.py:30
  63.8 14.4 %collective-permute-start.10 = (f32[128,768]{1,0:T(8,128)S(1)}, f32[128,768]{1,0:T(8,128)S(1)}, u32[]{:S(2)}, u32[]{:S(2)}) collective-permute-start(f32[128,768]{1,0:T(8,128)S(1)} %get-tuple-element.55), channel_id=1, source_target_pairs={{0,24},{1,25},{2,26},{3,27},{4,28},{5,29},{6,30},{7,31},{8,16},{9,... | collective-permute-start | bytes 1179656 | tf_op jit(solution)/shard_map/ppermute | solution.py:30
  64.9 13.4 %collective-permute-start.11 = (f32[128,768]{1,0:T(8,128)S(1)}, f32[128,768]{1,0:T(8,128)S(1)}, u32[]{:S(2)}, u32[]{:S(2)}) collective-permute-start(f32[128,768]{1,0:T(8,128)S(1)} %get-tuple-element.53), channel_id=1, source_target_pairs={{0,8},{1,9},{2,10},{3,11},{4,12},{5,13},{6,14},{7,15},{8,0},{9,1},... | collective-permute-start | bytes 1179656 | tf_op jit(solution)/shard_map/ppermute | solution.py:30
  71.7 10.6 %collective-permute-start.7 = (f32[32,1536]{1,0:T(8,128)S(1)}, f32[32,1536]{1,0:T(8,128)S(1)}, u32[]{:S(2)}, u32[]{:S(2)}) collective-permute-start(f32[32,1536]{1,0:T(8,128)S(1)} %pad_maximum_fusion), channel_id=1, source_target_pairs={{0,16},{1,17},{2,18},{3,19},{4,20},{5,21},{6,22},{7,23},{8,24},{9,... | collective-permute-start | bytes 589832 | tf_op jit(solution)/shard_map/ppermute | solution.py:30
  72.4 11.7 %collective-permute-start.9 = (f32[32,1536]{1,0:T(8,128)S(1)}, f32[32,1536]{1,0:T(8,128)S(1)}, u32[]{:S(2)}, u32[]{:S(2)}) collective-permute-start(f32[32,1536]{1,0:T(8,128)S(1)} %pad_maximum_fusion.2), channel_id=1, source_target_pairs={{0,24},{1,25},{2,26},{3,27},{4,28},{5,29},{6,30},{7,31},{8,16},{9,... | collective-permute-start | bytes 589832 | tf_op jit(solution)/shard_map/ppermute | solution.py:30
  74.2 9.8 %collective-permute-start.8 = (f32[32,1536]{1,0:T(8,128)S(1)}, f32[32,1536]{1,0:T(8,128)S(1)}, u32[]{:S(2)}, u32[]{:S(2)}) collective-permute-start(f32[32,1536]{1,0:T(8,128)S(1)} %pad_maximum_fusion.1), channel_id=1, source_target_pairs={{0,8},{1,9},{2,10},{3,11},{4,12},{5,13},{6,14},{7,15},{8,0},{9,1},... | collective-permute-start | bytes 589832 | tf_op jit(solution)/shard_map/ppermute | solution.py:30
  78.4 7.4 %collective-permute-start.12 = (f32[32,1536]{1,0:T(8,128)S(1)}, f32[32,1536]{1,0:T(8,128)S(1)}, u32[]{:S(2)}, u32[]{:S(2)}) collective-permute-start(f32[32,1536]{1,0:T(8,128)S(1)} %pad_maximum_fusion.3), channel_id=1, source_target_pairs={{0,4},{1,5},{2,6},{3,7},{4,0},{5,1},{6,2},{7,3},{8,12},{9,13},{10,... | collective-permute-start | bytes 589832 | tf_op jit(solution)/shard_map/ppermute | solution.py:30
  78.5 9.2 %collective-permute-start.14 = (f32[32,1536]{1,0:T(8,128)S(1)}, f32[32,1536]{1,0:T(8,128)S(1)}, u32[]{:S(2)}, u32[]{:S(2)}) collective-permute-start(f32[32,1536]{1,0:T(8,128)S(1)} %pad_maximum_fusion.5), channel_id=1, source_target_pairs={{0,6},{1,7},{2,4},{3,5},{4,2},{5,3},{6,0},{7,1},{8,14},{9,15},{10,... | collective-permute-start | bytes 589832 | tf_op jit(solution)/shard_map/ppermute | solution.py:30
  82.3 5.7 %collective-permute-start.13 = (f32[32,1536]{1,0:T(8,128)S(1)}, f32[32,1536]{1,0:T(8,128)S(1)}, u32[]{:S(2)}, u32[]{:S(2)}) collective-permute-start(f32[32,1536]{1,0:T(8,128)S(1)} %pad_maximum_fusion.4), channel_id=1, source_target_pairs={{0,2},{1,3},{2,0},{3,1},{4,6},{5,7},{6,4},{7,5},{8,10},{9,11},{10,... | collective-permute-start | bytes 589832 | tf_op jit(solution)/shard_map/ppermute | solution.py:30
  88.2 5.8 %collective-permute-start.15 = (f32[32,1536]{1,0:T(8,128)S(1)}, f32[32,1536]{1,0:T(8,128)S(1)}, u32[]{:S(2)}, u32[]{:S(2)}) collective-permute-start(f32[32,1536]{1,0:T(8,128)S(1)} %constant_dynamic-slice_fusion.3), channel_id=1, source_target_pairs={{0,32},{1,33},{2,34},{3,35},{4,36},{5,37},{6,38},{7,39},{8,40},{9,... | collective-permute-start | bytes 589832 | tf_op jit(solution)/shard_map/ppermute | solution.py:30
  94.2 9.9 %collective-permute-start.16 = (f32[32,384]{1,0:T(8,128)S(1)}, f32[32,384]{1,0:T(8,128)S(1)}, u32[]{:S(2)}, u32[]{:S(2)}) collective-permute-start(f32[32,384]{1,0:T(8,128)S(1)} %get-tuple-element.77), channel_id=1, source_target_pairs={{0,128},{1,129},{2,130},{3,131},{4,132},{5,133},{6,134},{7,135},{8... | collective-permute-start | bytes 147464 | tf_op jit(solution)/shard_map/ppermute | solution.py:30
  102.0 6.2 %collective-permute-start.18 = (f32[32,384]{1,0:T(8,128)S(1)}, f32[32,384]{1,0:T(8,128)S(1)}, u32[]{:S(2)}, u32[]{:S(2)}) collective-permute-start(f32[32,384]{1,0:T(8,128)S(1)} %get-tuple-element.78), channel_id=1, source_target_pairs={{0,192},{1,193},{2,194},{3,195},{4,196},{5,197},{6,198},{7,199},{8... | collective-permute-start | bytes 147464 | tf_op jit(solution)/shard_map/ppermute | solution.py:30
  102.0 6.2 %collective-permute-start.17 = (f32[32,384]{1,0:T(8,128)S(1)}, f32[32,384]{1,0:T(8,128)S(1)}, u32[]{:S(2)}, u32[]{:S(2)}) collective-permute-start(f32[32,384]{1,0:T(8,128)S(1)} %get-tuple-element.79), channel_id=1, source_target_pairs={{0,64},{1,65},{2,66},{3,67},{4,68},{5,69},{6,70},{7,71},{8,72},{9,... | collective-permute-start | bytes 147464 | tf_op jit(solution)/shard_map/ppermute | solution.py:30

commit v7 on v6

--- a/solution.py
+++ b/solution.py
@@ -62,7 +62,7 @@
 def multiply(group, half, other, hi_ref, lo_ref, b):
     blocks = (NEAR_FIRST, FAR_FIRST)[group % 2]
     order = [(outer, inner) for outer in blocks[2 * half : 2 * half + 2] for inner in SECOND]
-    order = [qy * 4 + qx if group < 2 else qx * 4 + qy for qx, qy in order]
+    order = [qx * 4 + qy if group < 2 else qy * 4 + qx for qx, qy in order]
     depth = pl.ds(other * DEPTH, DEPTH)
     a_hi, a_lo = (
         jnp.concatenate([ref[q * ROWS : (q + 1) * ROWS, depth] for q in order], 0)
@@ -145,13 +145,13 @@
         for group in range(GROUPS):
             keep = parts[group] if last is None else after(parts[group], last)
             mask = ((1, 3), (3, 1))[group % 2][step]
-            last = keep + exchange(sends[group], "xxyy"[group], mask)
+            last = keep + exchange(sends[group], "yyxx"[group], mask)
             if step == 0:
                 sends[group], parts[group] = last[: 4 * ROWS], last[4 * ROWS :]
             else:
                 parts[group] = last
     pairs = []
-    for first, axis in ((0, "y"), (2, "x")):
+    for first, axis in ((0, "x"), (2, "y")):
         pair = [
             jnp.concatenate([part[i * ROWS : (i + 1) * ROWS] for part in parts[first : first + 2]], 1)
             for i in range(4)

time: 109 us -> 109 us (level); the launches traced: 109 us -> 108 us
  waiting for transfers between devices: 28.9 us -> 27.5 us
    ppermute x19, waiting for transfers between devices: 28.9 us -> 27.5 us  [exchange(): return lax.ppermute(value, AXES, flip(axis, mask))]
where the time goes in v7:
time: 109 us; the launch traced here: 108 us
  blocking collectives  35.3 us (32%)
  starting transfers between devices  28.6 us (26%)
  waiting for transfers between devices  27.5 us (25%)
  Pallas kernels  12.1 us (11%)
  local copies, waits for them, and re-layouts  2.2 us (2%)
  other arithmetic  1.69 us (2%)
    all_to_all x1, blocking collectives, body(): mine = lax.all_to_all(laid, ('y', 'x'), split_axis=0, concat_axis=0)  35.3 us
    ppermute x19, starting transfers between devices, exchange(): return lax.ppermute(value, AXES, flip(axis, mask))  28.6 us
    ppermute x19, waiting for transfers between devices, exchange(): return lax.ppermute(value, AXES, flip(axis, mask))  27.5 us
    pallas_call x4, Pallas kernels, products(): keeps += call(kernel, (out,), [VMEM] * 4, 6)(hi, lo, own, oth)  5.86 us
    pallas_call x1, Pallas kernels, products(): call(first_kernel, (out,) * 2 + (part, part), [smem, VMEM, VMEM, VMEM], 6)  3.39 us
    pallas_call x1, Pallas kernels, products(): sends += call(later, (out,) * 2, [VMEM] * 4, 6)(hi, lo, own, oth)  2.73 us
  transfers between devices with their start and end apart: 19, of which 11 were waited for; matrix products, arithmetic and copies ran while one was open for 1% of the time, Pallas kernels for 8%

profile of v7, /device:TPU:2, one launch (start us, length us, event | category | flops | bytes accessed | tf_op | source)
XLA Modules:
  0.0 107.7 jit_solution(7186001141930518045)
XLA Ops:
  0.0 0.1 pad_add_fusion.where
  0.1 1.6 %copy-done.1 = f32[32,16384]{1,0:T(8,128)S(1)} copy-done((f32[32,16384]{1,0:T(8,128)S(1)}, f32[32,16384]{1,0:T(8,128)}, u32[]{:S(2)}) %copy-start.1) | copy-done | bytes 2097176
  1.7 0.1 shard_map.28
  1.9 35.3 %all_to_all.5 = f32[16,32,1024]{2,1,0:T(8,128)S(1)} all-to-all(f32[16,32,1024]{2,1,0:T(8,128)S(1)} %shard_map.28), channel_id=1, replica_groups=mesh['z'=8,'y'=4,'x'=4,'core'=2] {'y','x'}, dimensions={0} | all-to-all | bytes 4194304 | tf_op jit(solution)/shard_map/all_to_all | solution.py:139
  37.2 3.4 %shard_map.29 = (f32[256,768]{1,0:T(8,128)S(1)}, f32[256,768]{1,0:T(8,128)S(1)}, bf16[512,1024]{1,0:T(8,128)(2,1)S(1)}, bf16[512,1024]{1,0:T(8,128)(2,1)S(1)}) custom-call(s32[3]{0:T(128)S(1)} %pad_add_fusion.where, f32[512,1024]{1,0:T(8,128)S(1)} %bitcast.4, f32[512,3072]{1,0:T(8,128)S(1)} %copy-done, f32[512,3072]{1,0:T(8,128)S(1)} %collective-permute-done.oth_ref.refs_3_), custom_call_target="tpu_custom_call" | custom-call | flops 1048576 | bytes 65536 | tf_op jit(solution)/shard_map/pallas_call | solution.py:116
  40.6 0.1 collective-permute-start.1
  40.7 1.4 %collective-permute-start.2 = (f32[256,768]{1,0:T(8,128)S(1)}, f32[256,768]{1,0:T(8,128)S(1)}, u32[]{:S(2)}, u32[]{:S(2)}) collective-permute-start(f32[256,768]{1,0:T(8,128)S(1)} %get-tuple-element.39), channel_id=1, source_target_pairs={{0,24},{1,25},{2,26},{3,27},{4,28},{5,29},{6,30},{7,31},{8,16},{9,... | collective-permute-start | bytes 2359304 | tf_op jit(solution)/shard_map/ppermute | solution.py:30
  42.1 2.7 %shard_map.30 = (f32[256,768]{1,0:T(8,128)S(1)}, f32[256,768]{1,0:T(8,128)S(1)}) custom-call(bf16[512,1024]{1,0:T(8,128)(2,1)S(1)} %get-tuple-element.35.refs_0_, bf16[512,1024]{1,0:T(8,128)(2,1)S(1)} %get-tuple-element.33.refs_1_, f32[512,3072]{1,0:T(8,128)S(1)} %copy-done, f32[512,3072]{1,0:T(8,128)S(1)} %collective-permute-done.oth_ref.refs_3_), custom_call_target="tpu_custom_call" | custom-call | flops 1048576 | bytes 65536 | tf_op jit(solution)/shard_map/pallas_call | solution.py:120
  44.8 1.6 %collective-permute-start.3 = (f32[256,768]{1,0:T(8,128)S(1)}, f32[256,768]{1,0:T(8,128)S(1)}, u32[]{:S(2)}, u32[]{:S(2)}) collective-permute-start(f32[256,768]{1,0:T(8,128)S(1)} %get-tuple-element.41), channel_id=1, source_target_pairs={{0,2},{1,3},{2,0},{3,1},{4,6},{5,7},{6,4},{7,5},{8,10},{9,11},{10,... | collective-permute-start | bytes 2359304 | tf_op jit(solution)/shard_map/ppermute | solution.py:30
  46.4 0.6 collective-permute-start.4
  47.0 1.5 %shard_map.34 = f32[256,768]{1,0:T(8,128)S(1)} custom-call(bf16[512,1024]{1,0:T(8,128)(2,1)S(1)} %get-tuple-element.35.refs_0_, bf16[512,1024]{1,0:T(8,128)(2,1)S(1)} %get-tuple-element.33.refs_1_, f32[512,3072]{1,0:T(8,128)S(1)} %copy-done, f32[512,3072]{1,0:T(8,128)S(1)} %collective-permute-done.oth_ref.refs_3_), custom_call_target="tpu_custom_call" | custom-call | flops 1048576 | bytes 65536 | tf_op jit(solution)/shard_map/pallas_call | solution.py:125
  48.4 1.5 %shard_map.33 = f32[256,768]{1,0:T(8,128)S(1)} custom-call(bf16[512,1024]{1,0:T(8,128)(2,1)S(1)} %get-tuple-element.35.refs_0_, bf16[512,1024]{1,0:T(8,128)(2,1)S(1)} %get-tuple-element.33.refs_1_, f32[512,3072]{1,0:T(8,128)S(1)} %copy-done, f32[512,3072]{1,0:T(8,128)S(1)} %collective-permute-done.oth_ref.refs_3_), custom_call_target="tpu_custom_call" | custom-call | flops 1048576 | bytes 65536 | tf_op jit(solution)/shard_map/pallas_call | solution.py:125
  49.9 1.5 %shard_map.32 = f32[256,768]{1,0:T(8,128)S(1)} custom-call(bf16[512,1024]{1,0:T(8,128)(2,1)S(1)} %get-tuple-element.35.refs_0_, bf16[512,1024]{1,0:T(8,128)(2,1)S(1)} %get-tuple-element.33.refs_1_, f32[512,3072]{1,0:T(8,128)S(1)} %copy-done, f32[512,3072]{1,0:T(8,128)S(1)} %collective-permute-done.oth_ref.refs_3_), custom_call_target="tpu_custom_call" | custom-call | flops 1048576 | bytes 65536 | tf_op jit(solution)/shard_map/pallas_call | solution.py:125
  51.4 1.5 %shard_map.31 = f32[256,768]{1,0:T(8,128)S(1)} custom-call(bf16[512,1024]{1,0:T(8,128)(2,1)S(1)} %get-tuple-element.35.refs_0_, bf16[512,1024]{1,0:T(8,128)(2,1)S(1)} %get-tuple-element.33.refs_1_, f32[512,3072]{1,0:T(8,128)S(1)} %copy-done, f32[512,3072]{1,0:T(8,128)S(1)} %collective-permute-done.oth_ref.refs_3_), custom_call_target="tpu_custom_call" | custom-call | flops 1048576 | bytes 65536 | tf_op jit(solution)/shard_map/pallas_call | solution.py:125
  52.9 6.4 %collective-permute-done.1 = f32[256,768]{1,0:T(8,128)S(1)} collective-permute-done((f32[256,768]{1,0:T(8,128)S(1)}, f32[256,768]{1,0:T(8,128)S(1)}, u32[]{:S(2)}, u32[]{:S(2)}) %collective-permute-start.1) | collective-permute-done | bytes 786464 | tf_op jit(solution)/shard_map/ppermute | solution.py:30
  59.2 0.1 add.54
  59.3 1.2 %collective-permute-done.2 = f32[256,768]{1,0:T(8,128)S(1)} collective-permute-done((f32[256,768]{1,0:T(8,128)S(1)}, f32[256,768]{1,0:T(8,128)S(1)}, u32[]{:S(2)}, u32[]{:S(2)}) %collective-permute-start.2) | collective-permute-done | bytes 786464 | tf_op jit(solution)/shard_map/ppermute | solution.py:30
  60.5 0.1 add.55
  60.6 0.1 fusion.2
  60.7 0.5 collective-permute-start.6
  61.3 1.0 collective-permute-start.5
  62.3 0.6 collective-permute-done.3
  62.9 0.1 add.56
  63.1 1.2 %collective-permute-start.10 = (f32[128,768]{1,0:T(8,128)S(1)}, f32[128,768]{1,0:T(8,128)S(1)}, u32[]{:S(2)}, u32[]{:S(2)}) collective-permute-start(f32[128,768]{1,0:T(8,128)S(1)} %get-tuple-element.55), channel_id=1, source_target_pairs={{0,6},{1,7},{2,4},{3,5},{4,2},{5,3},{6,0},{7,1},{8,14},{9,15},{10,... | collective-permute-start | bytes 1179656 | tf_op jit(solution)/shard_map/ppermute | solution.py:30
  64.3 0.4 collective-permute-done.4
  64.7 0.1 add.57
  64.9 1.2 %collective-permute-start.11 = (f32[128,768]{1,0:T(8,128)S(1)}, f32[128,768]{1,0:T(8,128)S(1)}, u32[]{:S(2)}, u32[]{:S(2)}) collective-permute-start(f32[128,768]{1,0:T(8,128)S(1)} %get-tuple-element.53), channel_id=1, source_target_pairs={{0,2},{1,3},{2,0},{3,1},{4,6},{5,7},{6,4},{7,5},{8,10},{9,11},{10,... | collective-permute-start | bytes 1179656 | tf_op jit(solution)/shard_map/ppermute | solution.py:30
  66.1 5.2 %collective-permute-done.5 = f32[128,768]{1,0:T(8,128)S(1)} collective-permute-done((f32[128,768]{1,0:T(8,128)S(1)}, f32[128,768]{1,0:T(8,128)S(1)}, u32[]{:S(2)}, u32[]{:S(2)}) %collective-permute-start.5) | collective-permute-done | bytes 393248 | tf_op jit(solution)/shard_map/ppermute | solution.py:30
  71.6 1.4 %collective-permute-start.7 = (f32[32,1536]{1,0:T(8,128)S(1)}, f32[32,1536]{1,0:T(8,128)S(1)}, u32[]{:S(2)}, u32[]{:S(2)}) collective-permute-start(f32[32,1536]{1,0:T(8,128)S(1)} %pad_maximum_fusion), channel_id=1, source_target_pairs={{0,4},{1,5},{2,6},{3,7},{4,0},{5,1},{6,2},{7,3},{8,12},{9,13},{10,... | collective-permute-start | bytes 589832 | tf_op jit(solution)/shard_map/ppermute | solution.py:30
  73.0 1.7 %collective-permute-start.9 = (f32[32,1536]{1,0:T(8,128)S(1)}, f32[32,1536]{1,0:T(8,128)S(1)}, u32[]{:S(2)}, u32[]{:S(2)}) collective-permute-start(f32[32,1536]{1,0:T(8,128)S(1)} %pad_maximum_fusion.2), channel_id=1, source_target_pairs={{0,6},{1,7},{2,4},{3,5},{4,2},{5,3},{6,0},{7,1},{8,14},{9,15},{10,... | collective-permute-start | bytes 589832 | tf_op jit(solution)/shard_map/ppermute | solution.py:30
  74.7 1.9 %collective-permute-start.8 = (f32[32,1536]{1,0:T(8,128)S(1)}, f32[32,1536]{1,0:T(8,128)S(1)}, u32[]{:S(2)}, u32[]{:S(2)}) collective-permute-start(f32[32,1536]{1,0:T(8,128)S(1)} %pad_maximum_fusion.1), channel_id=1, source_target_pairs={{0,2},{1,3},{2,0},{3,1},{4,6},{5,7},{6,4},{7,5},{8,10},{9,11},{10,... | collective-permute-start | bytes 589832 | tf_op jit(solution)/shard_map/ppermute | solution.py:30
  76.8 2.9 %collective-permute-start.12 = (f32[32,1536]{1,0:T(8,128)S(1)}, f32[32,1536]{1,0:T(8,128)S(1)}, u32[]{:S(2)}, u32[]{:S(2)}) collective-permute-start(f32[32,1536]{1,0:T(8,128)S(1)} %pad_maximum_fusion.3), channel_id=1, source_target_pairs={{0,16},{1,17},{2,18},{3,19},{4,20},{5,21},{6,22},{7,23},{8,24},{9,... | collective-permute-start | bytes 589832 | tf_op jit(solution)/shard_map/ppermute | solution.py:30
  79.7 0.4 collective-permute-start.14
  80.2 0.9 collective-permute-start.13
  81.1 1.3 %collective-permute-done.8 = f32[32,1536]{1,0:T(8,128)S(1)} collective-permute-done((f32[32,1536]{1,0:T(8,128)S(1)}, f32[32,1536]{1,0:T(8,128)S(1)}, u32[]{:S(2)}, u32[]{:S(2)}) %collective-permute-start.8) | collective-permute-done | bytes 196640 | tf_op jit(solution)/shard_map/ppermute | solution.py:30
  82.4 1.6 %collective-permute-done.12 = f32[32,1536]{1,0:T(8,128)S(1)} collective-permute-done((f32[32,1536]{1,0:T(8,128)S(1)}, f32[32,1536]{1,0:T(8,128)S(1)}, u32[]{:S(2)}, u32[]{:S(2)}) %collective-permute-start.12) | collective-permute-done | bytes 196640 | tf_op jit(solution)/shard_map/ppermute | solution.py:30
  84.0 2.7 %collective-permute-done.14 = f32[32,1536]{1,0:T(8,128)S(1)} collective-permute-done((f32[32,1536]{1,0:T(8,128)S(1)}, f32[32,1536]{1,0:T(8,128)S(1)}, u32[]{:S(2)}, u32[]{:S(2)}) %collective-permute-start.14) | collective-permute-done | bytes 196640 | tf_op jit(solution)/shard_map/ppermute | solution.py:30
  86.7 0.1 maximum_add_fusion.1
  86.8 0.1 constant_dynamic-slice_fusion.3
  87.0 2.0 %collective-permute-start.15 = (f32[32,1536]{1,0:T(8,128)S(1)}, f32[32,1536]{1,0:T(8,128)S(1)}, u32[]{:S(2)}, u32[]{:S(2)}) collective-permute-start(f32[32,1536]{1,0:T(8,128)S(1)} %constant_dynamic-slice_fusion.3), channel_id=1, source_target_pairs={{0,32},{1,33},{2,34},{3,35},{4,36},{5,37},{6,38},{7,39},{8,40},{9,... | collective-permute-start | bytes 589832 | tf_op jit(solution)/shard_map/ppermute | solution.py:30
  89.0 3.8 %collective-permute-done.15 = f32[32,1536]{1,0:T(8,128)S(1)} collective-permute-done((f32[32,1536]{1,0:T(8,128)S(1)}, f32[32,1536]{1,0:T(8,128)S(1)}, u32[]{:S(2)}, u32[]{:S(2)}) %collective-permute-start.15) | collective-permute-done | bytes 196640 | tf_op jit(solution)/shard_map/ppermute | solution.py:30
  92.7 0.1 dynamic-slice_add_fusion
  92.8 0.1 constant_dynamic-slice_fusion.2
  93.0 7.8 %collective-permute-start.16 = (f32[32,384]{1,0:T(8,128)S(1)}, f32[32,384]{1,0:T(8,128)S(1)}, u32[]{:S(2)}, u32[]{:S(2)}) collective-permute-start(f32[32,384]{1,0:T(8,128)S(1)} %get-tuple-element.77), channel_id=1, source_target_pairs={{0,128},{1,129},{2,130},{3,131},{4,132},{5,133},{6,134},{7,135},{8... | collective-permute-start | bytes 147464 | tf_op jit(solution)/shard_map/ppermute | solution.py:30
  100.8 2.0 %collective-permute-start.17 = (f32[32,384]{1,0:T(8,128)S(1)}, f32[32,384]{1,0:T(8,128)S(1)}, u32[]{:S(2)}, u32[]{:S(2)}) collective-permute-start(f32[32,384]{1,0:T(8,128)S(1)} %get-tuple-element.79), channel_id=1, source_target_pairs={{0,64},{1,65},{2,66},{3,67},{4,68},{5,69},{6,70},{7,71},{8,72},{9,... | collective-permute-start | bytes 147464 | tf_op jit(solution)/shard_map/ppermute | solution.py:30
  102.8 0.2 collective-permute-done.16
  102.9 4.1 %collective-permute-done.18 = f32[32,384]{1,0:T(8,128)S(1)} collective-permute-done((f32[32,384]{1,0:T(8,128)S(1)}, f32[32,384]{1,0:T(8,128)S(1)}, u32[]{:S(2)}, u32[]{:S(2)}) %collective-permute-start.18) | collective-permute-done | bytes 49184 | tf_op jit(solution)/shard_map/ppermute | solution.py:30
  107.0 0.7 add_multiply_fusion
  (39 shorter events, 0.7 us)
Async XLA Ops:
  0.1 37.1 %collective-permute-start = (f32[512,3072]{1,0:T(8,128)}, f32[512,3072]{1,0:T(8,128)S(1)}, u32[]{:S(2)}, u32[]{:S(2)}) collective-permute-start(f32[512,3072]{1,0:T(8,128)} %refs_2_.4), channel_id=1, source_target_pairs={{0,1},{1,0},{2,3},{3,2},{4,5},{5,4},{6,7},{7,6},{8,9},{9,8},{10,11... | collective-permute-start | bytes 18874376 | tf_op jit(solution)/shard_map/ppermute | solution.py:30
  0.1 1.6 %copy-start.1 = (f32[32,16384]{1,0:T(8,128)S(1)}, f32[32,16384]{1,0:T(8,128)}, u32[]{:S(2)}) copy-start(f32[32,16384]{1,0:T(8,128)} %a_ref) | copy-start | bytes 6291460
  1.7 35.5 %copy-start = (f32[512,3072]{1,0:T(8,128)S(1)}, f32[512,3072]{1,0:T(8,128)}, u32[]{:S(2)}) copy-start(f32[512,3072]{1,0:T(8,128)} %refs_2_.4) | copy-start | bytes 18874372
  40.6 18.6 %collective-permute-start.1 = (f32[256,768]{1,0:T(8,128)S(1)}, f32[256,768]{1,0:T(8,128)S(1)}, u32[]{:S(2)}, u32[]{:S(2)}) collective-permute-start(f32[256,768]{1,0:T(8,128)S(1)} %get-tuple-element.37), channel_id=1, source_target_pairs={{0,8},{1,9},{2,10},{3,11},{4,12},{5,13},{6,14},{7,15},{8,0},{9,1},... | collective-permute-start | bytes 2359304 | tf_op jit(solution)/shard_map/ppermute | solution.py:30
  40.7 19.8 %collective-permute-start.2 = (f32[256,768]{1,0:T(8,128)S(1)}, f32[256,768]{1,0:T(8,128)S(1)}, u32[]{:S(2)}, u32[]{:S(2)}) collective-permute-start(f32[256,768]{1,0:T(8,128)S(1)} %get-tuple-element.39), channel_id=1, source_target_pairs={{0,24},{1,25},{2,26},{3,27},{4,28},{5,29},{6,30},{7,31},{8,16},{9,... | collective-permute-start | bytes 2359304 | tf_op jit(solution)/shard_map/ppermute | solution.py:30
  44.8 18.1 %collective-permute-start.3 = (f32[256,768]{1,0:T(8,128)S(1)}, f32[256,768]{1,0:T(8,128)S(1)}, u32[]{:S(2)}, u32[]{:S(2)}) collective-permute-start(f32[256,768]{1,0:T(8,128)S(1)} %get-tuple-element.41), channel_id=1, source_target_pairs={{0,2},{1,3},{2,0},{3,1},{4,6},{5,7},{6,4},{7,5},{8,10},{9,11},{10,... | collective-permute-start | bytes 2359304 | tf_op jit(solution)/shard_map/ppermute | solution.py:30
  46.4 18.3 %collective-permute-start.4 = (f32[256,768]{1,0:T(8,128)S(1)}, f32[256,768]{1,0:T(8,128)S(1)}, u32[]{:S(2)}, u32[]{:S(2)}) collective-permute-start(f32[256,768]{1,0:T(8,128)S(1)} %get-tuple-element.34), channel_id=1, source_target_pairs={{0,6},{1,7},{2,4},{3,5},{4,2},{5,3},{6,0},{7,1},{8,14},{9,15},{10,... | collective-permute-start | bytes 2359304 | tf_op jit(solution)/shard_map/ppermute | solution.py:30
  60.7 10.7 %collective-permute-start.6 = (f32[128,768]{1,0:T(8,128)S(1)}, f32[128,768]{1,0:T(8,128)S(1)}, u32[]{:S(2)}, u32[]{:S(2)}) collective-permute-start(f32[128,768]{1,0:T(8,128)S(1)} %get-tuple-element.57), channel_id=1, source_target_pairs={{0,8},{1,9},{2,10},{3,11},{4,12},{5,13},{6,14},{7,15},{8,0},{9,1},... | collective-permute-start | bytes 1179656 | tf_op jit(solution)/shard_map/ppermute | solution.py:30
  61.3 10.1 %collective-permute-start.5 = (f32[128,768]{1,0:T(8,128)S(1)}, f32[128,768]{1,0:T(8,128)S(1)}, u32[]{:S(2)}, u32[]{:S(2)}) collective-permute-start(f32[128,768]{1,0:T(8,128)S(1)} %get-tuple-element.59), channel_id=1, source_target_pairs={{0,24},{1,25},{2,26},{3,27},{4,28},{5,29},{6,30},{7,31},{8,16},{9,... | collective-permute-start | bytes 1179656 | tf_op jit(solution)/shard_map/ppermute | solution.py:30
  63.1 13.5 %collective-permute-start.10 = (f32[128,768]{1,0:T(8,128)S(1)}, f32[128,768]{1,0:T(8,128)S(1)}, u32[]{:S(2)}, u32[]{:S(2)}) collective-permute-start(f32[128,768]{1,0:T(8,128)S(1)} %get-tuple-element.55), channel_id=1, source_target_pairs={{0,6},{1,7},{2,4},{3,5},{4,2},{5,3},{6,0},{7,1},{8,14},{9,15},{10,... | collective-permute-start | bytes 1179656 | tf_op jit(solution)/shard_map/ppermute | solution.py:30
  64.9 11.7 %collective-permute-start.11 = (f32[128,768]{1,0:T(8,128)S(1)}, f32[128,768]{1,0:T(8,128)S(1)}, u32[]{:S(2)}, u32[]{:S(2)}) collective-permute-start(f32[128,768]{1,0:T(8,128)S(1)} %get-tuple-element.53), channel_id=1, source_target_pairs={{0,2},{1,3},{2,0},{3,1},{4,6},{5,7},{6,4},{7,5},{8,10},{9,11},{10,... | collective-permute-start | bytes 1179656 | tf_op jit(solution)/shard_map/ppermute | solution.py:30
  71.6 8.6 %collective-permute-start.7 = (f32[32,1536]{1,0:T(8,128)S(1)}, f32[32,1536]{1,0:T(8,128)S(1)}, u32[]{:S(2)}, u32[]{:S(2)}) collective-permute-start(f32[32,1536]{1,0:T(8,128)S(1)} %pad_maximum_fusion), channel_id=1, source_target_pairs={{0,4},{1,5},{2,6},{3,7},{4,0},{5,1},{6,2},{7,3},{8,12},{9,13},{10,... | collective-permute-start | bytes 589832 | tf_op jit(solution)/shard_map/ppermute | solution.py:30
  73.0 8.1 %collective-permute-start.9 = (f32[32,1536]{1,0:T(8,128)S(1)}, f32[32,1536]{1,0:T(8,128)S(1)}, u32[]{:S(2)}, u32[]{:S(2)}) collective-permute-start(f32[32,1536]{1,0:T(8,128)S(1)} %pad_maximum_fusion.2), channel_id=1, source_target_pairs={{0,6},{1,7},{2,4},{3,5},{4,2},{5,3},{6,0},{7,1},{8,14},{9,15},{10,... | collective-permute-start | bytes 589832 | tf_op jit(solution)/shard_map/ppermute | solution.py:30
  74.7 7.6 %collective-permute-start.8 = (f32[32,1536]{1,0:T(8,128)S(1)}, f32[32,1536]{1,0:T(8,128)S(1)}, u32[]{:S(2)}, u32[]{:S(2)}) collective-permute-start(f32[32,1536]{1,0:T(8,128)S(1)} %pad_maximum_fusion.1), channel_id=1, source_target_pairs={{0,2},{1,3},{2,0},{3,1},{4,6},{5,7},{6,4},{7,5},{8,10},{9,11},{10,... | collective-permute-start | bytes 589832 | tf_op jit(solution)/shard_map/ppermute | solution.py:30
  76.8 7.3 %collective-permute-start.12 = (f32[32,1536]{1,0:T(8,128)S(1)}, f32[32,1536]{1,0:T(8,128)S(1)}, u32[]{:S(2)}, u32[]{:S(2)}) collective-permute-start(f32[32,1536]{1,0:T(8,128)S(1)} %pad_maximum_fusion.3), channel_id=1, source_target_pairs={{0,16},{1,17},{2,18},{3,19},{4,20},{5,21},{6,22},{7,23},{8,24},{9,... | collective-permute-start | bytes 589832 | tf_op jit(solution)/shard_map/ppermute | solution.py:30
  79.7 7.0 %collective-permute-start.14 = (f32[32,1536]{1,0:T(8,128)S(1)}, f32[32,1536]{1,0:T(8,128)S(1)}, u32[]{:S(2)}, u32[]{:S(2)}) collective-permute-start(f32[32,1536]{1,0:T(8,128)S(1)} %pad_maximum_fusion.5), channel_id=1, source_target_pairs={{0,24},{1,25},{2,26},{3,27},{4,28},{5,29},{6,30},{7,31},{8,16},{9,... | collective-permute-start | bytes 589832 | tf_op jit(solution)/shard_map/ppermute | solution.py:30
  80.2 6.5 %collective-permute-start.13 = (f32[32,1536]{1,0:T(8,128)S(1)}, f32[32,1536]{1,0:T(8,128)S(1)}, u32[]{:S(2)}, u32[]{:S(2)}) collective-permute-start(f32[32,1536]{1,0:T(8,128)S(1)} %pad_maximum_fusion.4), channel_id=1, source_target_pairs={{0,8},{1,9},{2,10},{3,11},{4,12},{5,13},{6,14},{7,15},{8,0},{9,1},... | collective-permute-start | bytes 589832 | tf_op jit(solution)/shard_map/ppermute | solution.py:30
  87.0 5.8 %collective-permute-start.15 = (f32[32,1536]{1,0:T(8,128)S(1)}, f32[32,1536]{1,0:T(8,128)S(1)}, u32[]{:S(2)}, u32[]{:S(2)}) collective-permute-start(f32[32,1536]{1,0:T(8,128)S(1)} %constant_dynamic-slice_fusion.3), channel_id=1, source_target_pairs={{0,32},{1,33},{2,34},{3,35},{4,36},{5,37},{6,38},{7,39},{8,40},{9,... | collective-permute-start | bytes 589832 | tf_op jit(solution)/shard_map/ppermute | solution.py:30
  93.0 10.0 %collective-permute-start.16 = (f32[32,384]{1,0:T(8,128)S(1)}, f32[32,384]{1,0:T(8,128)S(1)}, u32[]{:S(2)}, u32[]{:S(2)}) collective-permute-start(f32[32,384]{1,0:T(8,128)S(1)} %get-tuple-element.77), channel_id=1, source_target_pairs={{0,128},{1,129},{2,130},{3,131},{4,132},{5,133},{6,134},{7,135},{8... | collective-permute-start | bytes 147464 | tf_op jit(solution)/shard_map/ppermute | solution.py:30
  100.8 6.2 %collective-permute-start.18 = (f32[32,384]{1,0:T(8,128)S(1)}, f32[32,384]{1,0:T(8,128)S(1)}, u32[]{:S(2)}, u32[]{:S(2)}) collective-permute-start(f32[32,384]{1,0:T(8,128)S(1)} %get-tuple-element.78), channel_id=1, source_target_pairs={{0,192},{1,193},{2,194},{3,195},{4,196},{5,197},{6,198},{7,199},{8... | collective-permute-start | bytes 147464 | tf_op jit(solution)/shard_map/ppermute | solution.py:30
  100.8 6.2 %collective-permute-start.17 = (f32[32,384]{1,0:T(8,128)S(1)}, f32[32,384]{1,0:T(8,128)S(1)}, u32[]{:S(2)}, u32[]{:S(2)}) collective-permute-start(f32[32,384]{1,0:T(8,128)S(1)} %get-tuple-element.79), channel_id=1, source_target_pairs={{0,64},{1,65},{2,66},{3,67},{4,68},{5,69},{6,70},{7,71},{8,72},{9,... | collective-permute-start | bytes 147464 | tf_op jit(solution)/shard_map/ppermute | solution.py:30

commit v8 on v6

--- a/solution.py
+++ b/solution.py
@@ -163,7 +163,7 @@
     keep, send = (cut(both, start, 4 * WIDTH) for start in halves)
     keep = keep + exchange(send, "z", 1)
     block = lambda v: cut(keep, blocks[v], WIDTH)
-    far = [exchange(block(v), "z", 2 * v) for v in (2, 1, 3)]
+    far = [exchange(block(v), "z", 2 * v) for v in (2, 3, 1)]
     return 0.5 * (block(0) + far[0] + far[1] + far[2])
 
 

time: 109 us -> 111 us (1.018)
  transfers between devices with their start and end apart: 19 -> 19, of which waited for: 11 -> 12; matrix products, arithmetic and copies ran while one was open for 1% -> 1% of each run, Pallas kernels for 8% -> 8%
where the time goes in v8:
time: 111 us
  blocking collectives  35.3 us (32%)
  waiting for transfers between devices  29.8 us (27%)
  starting transfers between devices  29.4 us (26%)
  Pallas kernels  12.1 us (11%)
  local copies, waits for them, and re-layouts  2.2 us (2%)
  other arithmetic  1.69 us (2%)
    all_to_all x1, blocking collectives, body(): mine = lax.all_to_all(laid, ('y', 'x'), split_axis=0, concat_axis=0)  35.3 us
    ppermute x19, waiting for transfers between devices, exchange(): return lax.ppermute(value, AXES, flip(axis, mask))  29.8 us
    ppermute x19, starting transfers between devices, exchange(): return lax.ppermute(value, AXES, flip(axis, mask))  29.4 us
    pallas_call x4, Pallas kernels, products(): keeps += call(kernel, (out,), [VMEM] * 4, 6)(hi, lo, own, oth)  5.86 us
    pallas_call x1, Pallas kernels, products(): call(first_kernel, (out,) * 2 + (part, part), [smem, VMEM, VMEM, VMEM], 6)  3.39 us
    pallas_call x1, Pallas kernels, products(): sends += call(later, (out,) * 2, [VMEM] * 4, 6)(hi, lo, own, oth)  2.73 us
  transfers between devices with their start and end apart: 19, of which 12 were waited for; matrix products, arithmetic and copies ran while one was open for 1% of the time, Pallas kernels for 8%

profile of v8, /device:TPU:2, one launch (start us, length us, event | category | flops | bytes accessed | tf_op | source)
XLA Modules:
  0.0 110.9 jit_solution(11580731735536099099)
XLA Ops:
  0.0 0.1 pad_add_fusion.where
  0.1 1.6 %copy-done.1 = f32[32,16384]{1,0:T(8,128)S(1)} copy-done((f32[32,16384]{1,0:T(8,128)S(1)}, f32[32,16384]{1,0:T(8,128)}, u32[]{:S(2)}) %copy-start.1) | copy-done | bytes 2097176
  1.7 0.1 shard_map.28
  1.9 35.3 %all_to_all.5 = f32[16,32,1024]{2,1,0:T(8,128)S(1)} all-to-all(f32[16,32,1024]{2,1,0:T(8,128)S(1)} %shard_map.28), channel_id=1, replica_groups=mesh['z'=8,'y'=4,'x'=4,'core'=2] {'y','x'}, dimensions={0} | all-to-all | bytes 4194304 | tf_op jit(solution)/shard_map/all_to_all | solution.py:139
  37.2 3.4 %shard_map.29 = (f32[256,768]{1,0:T(8,128)S(1)}, f32[256,768]{1,0:T(8,128)S(1)}, bf16[512,1024]{1,0:T(8,128)(2,1)S(1)}, bf16[512,1024]{1,0:T(8,128)(2,1)S(1)}) custom-call(s32[3]{0:T(128)S(1)} %pad_add_fusion.where, f32[512,1024]{1,0:T(8,128)S(1)} %bitcast.4, f32[512,3072]{1,0:T(8,128)S(1)} %copy-done, f32[512,3072]{1,0:T(8,128)S(1)} %collective-permute-done.oth_ref.refs_3_), custom_call_target="tpu_custom_call" | custom-call | flops 1048576 | bytes 65536 | tf_op jit(solution)/shard_map/pallas_call | solution.py:116
  40.6 1.5 %collective-permute-start.1 = (f32[256,768]{1,0:T(8,128)S(1)}, f32[256,768]{1,0:T(8,128)S(1)}, u32[]{:S(2)}, u32[]{:S(2)}) collective-permute-start(f32[256,768]{1,0:T(8,128)S(1)} %get-tuple-element.37), channel_id=1, source_target_pairs={{0,2},{1,3},{2,0},{3,1},{4,6},{5,7},{6,4},{7,5},{8,10},{9,11},{10,... | collective-permute-start | bytes 2359304 | tf_op jit(solution)/shard_map/ppermute | solution.py:30
  42.2 2.7 %shard_map.30 = (f32[256,768]{1,0:T(8,128)S(1)}, f32[256,768]{1,0:T(8,128)S(1)}) custom-call(bf16[512,1024]{1,0:T(8,128)(2,1)S(1)} %get-tuple-element.35.refs_0_, bf16[512,1024]{1,0:T(8,128)(2,1)S(1)} %get-tuple-element.33.refs_1_, f32[512,3072]{1,0:T(8,128)S(1)} %copy-done, f32[512,3072]{1,0:T(8,128)S(1)} %collective-permute-done.oth_ref.refs_3_), custom_call_target="tpu_custom_call" | custom-call | flops 1048576 | bytes 65536 | tf_op jit(solution)/shard_map/pallas_call | solution.py:120
  44.9 0.6 collective-permute-start.3
  45.5 1.4 %collective-permute-start.4 = (f32[256,768]{1,0:T(8,128)S(1)}, f32[256,768]{1,0:T(8,128)S(1)}, u32[]{:S(2)}, u32[]{:S(2)}) collective-permute-start(f32[256,768]{1,0:T(8,128)S(1)} %get-tuple-element.34), channel_id=1, source_target_pairs={{0,24},{1,25},{2,26},{3,27},{4,28},{5,29},{6,30},{7,31},{8,16},{9,... | collective-permute-start | bytes 2359304 | tf_op jit(solution)/shard_map/ppermute | solution.py:30
  47.0 1.5 %shard_map.34 = f32[256,768]{1,0:T(8,128)S(1)} custom-call(bf16[512,1024]{1,0:T(8,128)(2,1)S(1)} %get-tuple-element.35.refs_0_, bf16[512,1024]{1,0:T(8,128)(2,1)S(1)} %get-tuple-element.33.refs_1_, f32[512,3072]{1,0:T(8,128)S(1)} %copy-done, f32[512,3072]{1,0:T(8,128)S(1)} %collective-permute-done.oth_ref.refs_3_), custom_call_target="tpu_custom_call" | custom-call | flops 1048576 | bytes 65536 | tf_op jit(solution)/shard_map/pallas_call | solution.py:125
  48.4 1.5 %shard_map.33 = f32[256,768]{1,0:T(8,128)S(1)} custom-call(bf16[512,1024]{1,0:T(8,128)(2,1)S(1)} %get-tuple-element.35.refs_0_, bf16[512,1024]{1,0:T(8,128)(2,1)S(1)} %get-tuple-element.33.refs_1_, f32[512,3072]{1,0:T(8,128)S(1)} %copy-done, f32[512,3072]{1,0:T(8,128)S(1)} %collective-permute-done.oth_ref.refs_3_), custom_call_target="tpu_custom_call" | custom-call | flops 1048576 | bytes 65536 | tf_op jit(solution)/shard_map/pallas_call | solution.py:125
  49.9 1.5 %shard_map.32 = f32[256,768]{1,0:T(8,128)S(1)} custom-call(bf16[512,1024]{1,0:T(8,128)(2,1)S(1)} %get-tuple-element.35.refs_0_, bf16[512,1024]{1,0:T(8,128)(2,1)S(1)} %get-tuple-element.33.refs_1_, f32[512,3072]{1,0:T(8,128)S(1)} %copy-done, f32[512,3072]{1,0:T(8,128)S(1)} %collective-permute-done.oth_ref.refs_3_), custom_call_target="tpu_custom_call" | custom-call | flops 1048576 | bytes 65536 | tf_op jit(solution)/shard_map/pallas_call | solution.py:125
  51.4 1.5 %shard_map.31 = f32[256,768]{1,0:T(8,128)S(1)} custom-call(bf16[512,1024]{1,0:T(8,128)(2,1)S(1)} %get-tuple-element.35.refs_0_, bf16[512,1024]{1,0:T(8,128)(2,1)S(1)} %get-tuple-element.33.refs_1_, f32[512,3072]{1,0:T(8,128)S(1)} %copy-done, f32[512,3072]{1,0:T(8,128)S(1)} %collective-permute-done.oth_ref.refs_3_), custom_call_target="tpu_custom_call" | custom-call | flops 1048576 | bytes 65536 | tf_op jit(solution)/shard_map/pallas_call | solution.py:125
  52.9 6.4 %collective-permute-done.1 = f32[256,768]{1,0:T(8,128)S(1)} collective-permute-done((f32[256,768]{1,0:T(8,128)S(1)}, f32[256,768]{1,0:T(8,128)S(1)}, u32[]{:S(2)}, u32[]{:S(2)}) %collective-permute-start.1) | collective-permute-done | bytes 786464 | tf_op jit(solution)/shard_map/ppermute | solution.py:30
  59.2 0.1 add.54
  59.3 1.1 collective-permute-done.2
  60.4 0.1 add.55
  60.5 0.1 fusion.2
  60.6 1.9 %collective-permute-start.6 = (f32[128,768]{1,0:T(8,128)S(1)}, f32[128,768]{1,0:T(8,128)S(1)}, u32[]{:S(2)}, u32[]{:S(2)}) collective-permute-start(f32[128,768]{1,0:T(8,128)S(1)} %get-tuple-element.57), channel_id=1, source_target_pairs={{0,2},{1,3},{2,0},{3,1},{4,6},{5,7},{6,4},{7,5},{8,10},{9,11},{10,... | collective-permute-start | bytes 1179656 | tf_op jit(solution)/shard_map/ppermute | solution.py:30
  62.5 1.1 %collective-permute-start.5 = (f32[128,768]{1,0:T(8,128)S(1)}, f32[128,768]{1,0:T(8,128)S(1)}, u32[]{:S(2)}, u32[]{:S(2)}) collective-permute-start(f32[128,768]{1,0:T(8,128)S(1)} %get-tuple-element.59), channel_id=1, source_target_pairs={{0,6},{1,7},{2,4},{3,5},{4,2},{5,3},{6,0},{7,1},{8,14},{9,15},{10,... | collective-permute-start | bytes 1179656 | tf_op jit(solution)/shard_map/ppermute | solution.py:30
  63.6 0.1 add.56
  63.8 0.9 collective-permute-start.10
  64.7 0.1 add.57
  64.9 1.0 collective-permute-start.11
  65.8 5.6 %collective-permute-done.5 = f32[128,768]{1,0:T(8,128)S(1)} collective-permute-done((f32[128,768]{1,0:T(8,128)S(1)}, f32[128,768]{1,0:T(8,128)S(1)}, u32[]{:S(2)}, u32[]{:S(2)}) %collective-permute-start.5) | collective-permute-done | bytes 393248 | tf_op jit(solution)/shard_map/ppermute | solution.py:30
  71.7 0.7 collective-permute-start.7
  72.4 1.8 %collective-permute-start.9 = (f32[32,1536]{1,0:T(8,128)S(1)}, f32[32,1536]{1,0:T(8,128)S(1)}, u32[]{:S(2)}, u32[]{:S(2)}) collective-permute-start(f32[32,1536]{1,0:T(8,128)S(1)} %pad_maximum_fusion.2), channel_id=1, source_target_pairs={{0,24},{1,25},{2,26},{3,27},{4,28},{5,29},{6,30},{7,31},{8,16},{9,... | collective-permute-start | bytes 589832 | tf_op jit(solution)/shard_map/ppermute | solution.py:30
  74.2 1.2 %collective-permute-start.8 = (f32[32,1536]{1,0:T(8,128)S(1)}, f32[32,1536]{1,0:T(8,128)S(1)}, u32[]{:S(2)}, u32[]{:S(2)}) collective-permute-start(f32[32,1536]{1,0:T(8,128)S(1)} %pad_maximum_fusion.1), channel_id=1, source_target_pairs={{0,8},{1,9},{2,10},{3,11},{4,12},{5,13},{6,14},{7,15},{8,0},{9,1},... | collective-permute-start | bytes 589832 | tf_op jit(solution)/shard_map/ppermute | solution.py:30
  75.5 2.7 %collective-permute-done.10 = f32[128,768]{1,0:T(8,128)S(1)} collective-permute-done((f32[128,768]{1,0:T(8,128)S(1)}, f32[128,768]{1,0:T(8,128)S(1)}, u32[]{:S(2)}, u32[]{:S(2)}) %collective-permute-start.10) | collective-permute-done | bytes 393248 | tf_op jit(solution)/shard_map/ppermute | solution.py:30
  78.4 0.1 collective-permute-start.12
  78.5 3.5 %collective-permute-start.14 = (f32[32,1536]{1,0:T(8,128)S(1)}, f32[32,1536]{1,0:T(8,128)S(1)}, u32[]{:S(2)}, u32[]{:S(2)}) collective-permute-start(f32[32,1536]{1,0:T(8,128)S(1)} %pad_maximum_fusion.5), channel_id=1, source_target_pairs={{0,6},{1,7},{2,4},{3,5},{4,2},{5,3},{6,0},{7,1},{8,14},{9,15},{10,... | collective-permute-start | bytes 589832 | tf_op jit(solution)/shard_map/ppermute | solution.py:30
  82.1 0.2 collective-permute-done.7
  82.3 1.8 %collective-permute-start.13 = (f32[32,1536]{1,0:T(8,128)S(1)}, f32[32,1536]{1,0:T(8,128)S(1)}, u32[]{:S(2)}, u32[]{:S(2)}) collective-permute-start(f32[32,1536]{1,0:T(8,128)S(1)} %pad_maximum_fusion.4), channel_id=1, source_target_pairs={{0,2},{1,3},{2,0},{3,1},{4,6},{5,7},{6,4},{7,5},{8,10},{9,11},{10,... | collective-permute-start | bytes 589832 | tf_op jit(solution)/shard_map/ppermute | solution.py:30
  84.1 1.6 %collective-permute-done.12 = f32[32,1536]{1,0:T(8,128)S(1)} collective-permute-done((f32[32,1536]{1,0:T(8,128)S(1)}, f32[32,1536]{1,0:T(8,128)S(1)}, u32[]{:S(2)}, u32[]{:S(2)}) %collective-permute-start.12) | collective-permute-done | bytes 196640 | tf_op jit(solution)/shard_map/ppermute | solution.py:30
  85.8 2.0 %collective-permute-done.14 = f32[32,1536]{1,0:T(8,128)S(1)} collective-permute-done((f32[32,1536]{1,0:T(8,128)S(1)}, f32[32,1536]{1,0:T(8,128)S(1)}, u32[]{:S(2)}, u32[]{:S(2)}) %collective-permute-start.14) | collective-permute-done | bytes 196640 | tf_op jit(solution)/shard_map/ppermute | solution.py:30
  87.8 0.2 collective-permute-done.13
  87.9 0.1 maximum_add_fusion.1
  88.1 0.1 constant_dynamic-slice_fusion.3
  88.2 2.0 %collective-permute-start.15 = (f32[32,1536]{1,0:T(8,128)S(1)}, f32[32,1536]{1,0:T(8,128)S(1)}, u32[]{:S(2)}, u32[]{:S(2)}) collective-permute-start(f32[32,1536]{1,0:T(8,128)S(1)} %constant_dynamic-slice_fusion.3), channel_id=1, source_target_pairs={{0,32},{1,33},{2,34},{3,35},{4,36},{5,37},{6,38},{7,39},{8,40},{9,... | collective-permute-start | bytes 589832 | tf_op jit(solution)/shard_map/ppermute | solution.py:30
  90.2 3.8 %collective-permute-done.15 = f32[32,1536]{1,0:T(8,128)S(1)} collective-permute-done((f32[32,1536]{1,0:T(8,128)S(1)}, f32[32,1536]{1,0:T(8,128)S(1)}, u32[]{:S(2)}, u32[]{:S(2)}) %collective-permute-start.15) | collective-permute-done | bytes 196640 | tf_op jit(solution)/shard_map/ppermute | solution.py:30
  94.0 0.1 dynamic-slice_add_fusion
  94.1 0.1 constant_dynamic-slice_fusion.2
  94.2 8.3 %collective-permute-start.16 = (f32[32,384]{1,0:T(8,128)S(1)}, f32[32,384]{1,0:T(8,128)S(1)}, u32[]{:S(2)}, u32[]{:S(2)}) collective-permute-start(f32[32,384]{1,0:T(8,128)S(1)} %get-tuple-element.77), channel_id=1, source_target_pairs={{0,128},{1,129},{2,130},{3,131},{4,132},{5,133},{6,134},{7,135},{8... | collective-permute-start | bytes 147464 | tf_op jit(solution)/shard_map/ppermute | solution.py:30
  102.5 1.5 %collective-permute-start.18 = (f32[32,384]{1,0:T(8,128)S(1)}, f32[32,384]{1,0:T(8,128)S(1)}, u32[]{:S(2)}, u32[]{:S(2)}) collective-permute-start(f32[32,384]{1,0:T(8,128)S(1)} %get-tuple-element.78), channel_id=1, source_target_pairs={{0,64},{1,65},{2,66},{3,67},{4,68},{5,69},{6,70},{7,71},{8,72},{9,... | collective-permute-start | bytes 147464 | tf_op jit(solution)/shard_map/ppermute | solution.py:30
  104.0 0.6 collective-permute-done.16
  104.6 3.2 %collective-permute-done.18 = f32[32,384]{1,0:T(8,128)S(1)} collective-permute-done((f32[32,384]{1,0:T(8,128)S(1)}, f32[32,384]{1,0:T(8,128)S(1)}, u32[]{:S(2)}, u32[]{:S(2)}) %collective-permute-start.18) | collective-permute-done | bytes 49184 | tf_op jit(solution)/shard_map/ppermute | solution.py:30
  107.8 2.4 %collective-permute-done.17 = f32[32,384]{1,0:T(8,128)S(1)} collective-permute-done((f32[32,384]{1,0:T(8,128)S(1)}, f32[32,384]{1,0:T(8,128)S(1)}, u32[]{:S(2)}, u32[]{:S(2)}) %collective-permute-start.17) | collective-permute-done | bytes 49184 | tf_op jit(solution)/shard_map/ppermute | solution.py:30
  110.2 0.7 add_multiply_fusion
  (39 shorter events, 0.7 us)
Async XLA Ops:
  0.1 37.1 %collective-permute-start = (f32[512,3072]{1,0:T(8,128)}, f32[512,3072]{1,0:T(8,128)S(1)}, u32[]{:S(2)}, u32[]{:S(2)}) collective-permute-start(f32[512,3072]{1,0:T(8,128)} %refs_2_.4), channel_id=1, source_target_pairs={{0,1},{1,0},{2,3},{3,2},{4,5},{5,4},{6,7},{7,6},{8,9},{9,8},{10,11... | collective-permute-start | bytes 18874376 | tf_op jit(solution)/shard_map/ppermute | solution.py:30
  0.1 1.6 %copy-start.1 = (f32[32,16384]{1,0:T(8,128)S(1)}, f32[32,16384]{1,0:T(8,128)}, u32[]{:S(2)}) copy-start(f32[32,16384]{1,0:T(8,128)} %a_ref) | copy-start | bytes 6291460
  1.7 35.5 %copy-start = (f32[512,3072]{1,0:T(8,128)S(1)}, f32[512,3072]{1,0:T(8,128)}, u32[]{:S(2)}) copy-start(f32[512,3072]{1,0:T(8,128)} %refs_2_.4) | copy-start | bytes 18874372
  40.6 18.6 %collective-permute-start.1 = (f32[256,768]{1,0:T(8,128)S(1)}, f32[256,768]{1,0:T(8,128)S(1)}, u32[]{:S(2)}, u32[]{:S(2)}) collective-permute-start(f32[256,768]{1,0:T(8,128)S(1)} %get-tuple-element.37), channel_id=1, source_target_pairs={{0,2},{1,3},{2,0},{3,1},{4,6},{5,7},{6,4},{7,5},{8,10},{9,11},{10,... | collective-permute-start | bytes 2359304 | tf_op jit(solution)/shard_map/ppermute | solution.py:30
  42.2 18.3 %collective-permute-start.2 = (f32[256,768]{1,0:T(8,128)S(1)}, f32[256,768]{1,0:T(8,128)S(1)}, u32[]{:S(2)}, u32[]{:S(2)}) collective-permute-start(f32[256,768]{1,0:T(8,128)S(1)} %get-tuple-element.39), channel_id=1, source_target_pairs={{0,6},{1,7},{2,4},{3,5},{4,2},{5,3},{6,0},{7,1},{8,14},{9,15},{10,... | collective-permute-start | bytes 2359304 | tf_op jit(solution)/shard_map/ppermute | solution.py:30
  44.9 18.7 %collective-permute-start.3 = (f32[256,768]{1,0:T(8,128)S(1)}, f32[256,768]{1,0:T(8,128)S(1)}, u32[]{:S(2)}, u32[]{:S(2)}) collective-permute-start(f32[256,768]{1,0:T(8,128)S(1)} %get-tuple-element.41), channel_id=1, source_target_pairs={{0,8},{1,9},{2,10},{3,11},{4,12},{5,13},{6,14},{7,15},{8,0},{9,1},... | collective-permute-start | bytes 2359304 | tf_op jit(solution)/shard_map/ppermute | solution.py:30
  45.5 19.2 %collective-permute-start.4 = (f32[256,768]{1,0:T(8,128)S(1)}, f32[256,768]{1,0:T(8,128)S(1)}, u32[]{:S(2)}, u32[]{:S(2)}) collective-permute-start(f32[256,768]{1,0:T(8,128)S(1)} %get-tuple-element.34), channel_id=1, source_target_pairs={{0,24},{1,25},{2,26},{3,27},{4,28},{5,29},{6,30},{7,31},{8,16},{9,... | collective-permute-start | bytes 2359304 | tf_op jit(solution)/shard_map/ppermute | solution.py:30
  60.6 11.0 %collective-permute-start.6 = (f32[128,768]{1,0:T(8,128)S(1)}, f32[128,768]{1,0:T(8,128)S(1)}, u32[]{:S(2)}, u32[]{:S(2)}) collective-permute-start(f32[128,768]{1,0:T(8,128)S(1)} %get-tuple-element.57), channel_id=1, source_target_pairs={{0,2},{1,3},{2,0},{3,1},{4,6},{5,7},{6,4},{7,5},{8,10},{9,11},{10,... | collective-permute-start | bytes 1179656 | tf_op jit(solution)/shard_map/ppermute | solution.py:30
  62.5 9.0 %collective-permute-start.5 = (f32[128,768]{1,0:T(8,128)S(1)}, f32[128,768]{1,0:T(8,128)S(1)}, u32[]{:S(2)}, u32[]{:S(2)}) collective-permute-start(f32[128,768]{1,0:T(8,128)S(1)} %get-tuple-element.59), channel_id=1, source_target_pairs={{0,6},{1,7},{2,4},{3,5},{4,2},{5,3},{6,0},{7,1},{8,14},{9,15},{10,... | collective-permute-start | bytes 1179656 | tf_op jit(solution)/shard_map/ppermute | solution.py:30
  63.8 14.4 %collective-permute-start.10 = (f32[128,768]{1,0:T(8,128)S(1)}, f32[128,768]{1,0:T(8,128)S(1)}, u32[]{:S(2)}, u32[]{:S(2)}) collective-permute-start(f32[128,768]{1,0:T(8,128)S(1)} %get-tuple-element.55), channel_id=1, source_target_pairs={{0,24},{1,25},{2,26},{3,27},{4,28},{5,29},{6,30},{7,31},{8,16},{9,... | collective-permute-start | bytes 1179656 | tf_op jit(solution)/shard_map/ppermute | solution.py:30
  64.9 13.4 %collective-permute-start.11 = (f32[128,768]{1,0:T(8,128)S(1)}, f32[128,768]{1,0:T(8,128)S(1)}, u32[]{:S(2)}, u32[]{:S(2)}) collective-permute-start(f32[128,768]{1,0:T(8,128)S(1)} %get-tuple-element.53), channel_id=1, source_target_pairs={{0,8},{1,9},{2,10},{3,11},{4,12},{5,13},{6,14},{7,15},{8,0},{9,1},... | collective-permute-start | bytes 1179656 | tf_op jit(solution)/shard_map/ppermute | solution.py:30
  71.7 10.6 %collective-permute-start.7 = (f32[32,1536]{1,0:T(8,128)S(1)}, f32[32,1536]{1,0:T(8,128)S(1)}, u32[]{:S(2)}, u32[]{:S(2)}) collective-permute-start(f32[32,1536]{1,0:T(8,128)S(1)} %pad_maximum_fusion), channel_id=1, source_target_pairs={{0,16},{1,17},{2,18},{3,19},{4,20},{5,21},{6,22},{7,23},{8,24},{9,... | collective-permute-start | bytes 589832 | tf_op jit(solution)/shard_map/ppermute | solution.py:30
  72.4 11.7 %collective-permute-start.9 = (f32[32,1536]{1,0:T(8,128)S(1)}, f32[32,1536]{1,0:T(8,128)S(1)}, u32[]{:S(2)}, u32[]{:S(2)}) collective-permute-start(f32[32,1536]{1,0:T(8,128)S(1)} %pad_maximum_fusion.2), channel_id=1, source_target_pairs={{0,24},{1,25},{2,26},{3,27},{4,28},{5,29},{6,30},{7,31},{8,16},{9,... | collective-permute-start | bytes 589832 | tf_op jit(solution)/shard_map/ppermute | solution.py:30
  74.2 9.8 %collective-permute-start.8 = (f32[32,1536]{1,0:T(8,128)S(1)}, f32[32,1536]{1,0:T(8,128)S(1)}, u32[]{:S(2)}, u32[]{:S(2)}) collective-permute-start(f32[32,1536]{1,0:T(8,128)S(1)} %pad_maximum_fusion.1), channel_id=1, source_target_pairs={{0,8},{1,9},{2,10},{3,11},{4,12},{5,13},{6,14},{7,15},{8,0},{9,1},... | collective-permute-start | bytes 589832 | tf_op jit(solution)/shard_map/ppermute | solution.py:30
  78.4 7.4 %collective-permute-start.12 = (f32[32,1536]{1,0:T(8,128)S(1)}, f32[32,1536]{1,0:T(8,128)S(1)}, u32[]{:S(2)}, u32[]{:S(2)}) collective-permute-start(f32[32,1536]{1,0:T(8,128)S(1)} %pad_maximum_fusion.3), channel_id=1, source_target_pairs={{0,4},{1,5},{2,6},{3,7},{4,0},{5,1},{6,2},{7,3},{8,12},{9,13},{10,... | collective-permute-start | bytes 589832 | tf_op jit(solution)/shard_map/ppermute | solution.py:30
  78.5 9.2 %collective-permute-start.14 = (f32[32,1536]{1,0:T(8,128)S(1)}, f32[32,1536]{1,0:T(8,128)S(1)}, u32[]{:S(2)}, u32[]{:S(2)}) collective-permute-start(f32[32,1536]{1,0:T(8,128)S(1)} %pad_maximum_fusion.5), channel_id=1, source_target_pairs={{0,6},{1,7},{2,4},{3,5},{4,2},{5,3},{6,0},{7,1},{8,14},{9,15},{10,... | collective-permute-start | bytes 589832 | tf_op jit(solution)/shard_map/ppermute | solution.py:30
  82.3 5.7 %collective-permute-start.13 = (f32[32,1536]{1,0:T(8,128)S(1)}, f32[32,1536]{1,0:T(8,128)S(1)}, u32[]{:S(2)}, u32[]{:S(2)}) collective-permute-start(f32[32,1536]{1,0:T(8,128)S(1)} %pad_maximum_fusion.4), channel_id=1, source_target_pairs={{0,2},{1,3},{2,0},{3,1},{4,6},{5,7},{6,4},{7,5},{8,10},{9,11},{10,... | collective-permute-start | bytes 589832 | tf_op jit(solution)/shard_map/ppermute | solution.py:30
  88.2 5.8 %collective-permute-start.15 = (f32[32,1536]{1,0:T(8,128)S(1)}, f32[32,1536]{1,0:T(8,128)S(1)}, u32[]{:S(2)}, u32[]{:S(2)}) collective-permute-start(f32[32,1536]{1,0:T(8,128)S(1)} %constant_dynamic-slice_fusion.3), channel_id=1, source_target_pairs={{0,32},{1,33},{2,34},{3,35},{4,36},{5,37},{6,38},{7,39},{8,40},{9,... | collective-permute-start | bytes 589832 | tf_op jit(solution)/shard_map/ppermute | solution.py:30
  94.2 10.4 %collective-permute-start.16 = (f32[32,384]{1,0:T(8,128)S(1)}, f32[32,384]{1,0:T(8,128)S(1)}, u32[]{:S(2)}, u32[]{:S(2)}) collective-permute-start(f32[32,384]{1,0:T(8,128)S(1)} %get-tuple-element.77), channel_id=1, source_target_pairs={{0,128},{1,129},{2,130},{3,131},{4,132},{5,133},{6,134},{7,135},{8... | collective-permute-start | bytes 147464 | tf_op jit(solution)/shard_map/ppermute | solution.py:30
  102.5 5.3 %collective-permute-start.18 = (f32[32,384]{1,0:T(8,128)S(1)}, f32[32,384]{1,0:T(8,128)S(1)}, u32[]{:S(2)}, u32[]{:S(2)}) collective-permute-start(f32[32,384]{1,0:T(8,128)S(1)} %get-tuple-element.78), channel_id=1, source_target_pairs={{0,64},{1,65},{2,66},{3,67},{4,68},{5,69},{6,70},{7,71},{8,72},{9,... | collective-permute-start | bytes 147464 | tf_op jit(solution)/shard_map/ppermute | solution.py:30
  104.0 6.2 %collective-permute-start.17 = (f32[32,384]{1,0:T(8,128)S(1)}, f32[32,384]{1,0:T(8,128)S(1)}, u32[]{:S(2)}, u32[]{:S(2)}) collective-permute-start(f32[32,384]{1,0:T(8,128)S(1)} %get-tuple-element.79), channel_id=1, source_target_pairs={{0,192},{1,193},{2,194},{3,195},{4,196},{5,197},{6,198},{7,199},{8... | collective-permute-start | bytes 147464 | tf_op jit(solution)/shard_map/ppermute | solution.py:30
